TPU v7x, 32 devices: a whole 2x2x4 slice. The times are simulated.
32 devices in a mesh: tok: 16 (over z, y, core), head: 2 (over x).
Axes of the slice: x: 2, y: 2, z: 4, core: 2. Of those that a mesh axis runs over, the one named last changes fastest.
Arguments:
- query_rows: bfloat16 [4096, 40, 128], P('tok', 'head'), as said below
- key_rows: bfloat16 [4096, 40, 128], P('tok', 'head'), as said below
- value_rows: bfloat16 [4096, 40, 128], P('tok', 'head'), may hold values from -6 to 6
- query_gain: float32 [40, 128], P('head'), may hold values from 1.5 to 4
- key_gain: float32 [40, 128], P('head'), may hold values from 0.25 to 1.75
- rate_in: float32 [40, 4096], P('head', 'tok'), may hold values from 0.05 to 0.5
- rate_out: float32 [40, 4096], P('head', 'tok'), may hold values from 0.0002 to 0.002
- fast_in: bfloat16 [40, 128, 512], P('head'), may hold values from -6 to 6
- fast_out: bfloat16 [40, 256, 128], P('head'), may hold values from -0.375 to 0.375
- half_window: int32 [40], P('head'), may hold values from 128 to 1024, as said below
- boundaries: int32 [3], replicated, may hold values from 2049 to 4095, as said below
Outputs:
- layer_out: bfloat16 [4096, 40, 128], P('tok', 'head')
Inputs may be any that keep to these rules, and one draw needn't show every extreme that they name: `half_window`: no head sees more than 1024 tokens on either side; some head has exactly 1024 and some head exactly 128. `boundaries`: non-decreasing; the first is 2049 and the last 4095. `query_rows`: entries within -400 and 400. `key_rows`: entries within -400 and 400.
All inputs are finite; a program needn't handle non-finite values.
Results may differ from a plain program's by a relative error of at most 0.02.
Values may be sent and summed in bfloat16 or wider, within the bound.
No kernel may reach another device: no remote copies, remote signals or barrier semaphores. Data moves between devices by JAX's collectives and lax.ppermute only.
A program may use at most 128 MiB of HBM per device.

v0:
```python
import functools
import math

import jax
import jax.numpy as jnp
from jax import lax
from jax.experimental import pallas as pl
from jax.experimental.pallas import tpu as pltpu
from jax.sharding import PartitionSpec as P

HALF = 1024


epsilon = 1e-06


def passed_along(x, axis, by):
    peers = lax.axis_size(axis)
    pairs = [(i, i + by) for i in range(peers) if 0 <= i + by < peers]
    return lax.ppermute(x, axis, pairs)


def unit_rows(matrix):
    as_float = matrix.astype(jnp.float32)
    return (
        as_float * lax.rsqrt(jnp.sum(as_float * as_float, axis=-1, keepdims=True) + epsilon)
    ).astype(jnp.bfloat16)


def rescale(updated, base_norm, squares):
    return (updated * (base_norm / jnp.sqrt(squares + epsilon))[:, None, :]).astype(jnp.bfloat16)


def sliding_body(
    query_rows,
    key_rows,
    value_rows,
    query_gain,
    key_gain,
    rate_in,
    rate_out,
    fast_in,
    fast_out,
    half_window,
    boundaries,
):
    tok_rows = query_rows.shape[0]
    local_heads = query_rows.shape[1]
    head_dim = query_rows.shape[2]
    fast_hid = fast_out.shape[1]
    width_all = local_heads * head_dim * lax.axis_size("head")
    tok_count = tok_rows * lax.axis_size("tok")
    own_index = lax.axis_index("tok")
    first_row = own_index * tok_rows
    query_float = query_rows.astype(jnp.float32)
    key_float = key_rows.astype(jnp.float32)
    query_sq, key_sq = lax.psum(
        (
            jnp.sum(query_float * query_float, axis=(1, 2)),
            jnp.sum(key_float * key_float, axis=(1, 2)),
        ),
        "head",
    )
    q_normed = (
        query_float * lax.rsqrt(query_sq / width_all + epsilon)[:, None, None] * query_gain[None]
    ).astype(jnp.bfloat16)
    k_normed = (
        key_float * lax.rsqrt(key_sq / width_all + epsilon)[:, None, None] * key_gain[None]
    ).astype(jnp.bfloat16)

    def clip_of(places):
        return jnp.sum((places[:, None] >= boundaries[None, :]).astype(jnp.int32), axis=1)

    positions = first_row + jnp.arange(tok_rows, dtype=jnp.int32)
    query_clip = clip_of(positions)
    scaling = 1.0 / math.sqrt(head_dim)

    def absorb(state_now, block_keys, block_values, key_first):
        best, denominator, accum = state_now
        key_places = key_first + jnp.arange(tok_rows, dtype=jnp.int32)
        scores = (
            jnp.einsum("qhd,khd->hqk", q_normed, block_keys, preferred_element_type=jnp.float32)
            * scaling
        )
        inside = (key_places >= 0) & (key_places < tok_count)
        pair_ok = (query_clip[:, None] == clip_of(key_places)[None, :]) & inside[None, :]
        distance = jnp.abs(positions[:, None] - key_places[None, :])
        allowed = (distance[None, :, :] <= half_window[:, None, None]) & pair_ok[None, :, :]
        masked = jnp.where(allowed, scores, -jnp.inf)
        new_best = jnp.maximum(best, jnp.max(masked, axis=2))
        weights = jnp.exp(masked - new_best[:, :, None])
        shrink = jnp.exp(best - new_best)
        denominator = denominator * shrink + jnp.sum(weights, axis=2)
        accum = accum * shrink[:, :, None] + jnp.einsum(
            "hqk,khd->hqd",
            weights.astype(jnp.bfloat16),
            block_values,
            preferred_element_type=jnp.float32,
        )
        return (new_best, denominator, accum)

    start_state = (
        jnp.full((local_heads, tok_rows), -jnp.inf, jnp.float32),
        jnp.zeros((local_heads, tok_rows), jnp.float32),
        jnp.zeros((local_heads, tok_rows, head_dim), jnp.float32),
    )
    state_now = absorb(start_state, k_normed, value_rows, first_row)
    reach_blocks = HALF // tok_rows
    for distance_step in range(1, reach_blocks + 1):
        left_keys, left_values = passed_along((k_normed, value_rows), "tok", distance_step)
        state_now = absorb(state_now, left_keys, left_values, first_row - distance_step * tok_rows)
        right_keys, right_values = passed_along((k_normed, value_rows), "tok", -distance_step)
        state_now = absorb(
            state_now, right_keys, right_values, first_row + distance_step * tok_rows
        )
    attended = state_now[2] / state_now[1][:, :, None]
    key_unit = unit_rows(k_normed)
    query_unit = unit_rows(q_normed)
    pre_keys = jnp.einsum("thd,hdf->htf", key_unit, fast_in, preferred_element_type=jnp.float32)
    gate_part = pre_keys[:, :, :fast_hid]
    lin_part = pre_keys[:, :, fast_hid:]
    sigmoid_gate = jax.nn.sigmoid(gate_part)
    swish_gate = gate_part * sigmoid_gate
    hidden = (swish_gate * lin_part).astype(jnp.bfloat16)
    value_float = value_rows.astype(jnp.float32)
    push_out = (-jnp.transpose(rate_out)[:, :, None] * value_float).astype(jnp.bfloat16)
    push_in = (-jnp.transpose(rate_in)[:, :, None] * value_float).astype(jnp.bfloat16)
    grad_out = jnp.einsum("htf,thd->hfd", hidden, push_out, preferred_element_type=jnp.float32)
    hidden_grad = jnp.einsum("thd,hfd->htf", push_in, fast_out, preferred_element_type=jnp.float32)
    d_gate = hidden_grad * lin_part * sigmoid_gate * (1.0 + gate_part * (1.0 - sigmoid_gate))
    d_lin = hidden_grad * swish_gate
    d_pre = jnp.concatenate([d_gate, d_lin], axis=2).astype(jnp.bfloat16)
    grad_in = jnp.einsum("thd,htf->hdf", key_unit, d_pre, preferred_element_type=jnp.float32)
    in_float = fast_in.astype(jnp.float32)
    out_float = fast_out.astype(jnp.float32)
    in_base = jnp.sqrt(jnp.sum(in_float * in_float, axis=1))
    out_base = jnp.sqrt(jnp.sum(out_float * out_float, axis=1))
    summed_in, summed_out = lax.psum((grad_in, grad_out), "tok")
    updated_in = in_float - summed_in
    updated_out = out_float - summed_out
    new_in = rescale(updated_in, in_base, jnp.sum(updated_in * updated_in, axis=1))
    new_out = rescale(updated_out, out_base, jnp.sum(updated_out * updated_out, axis=1))
    pre_query = jnp.einsum("thd,hdf->htf", query_unit, new_in, preferred_element_type=jnp.float32)
    query_gate = pre_query[:, :, :fast_hid]
    query_hidden = (query_gate * jax.nn.sigmoid(query_gate) * pre_query[:, :, fast_hid:]).astype(
        jnp.bfloat16
    )
    fast_result = jnp.einsum(
        "htf,hfd->htd", query_hidden, new_out, preferred_element_type=jnp.float32
    )
    combined = attended + fast_result
    return jnp.transpose(combined, (1, 0, 2)).astype(jnp.bfloat16)


VMEM_BYTES = 16 * 1024 * 1024
HIDDEN_MASK = -1e30
NT = (((1,), (1,)), ((), ()))


def exchanged(x, pairs):
    return lax.ppermute(x, "tok", pairs)


def nt_dot(a, b):
    return lax.dot_general(a, b, NT, preferred_element_type=jnp.float32)


def nn_dot(a, b):
    return jnp.dot(a, b, preferred_element_type=jnp.float32)


def in_vmem(kernel, name, scalars, arrays, after, out_shape, flops=0, scratch=()):
    specs = [pl.BlockSpec(memory_space=pltpu.SMEM)] * len(scalars)
    specs += [pl.BlockSpec(memory_space=pltpu.VMEM)] * len(arrays)
    specs += [pl.BlockSpec(memory_space=pl.ANY)] * len(after)
    return pl.pallas_call(
        kernel,
        out_shape=out_shape,
        in_specs=specs,
        out_specs=jax.tree.map(lambda _: pl.BlockSpec(memory_space=pltpu.VMEM), out_shape),
        scratch_shapes=scratch,
        compiler_params=pltpu.CompilerParams(vmem_limit_bytes=VMEM_BYTES),
        cost_estimate=pl.CostEstimate(flops=16 * flops, bytes_accessed=0, transcendentals=0),
        name=name,
    )(*scalars, *arrays, *after)


def pack_kernel(peers, first, count, width_all, fold, with_lone, place_ref, *refs):
    squares_ref, more_ref, q_gain_ref, k_gain_ref, rate_in_ref, rate_out_ref = refs[:6]
    q_ref, k_ref, v_ref = refs[6:9]
    outs = refs[-3 - peers : -3]
    aux_ref, q_scale_ref, k_scale_ref = refs[-3:]
    rows, dim = q_scale_ref.shape
    share = q_gain_ref.shape[0] // peers
    scales = lax.rsqrt((squares_ref[...] + more_ref[...]) / width_all + epsilon)
    q_scale_ref[...] = jnp.transpose(jnp.broadcast_to(scales[0:1] * fold, (dim, rows)))
    k_scale_ref[...] = jnp.transpose(jnp.broadcast_to(scales[1:2], (dim, rows)))
    aux_ref[...] = jnp.zeros_like(aux_ref)

    def normed(ref, c, scale_ref, gain_ref, head, some):
        gain = gain_ref[pl.ds(c * share + head, 1), :]
        scaled = ref[c, head, 0:some].astype(jnp.float32) * scale_ref[0:some] * gain
        return scaled.astype(jnp.bfloat16)

    def one_head(step, carry):
        for p in range(peers):
            c = place_ref[0] ^ p
            head = first + step
            outs[p][step, 0:rows, :] = normed(q_ref, c, q_scale_ref, q_gain_ref, head, rows)
            outs[p][step, rows : 2 * rows, :] = normed(
                k_ref, c, k_scale_ref, k_gain_ref, head, rows
            )
            for i in range(0, rows, 128):
                outs[p][step, 2 * rows + i : 2 * rows + i + 128, :] = jnp.transpose(
                    v_ref[c, head, i : i + 128, :]
                )
            at = 0
            for rate_ref in (rate_in_ref, rate_out_ref):
                rate = rate_ref[pl.ds(c * share + head, 1), :]
                high = rate.astype(jnp.bfloat16).astype(jnp.float32)
                for part in (high, rate - high):
                    for i in range(0, rows, 128):
                        aux_ref[at : at + 1, :] = part[:, i : i + 128]
                        at += 1
            if with_lone:
                for i in range(-(-share // count)):
                    head = jnp.minimum(step + i * count, share - 1)
                    q0 = normed(q_ref, c, q_scale_ref, q_gain_ref, head, 16)
                    k0 = normed(k_ref, c, k_scale_ref, k_gain_ref, head, 16)
                    for at, array in enumerate((q0, k0, v_ref[c, head, 0:16])):
                        at += aux_ref.shape[0] // 2 + 3 * i
                        aux_ref[at : at + 1, :] = array.astype(jnp.float32)[0:1]
            some = outs[p].shape[1] - 3 * rows
            outs[p][step, 3 * rows :, :] = aux_ref[0:some, :].astype(jnp.bfloat16)
        return carry

    lax.fori_loop(0, count, one_head, 0)


def pack(place, sums, q, k, v, gains, rates, peers, aux_rows, first, count, width_all, fold):
    heads, rows, dim = q.shape
    out_shape = (count, 3 * rows + aux_rows // (2 if first else 1), dim)
    q, k, v = [x.reshape(peers, heads // peers, rows, dim) for x in (q, k, v)]
    return in_vmem(
        functools.partial(pack_kernel, peers, first, count, width_all, fold, not first),
        "pack",
        [place],
        [*sums, *gains, *rates, q, k, v],
        [],
        [jax.ShapeDtypeStruct(out_shape, jnp.bfloat16)] * peers,
        scratch=[
            pltpu.VMEM((aux_rows, dim), jnp.float32),
            pltpu.VMEM((rows, dim), jnp.float32),
            pltpu.VMEM((rows, dim), jnp.float32),
        ],
    )


def stack_kernel(from_row, *refs):
    for p, ref in enumerate(refs[:-1]):
        refs[-1][p] = ref[:, from_row:, :]


def stacked(arrays, from_row):
    heads, rows, dim = arrays[0].shape
    return in_vmem(
        functools.partial(stack_kernel, from_row),
        "stack",
        [],
        arrays,
        [],
        jax.ShapeDtypeStruct((len(arrays), heads, rows - from_row, dim), jnp.bfloat16),
    )


def lone_kernel(place_ref, own_ref, other_ref, out_ref):
    extra = out_ref.shape[1]
    at = own_ref.shape[2] - extra
    mine = jnp.full(out_ref.shape, place_ref[1]) == 0
    own = own_ref[place_ref[0], :, at:, :].astype(jnp.float32)
    other = other_ref[place_ref[0], :, at:, :].astype(jnp.float32)
    out_ref[...] = jnp.where(mine, own, other).astype(jnp.bfloat16)


def lone_rows(place, own, other, rows):
    _, count, all_rows, dim = own.shape
    out_shape = (count, (all_rows - 2 * rows) // 2, dim)
    return in_vmem(
        lone_kernel,
        "lone_rows",
        [place],
        [own, other],
        [],
        jax.ShapeDtypeStruct(out_shape, jnp.bfloat16),
    )


def key_value_blocks(peers, rows, step, refs):
    for p in range(peers):
        yield p, True, refs[p].at[step, rows : 2 * rows], refs[p].at[step, 2 * rows :]
        yield p, False, refs[peers].at[p, step, 0:rows], refs[peers].at[p, step, rows:]


def grads_kernel(peers, rows, rate_rows, share, first, place_ref, in_ref, out_ref, *refs):
    grad_ref = refs[-1]
    hid = out_ref.shape[1]
    part = hid // 2
    own = pl.multiple_of(place_ref[1] * part, part)

    def one_head(step, carry):
        head = place_ref[0] * share + first + step
        in_half = jnp.concatenate(
            [
                jnp.transpose(in_ref[head, :, pl.ds(at, part)].astype(jnp.float32))
                for at in (own, pl.multiple_of(hid + own, part))
            ],
            axis=0,
        ).astype(jnp.bfloat16)
        out_half = out_ref[head, pl.ds(own, part), :]
        sum_in = jnp.zeros((2 * part, in_half.shape[1]), jnp.float32)
        sum_out = jnp.zeros((part, in_half.shape[1]), jnp.float32)
        for _, _, keys, values in key_value_blocks(peers, rows, step, refs):
            k = keys[...].astype(jnp.float32)
            v_t = jnp.concatenate([values[at : at + 128, :] for at in range(0, rows, 128)], axis=1)
            aux = values[rows : rows + 16, :].astype(jnp.float32)

            def rate(at):
                both = aux[at : at + rate_rows] + aux[at + rate_rows : at + 2 * rate_rows]
                return jnp.concatenate([both[i : i + 1] for i in range(rate_rows)], axis=1)

            rate_in, rate_out = rate(0), rate(2 * rate_rows)
            unit = (k * lax.rsqrt(jnp.sum(k * k, axis=1, keepdims=True) + epsilon)).astype(
                jnp.bfloat16
            )
            pre = nt_dot(in_half, unit)
            gate, lin = pre[:part], pre[part:]
            sig = jax.nn.sigmoid(gate)
            swish = gate * sig
            pushed = (swish * lin * -rate_out).astype(jnp.bfloat16)
            hidden_grad = nn_dot(out_half, v_t) * -rate_in
            d_gate = hidden_grad * lin * sig * (1.0 + gate * (1.0 - sig))
            d_lin = hidden_grad * swish
            d_pre = jnp.concatenate([d_gate, d_lin], axis=0).astype(jnp.bfloat16)
            sum_in += nn_dot(d_pre, unit)
            sum_out += nt_dot(pushed, v_t)
        grad_ref[step, 0 : 2 * part, :] = sum_in.astype(jnp.bfloat16)
        grad_ref[step, 2 * part :, :] = sum_out.astype(jnp.bfloat16)
        return carry

    lax.fori_loop(0, grad_ref.shape[0], one_head, 0)


def gradients(place, fast_in, fast_out, packets, share, rows, first, after):
    _, hid, dim = fast_out.shape
    own, other = packets
    peers, heads = other.shape[:2]
    return in_vmem(
        functools.partial(grads_kernel, peers, rows, rows // 128, share, first),
        "gradients",
        [place],
        [fast_in, fast_out, *own, other],
        after,
        jax.ShapeDtypeStruct((heads, 3 * hid // 2, dim), jnp.bfloat16),
    )


def attend_kernel(peers, rows, share, first, fwd_heads, place_ref, window_ref, edge_ref, *refs):
    fwd_ref = refs[peers + 1]
    out_ref, extra_ref, k_scr, vt_scr, q_scr = refs[-5:]
    span = 2 * peers * rows
    dim = k_scr.shape[1]
    pad = fwd_ref.shape[1]
    chip, core, half = place_ref[0], place_ref[1], place_ref[2]
    base = half * span
    limit = span + 1 - half
    k_scr[span:, :] = jnp.zeros((k_scr.shape[0] - span, dim), k_scr.dtype)
    vt_scr[:, span:] = jnp.zeros((vt_scr.shape[0], vt_scr.shape[1] - span), vt_scr.dtype)
    vt_scr[dim:, :] = jnp.ones((vt_scr.shape[0] - dim, vt_scr.shape[1]), vt_scr.dtype)

    def one_head(step, carry):
        window = window_ref[chip * share + first + step]
        for p, own, keys, values in key_value_blocks(peers, rows, step, refs):
            at = pl.multiple_of(((chip ^ p) * 2 + (core if own else 1 - core)) * rows, rows)
            k_scr[pl.ds(at, rows), :] = keys[...]
            for i in range(0, rows, 128):
                vt_scr[0:dim, pl.ds(pl.multiple_of(at + i, 128), 128)] = values[i : i + 128, :]
        for p in range(peers):
            q_scr[chip ^ p] = refs[p][step, 0:rows, :]
        fwd = fwd_ref[lax.rem(first + step, fwd_heads)].astype(jnp.float32)
        turn = (first + step) // fwd_heads
        q_lone, k_lone, v_lone = (
            sum(
                jnp.where(turn == t, fwd[3 * t + i : 3 * t + i + 1], 0.0)
                for t in range(-(-share // fwd_heads))
            )
            for i in range(3)
        )
        k_scr[span : span + pad, :] = jnp.broadcast_to(k_lone, (pad, dim)).astype(jnp.bfloat16)
        vt_scr[0:dim, span : span + 128] = jnp.transpose(
            jnp.broadcast_to(v_lone, (128, dim))
        ).astype(jnp.bfloat16)

        def clip_start(place):
            start = jnp.zeros_like(place)
            for i in range(edge_ref.shape[0]):
                start = jnp.maximum(start, jnp.where(edge_ref[i] <= place, edge_ref[i], 0))
            return start

        def clip_stop(place):
            stop = jnp.full_like(place, base + limit)
            for i in range(edge_ref.shape[0]):
                stop = jnp.minimum(stop, jnp.where(edge_ref[i] > place, edge_ref[i], base + limit))
            return stop

        def lowest(place):
            return jnp.maximum(jnp.maximum(place - window, clip_start(place)), base) - base

        def highest(place):
            return jnp.minimum(place + window, clip_stop(place) - 1) - base

        def one_pair(i, carry):
            pair = []
            for c in (i, peers - 1 - i):
                start = (c * 2 + core) * rows
                place = base + start + lax.broadcasted_iota(jnp.int32, (1, rows), 1)
                from_key = lowest(base + start) // 128 * 128
                count = (highest(base + start + rows - 1) - from_key) // 256 + 1
                pair.append((c, lowest(place), highest(place), from_key, count))
            count = jnp.maximum(pair[0][4], pair[1][4])

            def variant(chunks):
                froms = [
                    pl.multiple_of(jnp.minimum(each[3], k_scr.shape[0] - chunks * 256), 128)
                    for each in pair
                ]
                key = lax.broadcasted_iota(jnp.int32, (256, rows), 0)
                scores = [[], []]
                tops = [None, None]
                for i in range(chunks):
                    for n, (each, at) in enumerate(zip(pair, froms)):
                        from_key = pl.multiple_of(at + i * 256, 128)
                        piece = nt_dot(k_scr[pl.ds(from_key, 256), :], q_scr[each[0]])
                        seen = (key >= each[1] - from_key) & (key <= each[2] - from_key)
                        piece = jnp.where(seen, piece, HIDDEN_MASK)
                        top = jnp.max(piece.reshape(32, 8, rows), axis=0)
                        tops[n] = top if i == 0 else jnp.maximum(tops[n], top)
                        scores[n].append(piece)
                tops = [jnp.max(top, axis=0, keepdims=True) for top in tops]
                totals = [0.0, 0.0]
                for i in range(chunks):
                    for n, at in enumerate(froms):
                        weights = jnp.exp2(scores[n][i] - tops[n]).astype(jnp.bfloat16)
                        from_key = pl.multiple_of(at + i * 256, 128)
                        totals[n] += nn_dot(vt_scr[:, pl.ds(from_key, 256)], weights)
                for each, total in zip(pair, totals):
                    attended = total[0:dim] * (1.0 / total[dim : dim + 1])
                    out_ref[each[0], step] = jnp.transpose(attended)

            for chunks in range(1, span // 256 + 2):

                @pl.when(count == chunks)
                def _(chunks=chunks):
                    variant(chunks)

            return carry

        lax.fori_loop(0, peers // 2, one_pair, 0)
        extra_ref[step] = jnp.zeros(extra_ref.shape[1:], jnp.float32)

        @pl.when((half == 0) & (core == 1))
        def _():
            near = span - HALF
            width = HALF + 128
            q = jnp.broadcast_to(q_lone, (pad, dim)).astype(jnp.bfloat16)
            scores = nt_dot(q, k_scr[near : near + width, :])
            key = near + lax.broadcasted_iota(jnp.int32, (1, width), 1)
            scores = jnp.where((key >= span - window) & (key <= span), scores, HIDDEN_MASK)
            top = jnp.max(scores, axis=1, keepdims=True)
            weights = jnp.exp2(scores - top).astype(jnp.bfloat16)
            total = nt_dot(weights, vt_scr[:, near : near + width])
            extra_ref[step] = total[:, 0:dim] / total[:, dim : dim + 1]
        return carry

    lax.fori_loop(0, extra_ref.shape[0], one_head, 0)


def attend(place, half_window, boundaries, packets, forwarded, share, rows, first, after):
    own, other = packets
    peers, heads = other.shape[:2]
    fwd_heads, pad, dim = forwarded.shape
    scr_rows = 2 * peers * rows + 256
    out_shapes = [(peers, heads, rows, dim), (heads, pad, dim)]
    return in_vmem(
        functools.partial(attend_kernel, peers, rows, share, first, fwd_heads),
        "attend",
        [place, half_window, boundaries],
        [*own, other, forwarded],
        after,
        [jax.ShapeDtypeStruct(shape, jnp.float32) for shape in out_shapes],
        flops=4 * heads * peers * rows * HALF * 2 * dim,
        scratch=[
            pltpu.VMEM((scr_rows, dim), jnp.bfloat16),
            pltpu.VMEM((dim + 16, scr_rows), jnp.bfloat16),
            pltpu.VMEM((peers, rows, dim), jnp.bfloat16),
        ],
    )


def finish_kernel(peers, share, first, unit_epsilon, place_ref, *refs):
    att_ref, base_in_ref, base_out_ref, own_ref, other_ref, patch_ref = refs[:6]
    queries = refs[6 : 6 + peers]
    outs = refs[-2 - peers : -2]
    grad_in_scr, grad_out_scr = refs[-2:]
    chip, core, half = place_ref[0], place_ref[1], place_ref[2]
    rows = att_ref.shape[2]
    hid = base_out_ref.shape[1]
    part = hid // 2

    def one_head(step, carry):
        head = chip * share + first + step
        for summed, lane in ((own_ref, core), (other_ref, 1 - core)):
            at = pl.multiple_of(lane * part, part)
            grad_in_scr[pl.ds(at, part), :] = summed[step, 0:part, :].astype(jnp.float32)
            grad_in_scr[pl.ds(hid + at, part), :] = summed[step, part : 2 * part, :].astype(jnp.float32)
            grad_out_scr[pl.ds(at, part), :] = summed[step, 2 * part :, :].astype(jnp.float32)

        def renewed(base, grad):
            base = base.astype(jnp.float32)
            updated = base - grad
            norm = jnp.sqrt(jnp.sum(base * base, axis=0, keepdims=True))
            squares = jnp.sum(updated * updated, axis=0, keepdims=True)
            return (updated * (norm / jnp.sqrt(squares + epsilon))).astype(jnp.bfloat16)

        new_in = renewed(base_in_ref[head], jnp.transpose(grad_in_scr[...]))
        new_out = renewed(base_out_ref[head], grad_out_scr[...])
        patch = patch_ref[step, 0:8, :][0:1]
        row = lax.broadcasted_iota(jnp.int32, (rows, 1), 0)
        for p in range(peers):
            q = queries[p][step, 0:rows, :].astype(jnp.float32)
            unit = (q * lax.rsqrt(jnp.sum(q * q, axis=1, keepdims=True) + unit_epsilon)).astype(
                jnp.bfloat16
            )
            pre = nn_dot(unit, new_in)
            gate = pre[:, :hid]
            hidden = (gate * jax.nn.sigmoid(gate) * pre[:, hid:]).astype(jnp.bfloat16)
            patched = (half == 1) & (core == 0) & (chip == p)
            attended = jnp.where(patched & (row == 0), patch, att_ref[chip ^ p, step])
            outs[p][step] = (attended + nn_dot(hidden, new_out)).astype(jnp.bfloat16)
        return carry

    lax.fori_loop(0, att_ref.shape[1], one_head, 0)


def finish(place, attended, fast_in, fast_out, sums, patch, own, share, first, unit_epsilon, after):
    peers, heads, rows, dim = attended.shape
    hid = fast_out.shape[1]
    return in_vmem(
        functools.partial(finish_kernel, peers, share, first, unit_epsilon),
        "finish",
        [place],
        [attended, fast_in, fast_out, *sums, patch, *own],
        after,
        [jax.ShapeDtypeStruct((heads, rows, dim), jnp.bfloat16)] * peers,
        flops=12 * heads * peers * rows * hid * dim,
        scratch=[pltpu.VMEM((2 * hid, dim), jnp.float32), pltpu.VMEM((hid, dim), jnp.float32)],
    )


def place_kernel(peers, chunks, share, place_ref, *refs):
    pieces, out_ref, sems = refs[:-2], refs[-2], refs[-1]
    copies = []
    for first, heads in chunks:
        for p in range(peers):
            at = (place_ref[0] ^ p) * share + first
            i = len(copies)
            copies.append(
                pltpu.make_async_copy(pieces[i], out_ref.at[pl.ds(at, heads)], sems.at[i])
            )
    for copy in copies:
        copy.start()
    for copy in copies:
        copy.wait()


def put_in_place(place, pieces, peers, chunks, share):
    _, rows, dim = pieces[0].shape
    return pl.pallas_call(
        functools.partial(place_kernel, peers, chunks, share),
        out_shape=jax.ShapeDtypeStruct((peers * share, rows, dim), jnp.bfloat16),
        in_specs=[pl.BlockSpec(memory_space=pltpu.SMEM)]
        + [pl.BlockSpec(memory_space=pltpu.VMEM)] * len(pieces),
        out_specs=pl.BlockSpec(memory_space=pl.ANY),
        scratch_shapes=[pltpu.SemaphoreType.DMA((len(pieces),))],
        compiler_params=pltpu.CompilerParams(vmem_limit_bytes=VMEM_BYTES),
        name="put_in_place",
    )(place, *pieces)


def regrouping(tok_peers, rows, heads, dim, hid):
    half_peers = tok_peers // 2
    peers = math.gcd(half_peers, heads)
    fits = tok_peers % 2 == 0 and half_peers * rows == 2 * HALF
    fits = fits and half_peers == 2 * peers and peers & (peers - 1) == 0
    fits = fits and rows % 256 == 0 and dim == 128 and hid % 256 == 0
    return peers if fits else 0


def regrouped_body(
    peers,
    query_rows,
    key_rows,
    value_rows,
    query_gain,
    key_gain,
    rate_in,
    rate_out,
    fast_in,
    fast_out,
    half_window,
    boundaries,
):
    rows, heads, dim = query_rows.shape
    share = heads // peers
    tok_peers = lax.axis_size("tok")
    half_peers = tok_peers // 2
    width_all = heads * dim * lax.axis_size("head")
    chunks = [(0, (share + 1) // 2), ((share + 1) // 2, share // 2)]
    aux_rows = 2 * -(-max(4 * (rows // 128), 3 * -(-share // chunks[0][1])) // 16) * 16
    own_index = lax.axis_index("tok")
    half = own_index // half_peers
    chip = own_index % half_peers // 2
    core = own_index % 2
    place = jnp.stack([chip, core, half]).astype(jnp.int32)

    def dealt(sent):
        pairs = [
            [(t, t // half_peers * half_peers + ((t % half_peers) ^ (2 * p))) for t in range(tok_peers)]
            for p in range(peers)
        ]
        return [sent[0]] + [exchanged(sent[p], pairs[p]) for p in range(1, peers)]

    core_pairs = [(t, t ^ 1) for t in range(tok_peers)]
    half_pairs = [(t, (t + half_peers) % tok_peers) for t in range(tok_peers)]
    forward_pairs = [(t + half_peers, t) for t in range(half_peers)]
    back_pairs = [(t, t - 1 + half_peers) for t in range(half_peers) if t % 2 == 1]

    q = jnp.transpose(query_rows, (1, 0, 2))
    k = jnp.transpose(key_rows, (1, 0, 2))
    v = jnp.transpose(value_rows, (1, 0, 2))
    q_float = q.astype(jnp.float32)
    k_float = k.astype(jnp.float32)
    squares = jnp.stack(
        [jnp.sum(q_float * q_float, axis=(0, 2)), jnp.sum(k_float * k_float, axis=(0, 2))]
    )
    if lax.axis_size("head") == 2:
        sums = (squares, lax.ppermute(squares, "head", [(0, 1), (1, 0)]))
    else:
        sums = (lax.psum(squares, "head"), jnp.zeros_like(squares))
    fold = math.log2(math.e) / math.sqrt(dim)
    sent = [
        pack(
            place,
            sums,
            q,
            k,
            v,
            (query_gain, key_gain),
            (rate_in, rate_out),
            peers,
            aux_rows,
            first,
            count,
            width_all,
            fold,
        )
        for first, count in chunks
    ]
    received = []
    for each in sent:
        if received:
            each = [lax.optimization_barrier(pair)[0] for pair in zip(each, received[-1])]
        received.append(dealt(each))
    def finished(ready, after):
        attended, sums, patch, own, first = ready
        return finish(
            place,
            attended,
            fast_in,
            fast_out,
            sums,
            patch,
            own,
            share,
            first,
            epsilon * fold * fold,
            after,
        )

    forwarded = ready = None
    pieces = []
    for (first, count), own in zip(chunks, received):
        if ready:
            *own, _ = lax.optimization_barrier((*own, ready[1][0]))
        else:
            own = lax.optimization_barrier((*own, *sent[-1]))[:peers]
        stack = stacked(own, rows)
        packets = (own, exchanged(stack, core_pairs))
        if forwarded is None:
            forwarded = exchanged(lone_rows(place, stack, packets[1], rows), forward_pairs)
        before = [ready[0]] if ready else []
        grad = gradients(place, fast_in, fast_out, packets, share, rows, first, before)
        from_half = exchanged(grad, half_pairs)
        before = [grad]
        if ready:
            outs = finished(ready, [grad])
            before.append(outs[0])
            pieces = pieces + dealt(outs)
        attended, extra = attend(
            place,
            half_window,
            boundaries,
            packets,
            forwarded,
            share,
            rows,
            first,
            before,
        )
        patch = exchanged(extra, back_pairs)
        from_half, _ = lax.optimization_barrier((from_half, attended))
        own_sum = (grad.astype(jnp.float32) + from_half.astype(jnp.float32)).astype(jnp.bfloat16)
        ready = (attended, (own_sum, exchanged(own_sum, core_pairs)), patch, own, first)
    pieces = pieces + dealt(finished(ready, pieces))
    whole = put_in_place(place, pieces, peers, chunks, share)
    return jnp.transpose(whole, (1, 0, 2))


def body(query_rows, *others):
    rows, heads, dim = query_rows.shape
    hid = others[7].shape[1]
    peers = regrouping(lax.axis_size("tok"), rows, heads, dim, hid)
    if peers:
        return regrouped_body(peers, query_rows, *others)
    return sliding_body(query_rows, *others)


def solution(mesh):
    in_specs = (
        P("tok", "head", None),
        P("tok", "head", None),
        P("tok", "head", None),
        P("head", None),
        P("head", None),
        P("head", "tok"),
        P("head", "tok"),
        P("head", None, None),
        P("head", None, None),
        P("head"),
        P(),
    )
    out_specs = P("tok", "head", None)
    return jax.shard_map(body, mesh=mesh, in_specs=in_specs, out_specs=out_specs, check_vma=False)
```

profile of v0, /device:TPU:0, one launch (start us, length us, event | category | flops | bytes accessed | tf_op | source)
XLA Modules:
  0.0 115.0 jit_solution(10794357421574157134)
XLA Ops:
  0.0 1.8 %multiply_reduce_fusion.1 = f32[256]{0:T(256)S(1)} fusion(bf16[256,20,128]{2,0,1:T(8,128)(2,1)} %param.11), kind=kLoop, calls=%fused_computation.1 | loop fusion | flops 1965824 | bytes 1311744 | tf_op jit(solution)/shard_map/reduce_sum | solution.py:653
  1.8 0.3 multiply_reduce_fusion
  2.2 3.0 %collective-permute-start = (f32[2,256]{1,0:T(2,128)S(1)}, f32[2,256]{1,0:T(2,128)S(1)}, u32[]{:S(2)}, u32[]{:S(2)}) collective-permute-start(f32[2,256]{1,0:T(2,128)S(1)} %pad_maximum_fusion.refs_0_), channel_id=1, source_target_pairs={{0,1},{1,0},{2,3},{3,2},{4,5},{5,4},{6,7},{7,6},{8,9},{9,8},{10,11... | collective-permute-start | bytes 6152 | tf_op jit(solution)/shard_map/ppermute | solution.py:656
  5.2 0.1 pad_add_fusion.place_ref
  5.3 1.5 %collective-permute-done.refs_1_ = f32[2,256]{1,0:T(2,128)S(1)} collective-permute-done((f32[2,256]{1,0:T(2,128)S(1)}, f32[2,256]{1,0:T(2,128)S(1)}, u32[]{:S(2)}, u32[]{:S(2)}) %collective-permute-start) | collective-permute-done | bytes 2080 | tf_op jit(solution)/shard_map/ppermute | solution.py:656
  6.8 1.3 %copy-done.3 = bf16[256,20,128]{2,0,1:T(8,128)(2,1)S(1)} copy-done((bf16[256,20,128]{2,0,1:T(8,128)(2,1)S(1)}, bf16[256,20,128]{2,0,1:T(8,128)(2,1)}, u32[]{:S(2)}) %copy-start.3) | copy-done | bytes 1310744
  8.1 1.3 %pack.2 = (bf16[3,800,128]{2,1,0:T(8,128)(2,1)S(1)}, bf16[3,800,128]{2,1,0:T(8,128)(2,1)S(1)}, bf16[3,800,128]{2,1,0:T(8,128)(2,1)S(1)}, bf16[3,800,128]{2,1,0:T(8,128)(2,1)S(1)}) custom-call(s32[3]{0:T(128)S(1)} %pad_add_fusion.place_ref, f32[2,256]{1,0:T(2,128)S(1)} %pad_maximum_fusion.refs_0_, f32[2,256]{1,0:T(2,128)S(1)} %collective-permute-done.refs_1_, ...), custom_call_target="tpu_custom_call" | custom-call | tf_op jit(solution)/shard_map/pack/pallas_call | solution.py:176
  9.5 2.1 %collective-permute-start.1 = (bf16[3,800,128]{2,1,0:T(8,128)(2,1)S(1)}, bf16[3,800,128]{2,1,0:T(8,128)(2,1)S(1)}, u32[]{:S(2)}, u32[]{:S(2)}) collective-permute-start(bf16[3,800,128]{2,1,0:T(8,128)(2,1)S(1)} %get-tuple-element.40), channel_id=1, source_target_pairs={{0,4},{2,6},{4,0},{6,2},{8,12},{10,14},{12,8},{14,10},{16,20},{18,... | collective-permute-start | bytes 1843208 | tf_op jit(solution)/shard_map/ppermute | solution.py:161
  11.6 1.6 %collective-permute-start.2 = (bf16[3,800,128]{2,1,0:T(8,128)(2,1)S(1)}, bf16[3,800,128]{2,1,0:T(8,128)(2,1)S(1)}, u32[]{:S(2)}, u32[]{:S(2)}) collective-permute-start(bf16[3,800,128]{2,1,0:T(8,128)(2,1)S(1)} %get-tuple-element.41), channel_id=1, source_target_pairs={{0,8},{2,10},{4,12},{6,14},{8,0},{10,2},{12,4},{14,6},{16,24},{18,... | collective-permute-start | bytes 1843208 | tf_op jit(solution)/shard_map/ppermute | solution.py:161
  13.1 1.1 pack.3
  14.2 11.1 %collective-permute-done.1.refs_1_.refs_7_ = bf16[3,800,128]{2,1,0:T(8,128)(2,1)S(1)} collective-permute-done((bf16[3,800,128]{2,1,0:T(8,128)(2,1)S(1)}, bf16[3,800,128]{2,1,0:T(8,128)(2,1)S(1)}, u32[]{:S(2)}, u32[]{:S(2)}) %collective-permute-start.1) | collective-permute-done | bytes 614432 | tf_op jit(solution)/shard_map/ppermute | solution.py:161
  25.4 3.0 %collective-permute-done.2.refs_2_.refs_8_ = bf16[3,800,128]{2,1,0:T(8,128)(2,1)S(1)} collective-permute-done((bf16[3,800,128]{2,1,0:T(8,128)(2,1)S(1)}, bf16[3,800,128]{2,1,0:T(8,128)(2,1)S(1)}, u32[]{:S(2)}, u32[]{:S(2)}) %collective-permute-start.2) | collective-permute-done | bytes 614432 | tf_op jit(solution)/shard_map/ppermute | solution.py:161
  28.4 10.3 %collective-permute-done.3.refs_3_.refs_9_ = bf16[3,800,128]{2,1,0:T(8,128)(2,1)S(1)} collective-permute-done((bf16[3,800,128]{2,1,0:T(8,128)(2,1)S(1)}, bf16[3,800,128]{2,1,0:T(8,128)(2,1)S(1)}, u32[]{:S(2)}, u32[]{:S(2)}) %collective-permute-start.3) | collective-permute-done | bytes 614432 | tf_op jit(solution)/shard_map/ppermute | solution.py:161
  38.7 0.1 stack.30.own_ref
  38.8 0.1 collective-permute-start.4
  38.9 3.5 %collective-permute-done.4.other_ref.refs_4_ = bf16[4,3,544,128]{3,2,1,0:T(8,128)(2,1)S(1)} collective-permute-done((bf16[4,3,544,128]{3,2,1,0:T(8,128)(2,1)S(1)}, bf16[4,3,544,128]{3,2,1,0:T(8,128)(2,1)S(1)}, u32[]{:S(2)}, u32[]{:S(2)}) %collective-permute-start.4) | collective-permute-done | bytes 1671200 | tf_op jit(solution)/shard_map/ppermute | solution.py:161
  42.4 0.6 lone_rows.1
  43.0 1.3 %collective-permute-start.5 = (bf16[3,16,128]{2,1,0:T(8,128)(2,1)S(1)}, bf16[3,16,128]{2,1,0:T(8,128)(2,1)S(1)}, u32[]{:S(2)}, u32[]{:S(2)}) collective-permute-start(bf16[3,16,128]{2,1,0:T(8,128)(2,1)S(1)} %lone_rows.1), channel_id=1, source_target_pairs={{16,0},{18,2},{20,4},{22,6},{24,8},{26,10},{28,12},{30,14},{17,1},... | collective-permute-start | bytes 36872 | tf_op jit(solution)/shard_map/ppermute | solution.py:161
  44.3 1.8 %collective-permute-start.10 = (bf16[2,784,128]{2,1,0:T(8,128)(2,1)S(1)}, bf16[2,784,128]{2,1,0:T(8,128)(2,1)S(1)}, u32[]{:S(2)}, u32[]{:S(2)}) collective-permute-start(bf16[2,784,128]{2,1,0:T(8,128)(2,1)S(1)} %get-tuple-element.56), channel_id=1, source_target_pairs={{0,8},{2,10},{4,12},{6,14},{8,0},{10,2},{12,4},{14,6},{16,24},{18,... | collective-permute-start | bytes 1204232 | tf_op jit(solution)/shard_map/ppermute | solution.py:161
  46.1 1.4 %collective-permute-start.11 = (bf16[2,784,128]{2,1,0:T(8,128)(2,1)S(1)}, bf16[2,784,128]{2,1,0:T(8,128)(2,1)S(1)}, u32[]{:S(2)}, u32[]{:S(2)}) collective-permute-start(bf16[2,784,128]{2,1,0:T(8,128)(2,1)S(1)} %get-tuple-element.57), channel_id=1, source_target_pairs={{0,12},{2,14},{4,8},{6,10},{8,4},{10,6},{12,0},{14,2},{16,28},{18,... | collective-permute-start | bytes 1204232 | tf_op jit(solution)/shard_map/ppermute | solution.py:161
  47.5 0.4 collective-permute-start.9
  47.9 6.1 %gradients.2.refs_6_ = bf16[3,384,128]{2,1,0:T(8,128)(2,1)S(1)} custom-call(s32[3]{0:T(128)S(1)} %pad_add_fusion.place_ref, bf16[20,128,512]{2,1,0:T(8,128)(2,1)S(1)} %copy-done.2, bf16[20,256,128]{2,1,0:T(8,128)(2,1)S(1)} %copy-done.4, bf16[3,800,128]{2,1,0:T(8,128)(2,1)S(1)} %get-tuple-element.47.refs_0_.refs_6_, ...), custom_call_target="tpu_custom_call" | custom-call | tf_op jit(solution)/shard_map/gradients/pallas_call | solution.py:176
  54.0 3.6 %collective-permute-start.6 = (bf16[3,384,128]{2,1,0:T(8,128)(2,1)S(1)}, bf16[3,384,128]{2,1,0:T(8,128)(2,1)S(1)}, u32[]{:S(2)}, u32[]{:S(2)}) collective-permute-start(bf16[3,384,128]{2,1,0:T(8,128)(2,1)S(1)} %gradients.2.refs_6_), channel_id=1, source_target_pairs={{0,16},{2,18},{4,20},{6,22},{8,24},{10,26},{12,28},{14,30},{16,0},... | collective-permute-start | bytes 884744 | tf_op jit(solution)/shard_map/ppermute | solution.py:161
  57.6 14.9 %attend.2 = (f32[4,3,256,128]{3,2,1,0:T(8,128)S(1)}, f32[3,16,128]{2,1,0:T(8,128)S(1)}) custom-call(s32[3]{0:T(128)S(1)} %pad_add_fusion.place_ref, s32[20]{0:T(128)S(1)} %copy-done.9, s32[3]{0:T(128)S(1)} %copy-done.10, bf16[3,800,128]{2,1,0:T(8,128)(2,1)S(1)} %get-tuple-element.47.refs_0_.refs_6_, ...), custom_call_target="tpu_custom_call" | custom-call | flops 51539607552 | tf_op jit(solution)/shard_map/attend/pallas_call | solution.py:176
  72.5 0.1 add_convert_fusion.refs_3_
  72.6 0.1 stack.31
  72.7 0.1 collective-permute-start.12
  72.8 0.5 collective-permute-start.7
  73.3 0.7 collective-permute-start.8
  73.9 1.5 %collective-permute-done.12.refs_4_ = bf16[4,2,528,128]{3,2,1,0:T(8,128)(2,1)S(1)} collective-permute-done((bf16[4,2,528,128]{3,2,1,0:T(8,128)(2,1)S(1)}, bf16[4,2,528,128]{3,2,1,0:T(8,128)(2,1)S(1)}, u32[]{:S(2)}, u32[]{:S(2)}) %collective-permute-start.12) | collective-permute-done | bytes 1081376 | tf_op jit(solution)/shard_map/ppermute | solution.py:161
  75.5 4.2 %gradients.3.refs_10_.refs_6_ = bf16[2,384,128]{2,1,0:T(8,128)(2,1)S(1)} custom-call(s32[3]{0:T(128)S(1)} %pad_add_fusion.place_ref, bf16[20,128,512]{2,1,0:T(8,128)(2,1)S(1)} %copy-done.2, bf16[20,256,128]{2,1,0:T(8,128)(2,1)S(1)} %copy-done.4, bf16[2,784,128]{2,1,0:T(8,128)(2,1)S(1)} %get-tuple-element.58.refs_0_.refs_6_, ...), custom_call_target="tpu_custom_call" | custom-call | tf_op jit(solution)/shard_map/gradients/pallas_call | solution.py:176
  79.7 0.9 collective-permute-start.16
  80.6 4.0 %finish.2 = (bf16[3,256,128]{2,1,0:T(8,128)(2,1)S(1)}, bf16[3,256,128]{2,1,0:T(8,128)(2,1)S(1)}, bf16[3,256,128]{2,1,0:T(8,128)(2,1)S(1)}, bf16[3,256,128]{2,1,0:T(8,128)(2,1)S(1)}) custom-call(s32[3]{0:T(128)S(1)} %pad_add_fusion.place_ref, f32[4,3,256,128]{3,2,1,0:T(8,128)S(1)} %get-tuple-element.51.refs_5_.refs_0_, bf16[20,128,512]{2,1,0:T(8,128)(2,1)S(1)} %copy-done.2, ...), custom_call_target="tpu_custom_call" | custom-call | flops 19327352832 | tf_op jit(solution)/shard_map/finish/pallas_call | solution.py:176
  84.6 1.6 %collective-permute-start.13 = (bf16[3,256,128]{2,1,0:T(8,128)(2,1)S(1)}, bf16[3,256,128]{2,1,0:T(8,128)(2,1)S(1)}, u32[]{:S(2)}, u32[]{:S(2)}) collective-permute-start(bf16[3,256,128]{2,1,0:T(8,128)(2,1)S(1)} %get-tuple-element.63), channel_id=1, source_target_pairs={{0,4},{2,6},{4,0},{6,2},{8,12},{10,14},{12,8},{14,10},{16,20},{18,... | collective-permute-start | bytes 589832 | tf_op jit(solution)/shard_map/ppermute | solution.py:161
  86.2 2.1 %collective-permute-start.14 = (bf16[3,256,128]{2,1,0:T(8,128)(2,1)S(1)}, bf16[3,256,128]{2,1,0:T(8,128)(2,1)S(1)}, u32[]{:S(2)}, u32[]{:S(2)}) collective-permute-start(bf16[3,256,128]{2,1,0:T(8,128)(2,1)S(1)} %get-tuple-element.64), channel_id=1, source_target_pairs={{0,8},{2,10},{4,12},{6,14},{8,0},{10,2},{12,4},{14,6},{16,24},{18,... | collective-permute-start | bytes 589832 | tf_op jit(solution)/shard_map/ppermute | solution.py:161
  88.3 1.0 collective-permute-start.15
  89.3 10.0 %attend.3 = (f32[4,2,256,128]{3,2,1,0:T(8,128)S(1)}, f32[2,16,128]{2,1,0:T(8,128)S(1)}) custom-call(s32[3]{0:T(128)S(1)} %pad_add_fusion.place_ref, s32[20]{0:T(128)S(1)} %copy-done.9, s32[3]{0:T(128)S(1)} %copy-done.10, bf16[2,784,128]{2,1,0:T(8,128)(2,1)S(1)} %get-tuple-element.58.refs_0_.refs_6_, ...), custom_call_target="tpu_custom_call" | custom-call | flops 34359738368 | tf_op jit(solution)/shard_map/attend/pallas_call | solution.py:176
  99.4 0.7 collective-permute-start.18
  100.1 0.4 collective-permute-done.15.refs_13_.refs_3_
  100.5 0.4 collective-permute-done.17.refs_4_
  100.9 2.8 %finish.3 = (bf16[2,256,128]{2,1,0:T(8,128)(2,1)S(1)}, bf16[2,256,128]{2,1,0:T(8,128)(2,1)S(1)}, bf16[2,256,128]{2,1,0:T(8,128)(2,1)S(1)}, bf16[2,256,128]{2,1,0:T(8,128)(2,1)S(1)}) custom-call(s32[3]{0:T(128)S(1)} %pad_add_fusion.place_ref, f32[4,2,256,128]{3,2,1,0:T(8,128)S(1)} %get-tuple-element.66.refs_0_, bf16[20,128,512]{2,1,0:T(8,128)(2,1)S(1)} %copy-done.2, ...), custom_call_target="tpu_custom_call" | custom-call | flops 12884901888 | tf_op jit(solution)/shard_map/finish/pallas_call | solution.py:176
  103.7 0.6 collective-permute-start.19
  104.3 0.6 collective-permute-start.20
  104.9 2.4 %collective-permute-start.21 = (bf16[2,256,128]{2,1,0:T(8,128)(2,1)S(1)}, bf16[2,256,128]{2,1,0:T(8,128)(2,1)S(1)}, u32[]{:S(2)}, u32[]{:S(2)}) collective-permute-start(bf16[2,256,128]{2,1,0:T(8,128)(2,1)S(1)} %get-tuple-element.72), channel_id=1, source_target_pairs={{0,12},{2,14},{4,8},{6,10},{8,4},{10,6},{12,0},{14,2},{16,28},{18,... | collective-permute-start | bytes 393224 | tf_op jit(solution)/shard_map/ppermute | solution.py:161
  107.3 1.5 %collective-permute-done.19.refs_5_ = bf16[2,256,128]{2,1,0:T(8,128)(2,1)S(1)} collective-permute-done((bf16[2,256,128]{2,1,0:T(8,128)(2,1)S(1)}, bf16[2,256,128]{2,1,0:T(8,128)(2,1)S(1)}, u32[]{:S(2)}, u32[]{:S(2)}) %collective-permute-start.19) | collective-permute-done | bytes 131104 | tf_op jit(solution)/shard_map/ppermute | solution.py:161
  108.7 0.9 collective-permute-done.20.refs_6_
  109.6 3.5 %collective-permute-done.21.refs_7_ = bf16[2,256,128]{2,1,0:T(8,128)(2,1)S(1)} collective-permute-done((bf16[2,256,128]{2,1,0:T(8,128)(2,1)S(1)}, bf16[2,256,128]{2,1,0:T(8,128)(2,1)S(1)}, u32[]{:S(2)}, u32[]{:S(2)}) %collective-permute-start.21) | collective-permute-done | bytes 131104 | tf_op jit(solution)/shard_map/ppermute | solution.py:161
  113.1 1.7 %put_in_place.1 = bf16[20,256,128]{2,1,0:T(8,128)(2,1)} custom-call(s32[3]{0:T(128)S(1)} %pad_add_fusion.place_ref, bf16[3,256,128]{2,1,0:T(8,128)(2,1)S(1)} %get-tuple-element.62.refs_7_.refs_10_.refs_0_, bf16[3,256,128]{2,1,0:T(8,128)(2,1)S(1)} %collective-permute-done.13.refs_11_.refs_1_, ...), custom_call_target="tpu_custom_call" | custom-call | tf_op jit(solution)/shard_map/put_in_place/pallas_call | solution.py:587
  (36 shorter events, 0.2 us)
Async XLA Ops:
  0.0 1.8 %copy-start = (bf16[256,20,128]{2,0,1:T(8,128)(2,1)S(1)}, bf16[256,20,128]{2,0,1:T(8,128)(2,1)}, u32[]{:S(2)}) copy-start(bf16[256,20,128]{2,0,1:T(8,128)(2,1)} %param.12) | copy-start | bytes 3932164
  0.0 6.8 %copy-start.1 = (bf16[256,20,128]{2,0,1:T(8,128)(2,1)S(1)}, bf16[256,20,128]{2,0,1:T(8,128)(2,1)}, u32[]{:S(2)}) copy-start(bf16[256,20,128]{2,0,1:T(8,128)(2,1)} %param.11) | copy-start | bytes 3932164
  0.0 6.8 %copy-start.7 = (f32[20,128]{1,0:T(8,128)S(1)}, f32[20,128]{1,0:T(8,128)}, u32[]{:S(2)}) copy-start(f32[20,128]{1,0:T(8,128)} %refs_2_.5) | copy-start | bytes 30724
  0.0 6.8 %copy-start.8 = (f32[20,128]{1,0:T(8,128)S(1)}, f32[20,128]{1,0:T(8,128)}, u32[]{:S(2)}) copy-start(f32[20,128]{1,0:T(8,128)} %refs_3_.3) | copy-start | bytes 30724
  0.0 6.8 %copy-start.5 = (f32[20,256]{1,0:T(8,128)S(1)}, f32[20,256]{1,0:T(8,128)}, u32[]{:S(2)}) copy-start(f32[20,256]{1,0:T(8,128)} %refs_4_.3) | copy-start | bytes 61444
  0.0 6.8 %copy-start.6 = (f32[20,256]{1,0:T(8,128)S(1)}, f32[20,256]{1,0:T(8,128)}, u32[]{:S(2)}) copy-start(f32[20,256]{1,0:T(8,128)} %refs_5_.3) | copy-start | bytes 61444
  2.2 4.6 %collective-permute-start = (f32[2,256]{1,0:T(2,128)S(1)}, f32[2,256]{1,0:T(2,128)S(1)}, u32[]{:S(2)}, u32[]{:S(2)}) collective-permute-start(f32[2,256]{1,0:T(2,128)S(1)} %pad_maximum_fusion.refs_0_), channel_id=1, source_target_pairs={{0,1},{1,0},{2,3},{3,2},{4,5},{5,4},{6,7},{7,6},{8,9},{9,8},{10,11... | collective-permute-start | bytes 6152 | tf_op jit(solution)/shard_map/ppermute | solution.py:656
  6.8 1.3 %copy-start.3 = (bf16[256,20,128]{2,0,1:T(8,128)(2,1)S(1)}, bf16[256,20,128]{2,0,1:T(8,128)(2,1)}, u32[]{:S(2)}) copy-start(bf16[256,20,128]{2,0,1:T(8,128)(2,1)} %param.13) | copy-start | bytes 3932164
  9.5 15.9 %collective-permute-start.1 = (bf16[3,800,128]{2,1,0:T(8,128)(2,1)S(1)}, bf16[3,800,128]{2,1,0:T(8,128)(2,1)S(1)}, u32[]{:S(2)}, u32[]{:S(2)}) collective-permute-start(bf16[3,800,128]{2,1,0:T(8,128)(2,1)S(1)} %get-tuple-element.40), channel_id=1, source_target_pairs={{0,4},{2,6},{4,0},{6,2},{8,12},{10,14},{12,8},{14,10},{16,20},{18,... | collective-permute-start | bytes 1843208 | tf_op jit(solution)/shard_map/ppermute | solution.py:161
  11.6 16.8 %collective-permute-start.2 = (bf16[3,800,128]{2,1,0:T(8,128)(2,1)S(1)}, bf16[3,800,128]{2,1,0:T(8,128)(2,1)S(1)}, u32[]{:S(2)}, u32[]{:S(2)}) collective-permute-start(bf16[3,800,128]{2,1,0:T(8,128)(2,1)S(1)} %get-tuple-element.41), channel_id=1, source_target_pairs={{0,8},{2,10},{4,12},{6,14},{8,0},{10,2},{12,4},{14,6},{16,24},{18,... | collective-permute-start | bytes 1843208 | tf_op jit(solution)/shard_map/ppermute | solution.py:161
  13.1 25.6 %collective-permute-start.3 = (bf16[3,800,128]{2,1,0:T(8,128)(2,1)S(1)}, bf16[3,800,128]{2,1,0:T(8,128)(2,1)S(1)}, u32[]{:S(2)}, u32[]{:S(2)}) collective-permute-start(bf16[3,800,128]{2,1,0:T(8,128)(2,1)S(1)} %get-tuple-element.42), channel_id=1, source_target_pairs={{0,12},{2,14},{4,8},{6,10},{8,4},{10,6},{12,0},{14,2},{16,28},{18,... | collective-permute-start | bytes 1843208 | tf_op jit(solution)/shard_map/ppermute | solution.py:161
  38.7 9.2 %copy-start.4 = (bf16[20,256,128]{2,1,0:T(8,128)(2,1)S(1)}, bf16[20,256,128]{2,1,0:T(8,128)(2,1)}, u32[]{:S(2)}) copy-start(bf16[20,256,128]{2,1,0:T(8,128)(2,1)} %refs_2_.7) | copy-start | bytes 3932164
  38.8 9.1 %copy-start.2 = (bf16[20,128,512]{2,1,0:T(8,128)(2,1)S(1)}, bf16[20,128,512]{2,1,0:T(8,128)(2,1)}, u32[]{:S(2)}) copy-start(bf16[20,128,512]{2,1,0:T(8,128)(2,1)} %refs_1_.3) | copy-start | bytes 7864324
  38.8 3.6 %collective-permute-start.4 = (bf16[4,3,544,128]{3,2,1,0:T(8,128)(2,1)S(1)}, bf16[4,3,544,128]{3,2,1,0:T(8,128)(2,1)S(1)}, u32[]{:S(2)}, u32[]{:S(2)}) collective-permute-start(bf16[4,3,544,128]{3,2,1,0:T(8,128)(2,1)S(1)} %stack.30.own_ref), channel_id=1, source_target_pairs={{0,2},{2,0},{4,6},{6,4},{8,10},{10,8},{12,14},{14,12},{16,18},{18,... | collective-permute-start | bytes 5013512 | tf_op jit(solution)/shard_map/ppermute | solution.py:161
  43.0 14.6 %copy-start.9 = (s32[20]{0:T(128)S(1)}, s32[20]{0:T(128)}, u32[]{:S(2)}) copy-start(s32[20]{0:T(128)} %window_ref.3) | copy-start | bytes 244
  43.0 14.6 %copy-start.10 = (s32[3]{0:T(128)S(1)}, s32[3]{0:T(128)}, u32[]{:S(2)}) copy-start(s32[3]{0:T(128)} %edge_ref.3) | copy-start | bytes 40
  43.0 14.6 %collective-permute-start.5 = (bf16[3,16,128]{2,1,0:T(8,128)(2,1)S(1)}, bf16[3,16,128]{2,1,0:T(8,128)(2,1)S(1)}, u32[]{:S(2)}, u32[]{:S(2)}) collective-permute-start(bf16[3,16,128]{2,1,0:T(8,128)(2,1)S(1)} %lone_rows.1), channel_id=1, source_target_pairs={{16,0},{18,2},{20,4},{22,6},{24,8},{26,10},{28,12},{30,14},{17,1},... | collective-permute-start | bytes 36872 | tf_op jit(solution)/shard_map/ppermute | solution.py:161
  44.3 28.3 %collective-permute-start.10 = (bf16[2,784,128]{2,1,0:T(8,128)(2,1)S(1)}, bf16[2,784,128]{2,1,0:T(8,128)(2,1)S(1)}, u32[]{:S(2)}, u32[]{:S(2)}) collective-permute-start(bf16[2,784,128]{2,1,0:T(8,128)(2,1)S(1)} %get-tuple-element.56), channel_id=1, source_target_pairs={{0,8},{2,10},{4,12},{6,14},{8,0},{10,2},{12,4},{14,6},{16,24},{18,... | collective-permute-start | bytes 1204232 | tf_op jit(solution)/shard_map/ppermute | solution.py:161
  46.1 26.5 %collective-permute-start.11 = (bf16[2,784,128]{2,1,0:T(8,128)(2,1)S(1)}, bf16[2,784,128]{2,1,0:T(8,128)(2,1)S(1)}, u32[]{:S(2)}, u32[]{:S(2)}) collective-permute-start(bf16[2,784,128]{2,1,0:T(8,128)(2,1)S(1)} %get-tuple-element.57), channel_id=1, source_target_pairs={{0,12},{2,14},{4,8},{6,10},{8,4},{10,6},{12,0},{14,2},{16,28},{18,... | collective-permute-start | bytes 1204232 | tf_op jit(solution)/shard_map/ppermute | solution.py:161
  47.5 25.1 %collective-permute-start.9 = (bf16[2,784,128]{2,1,0:T(8,128)(2,1)S(1)}, bf16[2,784,128]{2,1,0:T(8,128)(2,1)S(1)}, u32[]{:S(2)}, u32[]{:S(2)}) collective-permute-start(bf16[2,784,128]{2,1,0:T(8,128)(2,1)S(1)} %get-tuple-element.55), channel_id=1, source_target_pairs={{0,4},{2,6},{4,0},{6,2},{8,12},{10,14},{12,8},{14,10},{16,20},{18,... | collective-permute-start | bytes 1204232 | tf_op jit(solution)/shard_map/ppermute | solution.py:161
  54.0 18.5 %collective-permute-start.6 = (bf16[3,384,128]{2,1,0:T(8,128)(2,1)S(1)}, bf16[3,384,128]{2,1,0:T(8,128)(2,1)S(1)}, u32[]{:S(2)}, u32[]{:S(2)}) collective-permute-start(bf16[3,384,128]{2,1,0:T(8,128)(2,1)S(1)} %gradients.2.refs_6_), channel_id=1, source_target_pairs={{0,16},{2,18},{4,20},{6,22},{8,24},{10,26},{12,28},{14,30},{16,0},... | collective-permute-start | bytes 884744 | tf_op jit(solution)/shard_map/ppermute | solution.py:161
  72.7 2.8 %collective-permute-start.12 = (bf16[4,2,528,128]{3,2,1,0:T(8,128)(2,1)S(1)}, bf16[4,2,528,128]{3,2,1,0:T(8,128)(2,1)S(1)}, u32[]{:S(2)}, u32[]{:S(2)}) collective-permute-start(bf16[4,2,528,128]{3,2,1,0:T(8,128)(2,1)S(1)} %stack.31), channel_id=1, source_target_pairs={{0,2},{2,0},{4,6},{6,4},{8,10},{10,8},{12,14},{14,12},{16,18},{18,... | collective-permute-start | bytes 3244040 | tf_op jit(solution)/shard_map/ppermute | solution.py:161
  72.8 7.8 %collective-permute-start.7 = (bf16[3,384,128]{2,1,0:T(8,128)(2,1)S(1)}, bf16[3,384,128]{2,1,0:T(8,128)(2,1)S(1)}, u32[]{:S(2)}, u32[]{:S(2)}) collective-permute-start(bf16[3,384,128]{2,1,0:T(8,128)(2,1)S(1)} %add_convert_fusion.refs_3_), channel_id=1, source_target_pairs={{0,2},{2,0},{4,6},{6,4},{8,10},{10,8},{12,14},{14,12},{16,18},{18,... | collective-permute-start | bytes 884744 | tf_op jit(solution)/shard_map/ppermute | solution.py:161
  73.3 7.3 %collective-permute-start.8 = (f32[3,16,128]{2,1,0:T(8,128)S(1)}, f32[3,16,128]{2,1,0:T(8,128)S(1)}, u32[]{:S(2)}, u32[]{:S(2)}) collective-permute-start(f32[3,16,128]{2,1,0:T(8,128)S(1)} %get-tuple-element.53), channel_id=1, source_target_pairs={{2,16},{6,20},{10,24},{14,28},{3,17},{7,21},{11,25},{15,29}} | collective-permute-start | bytes 73736 | tf_op jit(solution)/shard_map/ppermute | solution.py:161
  79.7 19.6 %collective-permute-start.16 = (bf16[2,384,128]{2,1,0:T(8,128)(2,1)S(1)}, bf16[2,384,128]{2,1,0:T(8,128)(2,1)S(1)}, u32[]{:S(2)}, u32[]{:S(2)}) collective-permute-start(bf16[2,384,128]{2,1,0:T(8,128)(2,1)S(1)} %gradients.3.refs_10_.refs_6_), channel_id=1, source_target_pairs={{0,16},{2,18},{4,20},{6,22},{8,24},{10,26},{12,28},{14,30},{16,0},... | collective-permute-start | bytes 589832 | tf_op jit(solution)/shard_map/ppermute | solution.py:161
  84.6 15.5 %collective-permute-start.13 = (bf16[3,256,128]{2,1,0:T(8,128)(2,1)S(1)}, bf16[3,256,128]{2,1,0:T(8,128)(2,1)S(1)}, u32[]{:S(2)}, u32[]{:S(2)}) collective-permute-start(bf16[3,256,128]{2,1,0:T(8,128)(2,1)S(1)} %get-tuple-element.63), channel_id=1, source_target_pairs={{0,4},{2,6},{4,0},{6,2},{8,12},{10,14},{12,8},{14,10},{16,20},{18,... | collective-permute-start | bytes 589832 | tf_op jit(solution)/shard_map/ppermute | solution.py:161
  86.2 13.9 %collective-permute-start.14 = (bf16[3,256,128]{2,1,0:T(8,128)(2,1)S(1)}, bf16[3,256,128]{2,1,0:T(8,128)(2,1)S(1)}, u32[]{:S(2)}, u32[]{:S(2)}) collective-permute-start(bf16[3,256,128]{2,1,0:T(8,128)(2,1)S(1)} %get-tuple-element.64), channel_id=1, source_target_pairs={{0,8},{2,10},{4,12},{6,14},{8,0},{10,2},{12,4},{14,6},{16,24},{18,... | collective-permute-start | bytes 589832 | tf_op jit(solution)/shard_map/ppermute | solution.py:161
  88.3 12.2 %collective-permute-start.15 = (bf16[3,256,128]{2,1,0:T(8,128)(2,1)S(1)}, bf16[3,256,128]{2,1,0:T(8,128)(2,1)S(1)}, u32[]{:S(2)}, u32[]{:S(2)}) collective-permute-start(bf16[3,256,128]{2,1,0:T(8,128)(2,1)S(1)} %get-tuple-element.65), channel_id=1, source_target_pairs={{0,12},{2,14},{4,8},{6,10},{8,4},{10,6},{12,0},{14,2},{16,28},{18,... | collective-permute-start | bytes 589832 | tf_op jit(solution)/shard_map/ppermute | solution.py:161
  99.4 1.5 %collective-permute-start.17 = (bf16[2,384,128]{2,1,0:T(8,128)(2,1)S(1)}, bf16[2,384,128]{2,1,0:T(8,128)(2,1)S(1)}, u32[]{:S(2)}, u32[]{:S(2)}) collective-permute-start(bf16[2,384,128]{2,1,0:T(8,128)(2,1)S(1)} %add_convert_fusion.1.refs_3_), channel_id=1, source_target_pairs={{0,2},{2,0},{4,6},{6,4},{8,10},{10,8},{12,14},{14,12},{16,18},{18,... | collective-permute-start | bytes 589832 | tf_op jit(solution)/shard_map/ppermute | solution.py:161
  99.4 0.7 collective-permute-start.18
  103.7 5.0 %collective-permute-start.19 = (bf16[2,256,128]{2,1,0:T(8,128)(2,1)S(1)}, bf16[2,256,128]{2,1,0:T(8,128)(2,1)S(1)}, u32[]{:S(2)}, u32[]{:S(2)}) collective-permute-start(bf16[2,256,128]{2,1,0:T(8,128)(2,1)S(1)} %get-tuple-element.70), channel_id=1, source_target_pairs={{0,4},{2,6},{4,0},{6,2},{8,12},{10,14},{12,8},{14,10},{16,20},{18,... | collective-permute-start | bytes 393224 | tf_op jit(solution)/shard_map/ppermute | solution.py:161
  104.3 5.3 %collective-permute-start.20 = (bf16[2,256,128]{2,1,0:T(8,128)(2,1)S(1)}, bf16[2,256,128]{2,1,0:T(8,128)(2,1)S(1)}, u32[]{:S(2)}, u32[]{:S(2)}) collective-permute-start(bf16[2,256,128]{2,1,0:T(8,128)(2,1)S(1)} %get-tuple-element.71), channel_id=1, source_target_pairs={{0,8},{2,10},{4,12},{6,14},{8,0},{10,2},{12,4},{14,6},{16,24},{18,... | collective-permute-start | bytes 393224 | tf_op jit(solution)/shard_map/ppermute | solution.py:161
  104.9 8.3 %collective-permute-start.21 = (bf16[2,256,128]{2,1,0:T(8,128)(2,1)S(1)}, bf16[2,256,128]{2,1,0:T(8,128)(2,1)S(1)}, u32[]{:S(2)}, u32[]{:S(2)}) collective-permute-start(bf16[2,256,128]{2,1,0:T(8,128)(2,1)S(1)} %get-tuple-element.72), channel_id=1, source_target_pairs={{0,12},{2,14},{4,8},{6,10},{8,4},{10,6},{12,0},{14,2},{16,28},{18,... | collective-permute-start | bytes 393224 | tf_op jit(solution)/shard_map/ppermute | solution.py:161
where the time goes:
time: 116 us; the launch traced here: 115 us
  Pallas kernels  46.8 us (40%)
  waiting for transfers between devices  37.7 us (33%)
  starting transfers between devices  26.3 us (23%)
  other arithmetic  2.37 us (2%)
  local copies, waits for them, and re-layouts  1.36 us (1%)
    pallas_call x11, Pallas kernels, in_vmem(): pl.pallas_call(kernel, out_shape=out_shape, in_specs=specs, out_specs=jax...  45.2 us
    ppermute x21, waiting for transfers between devices, exchanged(): return lax.ppermute(x, 'tok', pairs)  36.2 us
    ppermute x21, starting transfers between devices, exchanged(): return lax.ppermute(x, 'tok', pairs)  23.3 us
    ppermute x1, starting transfers between devices, regrouped_body(): sums = (squares, lax.ppermute(squares, 'head', [(0, 1), (1, 0)]))  3.02 us
  transfers between devices with their start and end apart: 22, of which 11 were waited for; matrix products, arithmetic and copies ran while one was open for 0% of the time, Pallas kernels for 35%

commit v1 on v0

--- a/solution.py
+++ b/solution.py
@@ -273,35 +273,42 @@
     )
 
 
-def lone_kernel(place_ref, own_ref, other_ref, out_ref):
+def lone_kernel(peers, place_ref, *refs):
+    own, others, out_ref = refs[:peers], refs[peers:-1], refs[-1]
     extra = out_ref.shape[1]
-    at = own_ref.shape[2] - extra
-    mine = jnp.full(out_ref.shape, place_ref[1]) == 0
-    own = own_ref[place_ref[0], :, at:, :].astype(jnp.float32)
-    other = other_ref[place_ref[0], :, at:, :].astype(jnp.float32)
-    out_ref[...] = jnp.where(mine, own, other).astype(jnp.bfloat16)
-
-
-def lone_rows(place, own, other, rows):
-    _, count, all_rows, dim = own.shape
-    out_shape = (count, (all_rows - 2 * rows) // 2, dim)
+    blocks = [ref.at[i] for ref in others for i in range(ref.shape[0])]
+    for p in range(peers):
+        for lane, ref in enumerate((own[p], blocks[p])):
+
+            @pl.when((place_ref[0] == p) & (place_ref[1] == lane))
+            def _(ref=ref):
+                out_ref[...] = ref[:, ref.shape[1] - extra :, :]
+
+
+def lone_rows(place, packets, extra):
+    own, others = packets
+    count, _, dim = own[0].shape
     return in_vmem(
-        lone_kernel,
+        functools.partial(lone_kernel, len(own)),
         "lone_rows",
         [place],
-        [own, other],
+        [*own, *others],
         [],
-        jax.ShapeDtypeStruct(out_shape, jnp.bfloat16),
+        jax.ShapeDtypeStruct((count, extra, dim), jnp.bfloat16),
     )
 
 
 def key_value_blocks(peers, rows, step, refs):
     for p in range(peers):
         yield p, True, refs[p].at[step, rows : 2 * rows], refs[p].at[step, 2 * rows :]
-        yield p, False, refs[peers].at[p, step, 0:rows], refs[peers].at[p, step, rows:]
-
-
-def grads_kernel(peers, rows, rate_rows, share, first, place_ref, in_ref, out_ref, *refs):
+    p = 0
+    for ref in refs[peers:]:
+        for i in range(ref.shape[0]):
+            yield p, False, ref.at[i, step, 0:rows], ref.at[i, step, rows:]
+            p += 1
+
+
+def grads_kernel(peers, held, rows, rate_rows, share, first, place_ref, in_ref, out_ref, *refs):
     grad_ref = refs[-1]
     hid = out_ref.shape[1]
     part = hid // 2
@@ -319,7 +326,7 @@
         out_half = out_ref[head, pl.ds(own, part), :]
         sum_in = jnp.zeros((2 * part, in_half.shape[1]), jnp.float32)
         sum_out = jnp.zeros((part, in_half.shape[1]), jnp.float32)
-        for _, _, keys, values in key_value_blocks(peers, rows, step, refs):
+        for _, _, keys, values in key_value_blocks(peers, rows, step, refs[:held]):
             k = keys[...].astype(jnp.float32)
             v_t = jnp.concatenate([values[at : at + 128, :] for at in range(0, rows, 128)], axis=1)
             aux = values[rows : rows + 16, :].astype(jnp.float32)
@@ -352,20 +359,21 @@
 
 def gradients(place, fast_in, fast_out, packets, share, rows, first, after):
     _, hid, dim = fast_out.shape
-    own, other = packets
-    peers, heads = other.shape[:2]
+    own, others = packets
+    heads = others[0].shape[1]
+    held = len(own) + len(others)
     return in_vmem(
-        functools.partial(grads_kernel, peers, rows, rows // 128, share, first),
+        functools.partial(grads_kernel, len(own), held, rows, rows // 128, share, first),
         "gradients",
         [place],
-        [fast_in, fast_out, *own, other],
+        [fast_in, fast_out, *own, *others],
         after,
         jax.ShapeDtypeStruct((heads, 3 * hid // 2, dim), jnp.bfloat16),
     )
 
 
-def attend_kernel(peers, rows, share, first, fwd_heads, place_ref, window_ref, edge_ref, *refs):
-    fwd_ref = refs[peers + 1]
+def attend_kernel(peers, held, rows, share, first, fwd_heads, place_ref, window_ref, edge_ref, *refs):
+    fwd_ref = refs[held]
     out_ref, extra_ref, k_scr, vt_scr, q_scr = refs[-5:]
     span = 2 * peers * rows
     dim = k_scr.shape[1]
@@ -379,7 +387,7 @@
 
     def one_head(step, carry):
         window = window_ref[chip * share + first + step]
-        for p, own, keys, values in key_value_blocks(peers, rows, step, refs):
+        for p, own, keys, values in key_value_blocks(peers, rows, step, refs[:held]):
             at = pl.multiple_of(((chip ^ p) * 2 + (core if own else 1 - core)) * rows, rows)
             k_scr[pl.ds(at, rows), :] = keys[...]
             for i in range(0, rows, 128):
@@ -485,16 +493,17 @@
 
 
 def attend(place, half_window, boundaries, packets, forwarded, share, rows, first, after):
-    own, other = packets
-    peers, heads = other.shape[:2]
+    own, others = packets
+    peers, heads = len(own), others[0].shape[1]
+    held = peers + len(others)
     fwd_heads, pad, dim = forwarded.shape
     scr_rows = 2 * peers * rows + 256
     out_shapes = [(peers, heads, rows, dim), (heads, pad, dim)]
     return in_vmem(
-        functools.partial(attend_kernel, peers, rows, share, first, fwd_heads),
+        functools.partial(attend_kernel, peers, held, rows, share, first, fwd_heads),
         "attend",
         [place, half_window, boundaries],
-        [*own, other, forwarded],
+        [*own, *others, forwarded],
         after,
         [jax.ShapeDtypeStruct(shape, jnp.float32) for shape in out_shapes],
         flops=4 * heads * peers * rows * HALF * 2 * dim,
@@ -566,34 +575,39 @@
     )
 
 
-def place_kernel(peers, chunks, share, place_ref, *refs):
-    pieces, out_ref, sems = refs[:-2], refs[-2], refs[-1]
-    copies = []
-    for first, heads in chunks:
-        for p in range(peers):
-            at = (place_ref[0] ^ p) * share + first
-            i = len(copies)
-            copies.append(
-                pltpu.make_async_copy(pieces[i], out_ref.at[pl.ds(at, heads)], sems.at[i])
-            )
+def place_kernel(peers, share, first, place_ref, *refs):
+    pieces, out_ref, sems = refs[:peers], refs[-2], refs[-1]
+    heads = pieces[0].shape[0]
+    copies = [
+        pltpu.make_async_copy(
+            pieces[p],
+            out_ref.at[pl.ds((place_ref[0] ^ p) * share + first, heads)],
+            sems.at[p],
+        )
+        for p in range(peers)
+    ]
     for copy in copies:
         copy.start()
     for copy in copies:
         copy.wait()
 
 
-def put_in_place(place, pieces, peers, chunks, share):
+def put_in_place(place, pieces, whole, share, first):
+    peers = len(pieces)
     _, rows, dim = pieces[0].shape
+    anywhere = pl.BlockSpec(memory_space=pl.ANY)
     return pl.pallas_call(
-        functools.partial(place_kernel, peers, chunks, share),
+        functools.partial(place_kernel, peers, share, first),
         out_shape=jax.ShapeDtypeStruct((peers * share, rows, dim), jnp.bfloat16),
         in_specs=[pl.BlockSpec(memory_space=pltpu.SMEM)]
-        + [pl.BlockSpec(memory_space=pltpu.VMEM)] * len(pieces),
-        out_specs=pl.BlockSpec(memory_space=pl.ANY),
-        scratch_shapes=[pltpu.SemaphoreType.DMA((len(pieces),))],
+        + [pl.BlockSpec(memory_space=pltpu.VMEM)] * peers
+        + [anywhere] * len(whole),
+        out_specs=anywhere,
+        input_output_aliases={1 + peers: 0} if whole else {},
+        scratch_shapes=[pltpu.SemaphoreType.DMA((peers,))],
         compiler_params=pltpu.CompilerParams(vmem_limit_bytes=VMEM_BYTES),
         name="put_in_place",
-    )(place, *pieces)
+    )(place, *pieces, *whole)
 
 
 def regrouping(tok_peers, rows, heads, dim, hid):
@@ -703,18 +717,25 @@
             *own, _ = lax.optimization_barrier((*own, ready[1][0]))
         else:
             own = lax.optimization_barrier((*own, *sent[-1]))[:peers]
-        stack = stacked(own, rows)
-        packets = (own, exchanged(stack, core_pairs))
         if forwarded is None:
-            forwarded = exchanged(lone_rows(place, stack, packets[1], rows), forward_pairs)
+            others = [exchanged(stacked(own[:-1], rows), core_pairs)]
+            farthest, _ = lax.optimization_barrier((own[-1], others[0]))
+            own = [*own[:-1], farthest]
+            others.append(exchanged(stacked([farthest], rows), core_pairs))
+            packets = (own, others)
+            forwarded = exchanged(lone_rows(place, packets, aux_rows // 2), forward_pairs)
+        else:
+            packets = (own, [exchanged(stacked(own, rows), core_pairs)])
         before = [ready[0]] if ready else []
         grad = gradients(place, fast_in, fast_out, packets, share, rows, first, before)
         from_half = exchanged(grad, half_pairs)
         before = [grad]
+        if not ready and len(received) > 1:
+            before += received[1][1:-1]
         if ready:
             outs = finished(ready, [grad])
             before.append(outs[0])
-            pieces = pieces + dealt(outs)
+            pieces.append(dealt(outs))
         attended, extra = attend(
             place,
             half_window,
@@ -730,9 +751,11 @@
         from_half, _ = lax.optimization_barrier((from_half, attended))
         own_sum = (grad.astype(jnp.float32) + from_half.astype(jnp.float32)).astype(jnp.bfloat16)
         ready = (attended, (own_sum, exchanged(own_sum, core_pairs)), patch, own, first)
-    pieces = pieces + dealt(finished(ready, pieces))
-    whole = put_in_place(place, pieces, peers, chunks, share)
-    return jnp.transpose(whole, (1, 0, 2))
+    pieces.append(dealt(finished(ready, sum(pieces, []))))
+    whole = []
+    for (first, _), chunk_pieces in zip(chunks, pieces):
+        whole = [put_in_place(place, chunk_pieces, whole, share, first)]
+    return jnp.transpose(whole[0], (1, 0, 2))
 
 
 def body(query_rows, *others):

time: 116 us -> 119 us (1.026)
  Pallas kernels: 46.8 us -> 40.5 us
  starting transfers between devices: 26.3 us -> 31.3 us
  waiting for transfers between devices: 37.7 us -> 41.9 us
    pallas_call x11 -> x12, Pallas kernels: 45.2 us -> 37.6 us  [in_vmem(): pl.pallas_call(kernel, out_shape=out_shape, in_specs=specs, out_specs=jax...]
    ppermute x21 -> x22, starting transfers between devices: 23.3 us -> 28.2 us  [exchanged(): return lax.ppermute(x, 'tok', pairs)]
    ppermute x21 -> x22, waiting for transfers between devices: 36.2 us -> 40.4 us  [exchanged(): return lax.ppermute(x, 'tok', pairs)]
    pallas_call x1 -> x2, Pallas kernels: 1.65 us -> 2.81 us  [put_in_place(): pl.pallas_call(functools.partial(place_kernel, peers, share, first), out_...]
  transfers between devices with their start and end apart: 22 -> 23, of which waited for: 11 -> 12; matrix products, arithmetic and copies ran while one was open for 0% -> 0% of each run, Pallas kernels for 35% -> 30%
where the time goes in v1:
time: 119 us; the launch traced here: 118 us
  waiting for transfers between devices  41.9 us (35%)
  Pallas kernels  40.5 us (34%)
  starting transfers between devices  31.3 us (26%)
  other arithmetic  2.37 us (2%)
  local copies, waits for them, and re-layouts  1.36 us (1%)
    ppermute x22, waiting for transfers between devices, exchanged(): return lax.ppermute(x, 'tok', pairs)  40.4 us
    pallas_call x12, Pallas kernels, in_vmem(): pl.pallas_call(kernel, out_shape=out_shape, in_specs=specs, out_specs=jax...  37.6 us
    ppermute x22, starting transfers between devices, exchanged(): return lax.ppermute(x, 'tok', pairs)  28.2 us
    ppermute x1, starting transfers between devices, regrouped_body(): sums = (squares, lax.ppermute(squares, 'head', [(0, 1), (1, 0)]))  3.02 us
    pallas_call x2, Pallas kernels, put_in_place(): pl.pallas_call(functools.partial(place_kernel, peers, share, first), out_...  2.81 us
  transfers between devices with their start and end apart: 23, of which 12 were waited for; matrix products, arithmetic and copies ran while one was open for 0% of the time, Pallas kernels for 30%

profile of v1, /device:TPU:0, one launch (start us, length us, event | category | flops | bytes accessed | tf_op | source)
XLA Modules:
  0.0 117.8 jit_solution(13717921608074350927)
XLA Ops:
  0.0 1.8 %multiply_reduce_fusion.1 = f32[256]{0:T(256)S(1)} fusion(bf16[256,20,128]{2,0,1:T(8,128)(2,1)} %param.11), kind=kLoop, calls=%fused_computation.1 | loop fusion | flops 1965824 | bytes 1311744 | tf_op jit(solution)/shard_map/reduce_sum | solution.py:667
  1.8 0.3 multiply_reduce_fusion
  2.2 3.0 %collective-permute-start = (f32[2,256]{1,0:T(2,128)S(1)}, f32[2,256]{1,0:T(2,128)S(1)}, u32[]{:S(2)}, u32[]{:S(2)}) collective-permute-start(f32[2,256]{1,0:T(2,128)S(1)} %pad_maximum_fusion.refs_0_), channel_id=1, source_target_pairs={{0,1},{1,0},{2,3},{3,2},{4,5},{5,4},{6,7},{7,6},{8,9},{9,8},{10,11... | collective-permute-start | bytes 6152 | tf_op jit(solution)/shard_map/ppermute | solution.py:670
  5.2 0.1 pad_add_fusion.place_ref
  5.3 1.5 %collective-permute-done.refs_1_ = f32[2,256]{1,0:T(2,128)S(1)} collective-permute-done((f32[2,256]{1,0:T(2,128)S(1)}, f32[2,256]{1,0:T(2,128)S(1)}, u32[]{:S(2)}, u32[]{:S(2)}) %collective-permute-start) | collective-permute-done | bytes 2080 | tf_op jit(solution)/shard_map/ppermute | solution.py:670
  6.8 1.3 %copy-done.3 = bf16[256,20,128]{2,0,1:T(8,128)(2,1)S(1)} copy-done((bf16[256,20,128]{2,0,1:T(8,128)(2,1)S(1)}, bf16[256,20,128]{2,0,1:T(8,128)(2,1)}, u32[]{:S(2)}) %copy-start.3) | copy-done | bytes 1310744
  8.1 1.3 %pack.3 = (bf16[3,800,128]{2,1,0:T(8,128)(2,1)S(1)}, bf16[3,800,128]{2,1,0:T(8,128)(2,1)S(1)}, bf16[3,800,128]{2,1,0:T(8,128)(2,1)S(1)}, bf16[3,800,128]{2,1,0:T(8,128)(2,1)S(1)}) custom-call(s32[3]{0:T(128)S(1)} %pad_add_fusion.place_ref, f32[2,256]{1,0:T(2,128)S(1)} %pad_maximum_fusion.refs_0_, f32[2,256]{1,0:T(2,128)S(1)} %collective-permute-done.refs_1_, ...), custom_call_target="tpu_custom_call" | custom-call | tf_op jit(solution)/shard_map/pack/pallas_call | solution.py:176
  9.5 2.1 %collective-permute-start.1 = (bf16[3,800,128]{2,1,0:T(8,128)(2,1)S(1)}, bf16[3,800,128]{2,1,0:T(8,128)(2,1)S(1)}, u32[]{:S(2)}, u32[]{:S(2)}) collective-permute-start(bf16[3,800,128]{2,1,0:T(8,128)(2,1)S(1)} %get-tuple-element.44), channel_id=1, source_target_pairs={{0,4},{2,6},{4,0},{6,2},{8,12},{10,14},{12,8},{14,10},{16,20},{18,... | collective-permute-start | bytes 1843208 | tf_op jit(solution)/shard_map/ppermute | solution.py:161
  11.6 1.6 %collective-permute-start.3 = (bf16[3,800,128]{2,1,0:T(8,128)(2,1)S(1)}, bf16[3,800,128]{2,1,0:T(8,128)(2,1)S(1)}, u32[]{:S(2)}, u32[]{:S(2)}) collective-permute-start(bf16[3,800,128]{2,1,0:T(8,128)(2,1)S(1)} %get-tuple-element.47), channel_id=1, source_target_pairs={{0,8},{2,10},{4,12},{6,14},{8,0},{10,2},{12,4},{14,6},{16,24},{18,... | collective-permute-start | bytes 1843208 | tf_op jit(solution)/shard_map/ppermute | solution.py:161
  13.1 1.1 pack.2
  14.2 11.1 %collective-permute-done.1.refs_1_.refs_7_ = bf16[3,800,128]{2,1,0:T(8,128)(2,1)S(1)} collective-permute-done((bf16[3,800,128]{2,1,0:T(8,128)(2,1)S(1)}, bf16[3,800,128]{2,1,0:T(8,128)(2,1)S(1)}, u32[]{:S(2)}, u32[]{:S(2)}) %collective-permute-start.1) | collective-permute-done | bytes 614432 | tf_op jit(solution)/shard_map/ppermute | solution.py:161
  25.4 3.0 %collective-permute-done.3.refs_2_.refs_8_ = bf16[3,800,128]{2,1,0:T(8,128)(2,1)S(1)} collective-permute-done((bf16[3,800,128]{2,1,0:T(8,128)(2,1)S(1)}, bf16[3,800,128]{2,1,0:T(8,128)(2,1)S(1)}, u32[]{:S(2)}, u32[]{:S(2)}) %collective-permute-start.3) | collective-permute-done | bytes 614432 | tf_op jit(solution)/shard_map/ppermute | solution.py:161
  28.4 10.3 %collective-permute-done.5.refs_0_.refs_3_.refs_9_ = bf16[3,800,128]{2,1,0:T(8,128)(2,1)S(1)} collective-permute-done((bf16[3,800,128]{2,1,0:T(8,128)(2,1)S(1)}, bf16[3,800,128]{2,1,0:T(8,128)(2,1)S(1)}, u32[]{:S(2)}, u32[]{:S(2)}) %collective-permute-start.5) | collective-permute-done | bytes 614432 | tf_op jit(solution)/shard_map/ppermute | solution.py:161
  38.7 0.1 stack.31
  38.9 2.9 %collective-permute-done.7.refs_4_ = bf16[3,3,544,128]{3,2,1,0:T(8,128)(2,1)S(1)} collective-permute-done((bf16[3,3,544,128]{3,2,1,0:T(8,128)(2,1)S(1)}, bf16[3,3,544,128]{3,2,1,0:T(8,128)(2,1)S(1)}, u32[]{:S(2)}, u32[]{:S(2)}) %collective-permute-start.7) | collective-permute-done | bytes 1253408 | tf_op jit(solution)/shard_map/ppermute | solution.py:161
  41.9 0.2 collective-permute-start.8
  42.1 1.7 %collective-permute-start.4 = (bf16[2,784,128]{2,1,0:T(8,128)(2,1)S(1)}, bf16[2,784,128]{2,1,0:T(8,128)(2,1)S(1)}, u32[]{:S(2)}, u32[]{:S(2)}) collective-permute-start(bf16[2,784,128]{2,1,0:T(8,128)(2,1)S(1)} %get-tuple-element.48), channel_id=1, source_target_pairs={{0,8},{2,10},{4,12},{6,14},{8,0},{10,2},{12,4},{14,6},{16,24},{18,... | collective-permute-start | bytes 1204232 | tf_op jit(solution)/shard_map/ppermute | solution.py:161
  43.8 1.5 %collective-permute-start.2 = (bf16[2,784,128]{2,1,0:T(8,128)(2,1)S(1)}, bf16[2,784,128]{2,1,0:T(8,128)(2,1)S(1)}, u32[]{:S(2)}, u32[]{:S(2)}) collective-permute-start(bf16[2,784,128]{2,1,0:T(8,128)(2,1)S(1)} %get-tuple-element.45), channel_id=1, source_target_pairs={{0,4},{2,6},{4,0},{6,2},{8,12},{10,14},{12,8},{14,10},{16,20},{18,... | collective-permute-start | bytes 1204232 | tf_op jit(solution)/shard_map/ppermute | solution.py:161
  45.3 0.6 lone_rows.1
  46.0 1.3 %collective-permute-start.10 = (bf16[3,16,128]{2,1,0:T(8,128)(2,1)S(1)}, bf16[3,16,128]{2,1,0:T(8,128)(2,1)S(1)}, u32[]{:S(2)}, u32[]{:S(2)}) collective-permute-start(bf16[3,16,128]{2,1,0:T(8,128)(2,1)S(1)} %lone_rows.1), channel_id=1, source_target_pairs={{16,0},{18,2},{20,4},{22,6},{24,8},{26,10},{28,12},{30,14},{17,1},... | collective-permute-start | bytes 36872 | tf_op jit(solution)/shard_map/ppermute | solution.py:161
  47.3 1.1 collective-permute-start.6
  48.4 6.1 %gradients.2.refs_7_ = bf16[3,384,128]{2,1,0:T(8,128)(2,1)S(1)} custom-call(s32[3]{0:T(128)S(1)} %pad_add_fusion.place_ref, bf16[20,128,512]{2,1,0:T(8,128)(2,1)S(1)} %copy-done.2, bf16[20,256,128]{2,1,0:T(8,128)(2,1)S(1)} %copy-done.4, bf16[3,800,128]{2,1,0:T(8,128)(2,1)S(1)} %get-tuple-element.52.refs_0_.refs_6_, ...), custom_call_target="tpu_custom_call" | custom-call | tf_op jit(solution)/shard_map/gradients/pallas_call | solution.py:176
  54.5 3.6 %collective-permute-start.9 = (bf16[3,384,128]{2,1,0:T(8,128)(2,1)S(1)}, bf16[3,384,128]{2,1,0:T(8,128)(2,1)S(1)}, u32[]{:S(2)}, u32[]{:S(2)}) collective-permute-start(bf16[3,384,128]{2,1,0:T(8,128)(2,1)S(1)} %gradients.2.refs_7_), channel_id=1, source_target_pairs={{0,16},{2,18},{4,20},{6,22},{8,24},{10,26},{12,28},{14,30},{16,0},... | collective-permute-start | bytes 884744 | tf_op jit(solution)/shard_map/ppermute | solution.py:161
  58.1 0.7 collective-permute-done.2.refs_8_.refs_1_.refs_7_
  58.8 10.4 %attend.2 = (f32[4,3,256,128]{3,2,1,0:T(8,128)S(1)}, f32[3,16,128]{2,1,0:T(8,128)S(1)}) custom-call(s32[3]{0:T(128)S(1)} %pad_add_fusion.place_ref, s32[20]{0:T(128)S(1)} %copy-done.9, s32[3]{0:T(128)S(1)} %copy-done.10, bf16[3,800,128]{2,1,0:T(8,128)(2,1)S(1)} %get-tuple-element.52.refs_0_.refs_6_, ...), custom_call_target="tpu_custom_call" | custom-call | flops 51539607552 | tf_op jit(solution)/shard_map/attend/pallas_call | solution.py:176
  69.2 2.0 %collective-permute-done.9 = bf16[3,384,128]{2,1,0:T(8,128)(2,1)S(1)} collective-permute-done((bf16[3,384,128]{2,1,0:T(8,128)(2,1)S(1)}, bf16[3,384,128]{2,1,0:T(8,128)(2,1)S(1)}, u32[]{:S(2)}, u32[]{:S(2)}) %collective-permute-start.9) | collective-permute-done | bytes 294944 | tf_op jit(solution)/shard_map/ppermute | solution.py:161
  71.2 0.1 add_convert_fusion.refs_3_
  71.3 0.1 stack.33
  71.4 0.5 collective-permute-start.12
  71.9 0.7 collective-permute-start.13
  72.6 1.5 %collective-permute-done.11.refs_4_ = bf16[4,2,528,128]{3,2,1,0:T(8,128)(2,1)S(1)} collective-permute-done((bf16[4,2,528,128]{3,2,1,0:T(8,128)(2,1)S(1)}, bf16[4,2,528,128]{3,2,1,0:T(8,128)(2,1)S(1)}, u32[]{:S(2)}, u32[]{:S(2)}) %collective-permute-start.11) | collective-permute-done | bytes 1081376 | tf_op jit(solution)/shard_map/ppermute | solution.py:161
  74.1 4.2 %gradients.3.refs_10_.refs_6_ = bf16[2,384,128]{2,1,0:T(8,128)(2,1)S(1)} custom-call(s32[3]{0:T(128)S(1)} %pad_add_fusion.place_ref, bf16[20,128,512]{2,1,0:T(8,128)(2,1)S(1)} %copy-done.2, bf16[20,256,128]{2,1,0:T(8,128)(2,1)S(1)} %copy-done.4, bf16[2,784,128]{2,1,0:T(8,128)(2,1)S(1)} %get-tuple-element.59.refs_0_.refs_6_, ...), custom_call_target="tpu_custom_call" | custom-call | tf_op jit(solution)/shard_map/gradients/pallas_call | solution.py:176
  78.4 4.1 %collective-permute-start.14 = (bf16[2,384,128]{2,1,0:T(8,128)(2,1)S(1)}, bf16[2,384,128]{2,1,0:T(8,128)(2,1)S(1)}, u32[]{:S(2)}, u32[]{:S(2)}) collective-permute-start(bf16[2,384,128]{2,1,0:T(8,128)(2,1)S(1)} %gradients.3.refs_10_.refs_6_), channel_id=1, source_target_pairs={{0,16},{2,18},{4,20},{6,22},{8,24},{10,26},{12,28},{14,30},{16,0},... | collective-permute-start | bytes 589832 | tf_op jit(solution)/shard_map/ppermute | solution.py:161
  82.5 4.0 %finish.2 = (bf16[3,256,128]{2,1,0:T(8,128)(2,1)S(1)}, bf16[3,256,128]{2,1,0:T(8,128)(2,1)S(1)}, bf16[3,256,128]{2,1,0:T(8,128)(2,1)S(1)}, bf16[3,256,128]{2,1,0:T(8,128)(2,1)S(1)}) custom-call(s32[3]{0:T(128)S(1)} %pad_add_fusion.place_ref, f32[4,3,256,128]{3,2,1,0:T(8,128)S(1)} %get-tuple-element.57.refs_5_.refs_0_, bf16[20,128,512]{2,1,0:T(8,128)(2,1)S(1)} %copy-done.2, ...), custom_call_target="tpu_custom_call" | custom-call | flops 19327352832 | tf_op jit(solution)/shard_map/finish/pallas_call | solution.py:176
  86.5 3.7 %collective-permute-start.17 = (bf16[3,256,128]{2,1,0:T(8,128)(2,1)S(1)}, bf16[3,256,128]{2,1,0:T(8,128)(2,1)S(1)}, u32[]{:S(2)}, u32[]{:S(2)}) collective-permute-start(bf16[3,256,128]{2,1,0:T(8,128)(2,1)S(1)} %get-tuple-element.68), channel_id=1, source_target_pairs={{0,4},{2,6},{4,0},{6,2},{8,12},{10,14},{12,8},{14,10},{16,20},{18,... | collective-permute-start | bytes 589832 | tf_op jit(solution)/shard_map/ppermute | solution.py:161
  90.2 1.5 %collective-permute-start.19 = (bf16[3,256,128]{2,1,0:T(8,128)(2,1)S(1)}, bf16[3,256,128]{2,1,0:T(8,128)(2,1)S(1)}, u32[]{:S(2)}, u32[]{:S(2)}) collective-permute-start(bf16[3,256,128]{2,1,0:T(8,128)(2,1)S(1)} %get-tuple-element.70), channel_id=1, source_target_pairs={{0,12},{2,14},{4,8},{6,10},{8,4},{10,6},{12,0},{14,2},{16,28},{18,... | collective-permute-start | bytes 589832 | tf_op jit(solution)/shard_map/ppermute | solution.py:161
  91.8 6.9 %attend.3 = (f32[4,2,256,128]{3,2,1,0:T(8,128)S(1)}, f32[2,16,128]{2,1,0:T(8,128)S(1)}) custom-call(s32[3]{0:T(128)S(1)} %pad_add_fusion.place_ref, s32[20]{0:T(128)S(1)} %copy-done.9, s32[3]{0:T(128)S(1)} %copy-done.10, bf16[2,784,128]{2,1,0:T(8,128)(2,1)S(1)} %get-tuple-element.59.refs_0_.refs_6_, ...), custom_call_target="tpu_custom_call" | custom-call | flops 34359738368 | tf_op jit(solution)/shard_map/attend/pallas_call | solution.py:176
  98.8 0.2 collective-permute-start.15
  99.0 0.7 collective-permute-start.16
  99.7 4.3 %collective-permute-done.19.refs_13_.refs_3_ = bf16[3,256,128]{2,1,0:T(8,128)(2,1)S(1)} collective-permute-done((bf16[3,256,128]{2,1,0:T(8,128)(2,1)S(1)}, bf16[3,256,128]{2,1,0:T(8,128)(2,1)S(1)}, u32[]{:S(2)}, u32[]{:S(2)}) %collective-permute-start.19) | collective-permute-done | bytes 196640 | tf_op jit(solution)/shard_map/ppermute | solution.py:161
  104.0 2.8 %finish.3 = (bf16[2,256,128]{2,1,0:T(8,128)(2,1)S(1)}, bf16[2,256,128]{2,1,0:T(8,128)(2,1)S(1)}, bf16[2,256,128]{2,1,0:T(8,128)(2,1)S(1)}, bf16[2,256,128]{2,1,0:T(8,128)(2,1)S(1)}) custom-call(s32[3]{0:T(128)S(1)} %pad_add_fusion.place_ref, f32[4,2,256,128]{3,2,1,0:T(8,128)S(1)} %get-tuple-element.65.refs_0_, bf16[20,128,512]{2,1,0:T(8,128)(2,1)S(1)} %copy-done.2, ...), custom_call_target="tpu_custom_call" | custom-call | flops 12884901888 | tf_op jit(solution)/shard_map/finish/pallas_call | solution.py:176
  106.9 0.1 collective-permute-start.21
  107.0 3.4 %collective-permute-start.22 = (bf16[2,256,128]{2,1,0:T(8,128)(2,1)S(1)}, bf16[2,256,128]{2,1,0:T(8,128)(2,1)S(1)}, u32[]{:S(2)}, u32[]{:S(2)}) collective-permute-start(bf16[2,256,128]{2,1,0:T(8,128)(2,1)S(1)} %get-tuple-element.74), channel_id=1, source_target_pairs={{0,12},{2,14},{4,8},{6,10},{8,4},{10,6},{12,0},{14,2},{16,28},{18,... | collective-permute-start | bytes 393224 | tf_op jit(solution)/shard_map/ppermute | solution.py:161
  110.4 1.4 %put_in_place.2.refs_4_ = bf16[20,256,128]{2,1,0:T(8,128)(2,1)} custom-call(s32[3]{0:T(128)S(1)} %pad_add_fusion.place_ref, bf16[3,256,128]{2,1,0:T(8,128)(2,1)S(1)} %get-tuple-element.64.refs_7_.refs_10_.refs_0_, bf16[3,256,128]{2,1,0:T(8,128)(2,1)S(1)} %collective-permute-done.17.refs_11_.refs_1_, ...), custom_call_target="tpu_custom_call" | custom-call | tf_op jit(solution)/shard_map/put_in_place/pallas_call | solution.py:599
  111.8 0.5 collective-permute-done.20.refs_1_
  112.4 0.9 collective-permute-done.21.refs_2_
  113.3 3.0 %collective-permute-done.22.refs_3_ = bf16[2,256,128]{2,1,0:T(8,128)(2,1)S(1)} collective-permute-done((bf16[2,256,128]{2,1,0:T(8,128)(2,1)S(1)}, bf16[2,256,128]{2,1,0:T(8,128)(2,1)S(1)}, u32[]{:S(2)}, u32[]{:S(2)}) %collective-permute-start.22) | collective-permute-done | bytes 131104 | tf_op jit(solution)/shard_map/ppermute | solution.py:161
  116.3 1.4 %put_in_place.3 = bf16[20,256,128]{2,1,0:T(8,128)(2,1)} custom-call(s32[3]{0:T(128)S(1)} %pad_add_fusion.place_ref, bf16[2,256,128]{2,1,0:T(8,128)(2,1)S(1)} %get-tuple-element.71.refs_0_, bf16[2,256,128]{2,1,0:T(8,128)(2,1)S(1)} %collective-permute-done.20.refs_1_, ...), custom_call_target="tpu_custom_call", output_to_operand_aliasing={{}: (5, {})} | custom-call | tf_op jit(solution)/shard_map/put_in_place/pallas_call | solution.py:599
  (40 shorter events, 0.4 us)
Async XLA Ops:
  0.0 1.8 %copy-start = (bf16[256,20,128]{2,0,1:T(8,128)(2,1)S(1)}, bf16[256,20,128]{2,0,1:T(8,128)(2,1)}, u32[]{:S(2)}) copy-start(bf16[256,20,128]{2,0,1:T(8,128)(2,1)} %param.12) | copy-start | bytes 3932164
  0.0 6.8 %copy-start.1 = (bf16[256,20,128]{2,0,1:T(8,128)(2,1)S(1)}, bf16[256,20,128]{2,0,1:T(8,128)(2,1)}, u32[]{:S(2)}) copy-start(bf16[256,20,128]{2,0,1:T(8,128)(2,1)} %param.11) | copy-start | bytes 3932164
  0.0 6.8 %copy-start.7 = (f32[20,128]{1,0:T(8,128)S(1)}, f32[20,128]{1,0:T(8,128)}, u32[]{:S(2)}) copy-start(f32[20,128]{1,0:T(8,128)} %refs_2_.5) | copy-start | bytes 30724
  0.0 6.8 %copy-start.8 = (f32[20,128]{1,0:T(8,128)S(1)}, f32[20,128]{1,0:T(8,128)}, u32[]{:S(2)}) copy-start(f32[20,128]{1,0:T(8,128)} %refs_3_.3) | copy-start | bytes 30724
  0.0 6.8 %copy-start.5 = (f32[20,256]{1,0:T(8,128)S(1)}, f32[20,256]{1,0:T(8,128)}, u32[]{:S(2)}) copy-start(f32[20,256]{1,0:T(8,128)} %refs_4_.3) | copy-start | bytes 61444
  0.0 6.8 %copy-start.6 = (f32[20,256]{1,0:T(8,128)S(1)}, f32[20,256]{1,0:T(8,128)}, u32[]{:S(2)}) copy-start(f32[20,256]{1,0:T(8,128)} %refs_5_.3) | copy-start | bytes 61444
  2.2 4.6 %collective-permute-start = (f32[2,256]{1,0:T(2,128)S(1)}, f32[2,256]{1,0:T(2,128)S(1)}, u32[]{:S(2)}, u32[]{:S(2)}) collective-permute-start(f32[2,256]{1,0:T(2,128)S(1)} %pad_maximum_fusion.refs_0_), channel_id=1, source_target_pairs={{0,1},{1,0},{2,3},{3,2},{4,5},{5,4},{6,7},{7,6},{8,9},{9,8},{10,11... | collective-permute-start | bytes 6152 | tf_op jit(solution)/shard_map/ppermute | solution.py:670
  6.8 1.3 %copy-start.3 = (bf16[256,20,128]{2,0,1:T(8,128)(2,1)S(1)}, bf16[256,20,128]{2,0,1:T(8,128)(2,1)}, u32[]{:S(2)}) copy-start(bf16[256,20,128]{2,0,1:T(8,128)(2,1)} %param.13) | copy-start | bytes 3932164
  9.5 15.9 %collective-permute-start.1 = (bf16[3,800,128]{2,1,0:T(8,128)(2,1)S(1)}, bf16[3,800,128]{2,1,0:T(8,128)(2,1)S(1)}, u32[]{:S(2)}, u32[]{:S(2)}) collective-permute-start(bf16[3,800,128]{2,1,0:T(8,128)(2,1)S(1)} %get-tuple-element.44), channel_id=1, source_target_pairs={{0,4},{2,6},{4,0},{6,2},{8,12},{10,14},{12,8},{14,10},{16,20},{18,... | collective-permute-start | bytes 1843208 | tf_op jit(solution)/shard_map/ppermute | solution.py:161
  11.6 16.8 %collective-permute-start.3 = (bf16[3,800,128]{2,1,0:T(8,128)(2,1)S(1)}, bf16[3,800,128]{2,1,0:T(8,128)(2,1)S(1)}, u32[]{:S(2)}, u32[]{:S(2)}) collective-permute-start(bf16[3,800,128]{2,1,0:T(8,128)(2,1)S(1)} %get-tuple-element.47), channel_id=1, source_target_pairs={{0,8},{2,10},{4,12},{6,14},{8,0},{10,2},{12,4},{14,6},{16,24},{18,... | collective-permute-start | bytes 1843208 | tf_op jit(solution)/shard_map/ppermute | solution.py:161
  13.1 25.6 %collective-permute-start.5 = (bf16[3,800,128]{2,1,0:T(8,128)(2,1)S(1)}, bf16[3,800,128]{2,1,0:T(8,128)(2,1)S(1)}, u32[]{:S(2)}, u32[]{:S(2)}) collective-permute-start(bf16[3,800,128]{2,1,0:T(8,128)(2,1)S(1)} %get-tuple-element.50), channel_id=1, source_target_pairs={{0,12},{2,14},{4,8},{6,10},{8,4},{10,6},{12,0},{14,2},{16,28},{18,... | collective-permute-start | bytes 1843208 | tf_op jit(solution)/shard_map/ppermute | solution.py:161
  38.8 3.0 %collective-permute-start.7 = (bf16[3,3,544,128]{3,2,1,0:T(8,128)(2,1)S(1)}, bf16[3,3,544,128]{3,2,1,0:T(8,128)(2,1)S(1)}, u32[]{:S(2)}, u32[]{:S(2)}) collective-permute-start(bf16[3,3,544,128]{3,2,1,0:T(8,128)(2,1)S(1)} %stack.31), channel_id=1, source_target_pairs={{0,2},{2,0},{4,6},{6,4},{8,10},{10,8},{12,14},{14,12},{16,18},{18,... | collective-permute-start | bytes 3760136 | tf_op jit(solution)/shard_map/ppermute | solution.py:161
  41.8 6.5 %copy-start.2 = (bf16[20,128,512]{2,1,0:T(8,128)(2,1)S(1)}, bf16[20,128,512]{2,1,0:T(8,128)(2,1)}, u32[]{:S(2)}) copy-start(bf16[20,128,512]{2,1,0:T(8,128)(2,1)} %refs_1_.3) | copy-start | bytes 7864324
  41.8 6.5 %copy-start.4 = (bf16[20,256,128]{2,1,0:T(8,128)(2,1)S(1)}, bf16[20,256,128]{2,1,0:T(8,128)(2,1)}, u32[]{:S(2)}) copy-start(bf16[20,256,128]{2,1,0:T(8,128)(2,1)} %refs_2_.7) | copy-start | bytes 3932164
  41.9 3.5 %collective-permute-start.8 = (bf16[1,3,544,128]{3,2,1,0:T(8,128)(2,1)S(1)}, bf16[1,3,544,128]{3,2,1,0:T(8,128)(2,1)S(1)}, u32[]{:S(2)}, u32[]{:S(2)}) collective-permute-start(bf16[1,3,544,128]{3,2,1,0:T(8,128)(2,1)S(1)} %stack.32), channel_id=1, source_target_pairs={{0,2},{2,0},{4,6},{6,4},{8,10},{10,8},{12,14},{14,12},{16,18},{18,... | collective-permute-start | bytes 1253384 | tf_op jit(solution)/shard_map/ppermute | solution.py:161
  42.1 16.0 %collective-permute-start.4 = (bf16[2,784,128]{2,1,0:T(8,128)(2,1)S(1)}, bf16[2,784,128]{2,1,0:T(8,128)(2,1)S(1)}, u32[]{:S(2)}, u32[]{:S(2)}) collective-permute-start(bf16[2,784,128]{2,1,0:T(8,128)(2,1)S(1)} %get-tuple-element.48), channel_id=1, source_target_pairs={{0,8},{2,10},{4,12},{6,14},{8,0},{10,2},{12,4},{14,6},{16,24},{18,... | collective-permute-start | bytes 1204232 | tf_op jit(solution)/shard_map/ppermute | solution.py:161
  43.8 15.0 %collective-permute-start.2 = (bf16[2,784,128]{2,1,0:T(8,128)(2,1)S(1)}, bf16[2,784,128]{2,1,0:T(8,128)(2,1)S(1)}, u32[]{:S(2)}, u32[]{:S(2)}) collective-permute-start(bf16[2,784,128]{2,1,0:T(8,128)(2,1)S(1)} %get-tuple-element.45), channel_id=1, source_target_pairs={{0,4},{2,6},{4,0},{6,2},{8,12},{10,14},{12,8},{14,10},{16,20},{18,... | collective-permute-start | bytes 1204232 | tf_op jit(solution)/shard_map/ppermute | solution.py:161
  45.9 12.8 %copy-start.9 = (s32[20]{0:T(128)S(1)}, s32[20]{0:T(128)}, u32[]{:S(2)}) copy-start(s32[20]{0:T(128)} %window_ref.3) | copy-start | bytes 244
  45.9 12.8 %copy-start.10 = (s32[3]{0:T(128)S(1)}, s32[3]{0:T(128)}, u32[]{:S(2)}) copy-start(s32[3]{0:T(128)} %edge_ref.3) | copy-start | bytes 40
  46.0 12.8 %collective-permute-start.10 = (bf16[3,16,128]{2,1,0:T(8,128)(2,1)S(1)}, bf16[3,16,128]{2,1,0:T(8,128)(2,1)S(1)}, u32[]{:S(2)}, u32[]{:S(2)}) collective-permute-start(bf16[3,16,128]{2,1,0:T(8,128)(2,1)S(1)} %lone_rows.1), channel_id=1, source_target_pairs={{16,0},{18,2},{20,4},{22,6},{24,8},{26,10},{28,12},{30,14},{17,1},... | collective-permute-start | bytes 36872 | tf_op jit(solution)/shard_map/ppermute | solution.py:161
  47.3 24.0 %collective-permute-start.6 = (bf16[2,784,128]{2,1,0:T(8,128)(2,1)S(1)}, bf16[2,784,128]{2,1,0:T(8,128)(2,1)S(1)}, u32[]{:S(2)}, u32[]{:S(2)}) collective-permute-start(bf16[2,784,128]{2,1,0:T(8,128)(2,1)S(1)} %get-tuple-element.51), channel_id=1, source_target_pairs={{0,12},{2,14},{4,8},{6,10},{8,4},{10,6},{12,0},{14,2},{16,28},{18,... | collective-permute-start | bytes 1204232 | tf_op jit(solution)/shard_map/ppermute | solution.py:161
  54.5 16.7 %collective-permute-start.9 = (bf16[3,384,128]{2,1,0:T(8,128)(2,1)S(1)}, bf16[3,384,128]{2,1,0:T(8,128)(2,1)S(1)}, u32[]{:S(2)}, u32[]{:S(2)}) collective-permute-start(bf16[3,384,128]{2,1,0:T(8,128)(2,1)S(1)} %gradients.2.refs_7_), channel_id=1, source_target_pairs={{0,16},{2,18},{4,20},{6,22},{8,24},{10,26},{12,28},{14,30},{16,0},... | collective-permute-start | bytes 884744 | tf_op jit(solution)/shard_map/ppermute | solution.py:161
  71.4 2.8 %collective-permute-start.11 = (bf16[4,2,528,128]{3,2,1,0:T(8,128)(2,1)S(1)}, bf16[4,2,528,128]{3,2,1,0:T(8,128)(2,1)S(1)}, u32[]{:S(2)}, u32[]{:S(2)}) collective-permute-start(bf16[4,2,528,128]{3,2,1,0:T(8,128)(2,1)S(1)} %stack.33), channel_id=1, source_target_pairs={{0,2},{2,0},{4,6},{6,4},{8,10},{10,8},{12,14},{14,12},{16,18},{18,... | collective-permute-start | bytes 3244040 | tf_op jit(solution)/shard_map/ppermute | solution.py:161
  71.4 11.1 %collective-permute-start.12 = (bf16[3,384,128]{2,1,0:T(8,128)(2,1)S(1)}, bf16[3,384,128]{2,1,0:T(8,128)(2,1)S(1)}, u32[]{:S(2)}, u32[]{:S(2)}) collective-permute-start(bf16[3,384,128]{2,1,0:T(8,128)(2,1)S(1)} %add_convert_fusion.refs_3_), channel_id=1, source_target_pairs={{0,2},{2,0},{4,6},{6,4},{8,10},{10,8},{12,14},{14,12},{16,18},{18,... | collective-permute-start | bytes 884744 | tf_op jit(solution)/shard_map/ppermute | solution.py:161
  71.9 10.6 %collective-permute-start.13 = (f32[3,16,128]{2,1,0:T(8,128)S(1)}, f32[3,16,128]{2,1,0:T(8,128)S(1)}, u32[]{:S(2)}, u32[]{:S(2)}) collective-permute-start(f32[3,16,128]{2,1,0:T(8,128)S(1)} %get-tuple-element.63), channel_id=1, source_target_pairs={{2,16},{6,20},{10,24},{14,28},{3,17},{7,21},{11,25},{15,29}} | collective-permute-start | bytes 73736 | tf_op jit(solution)/shard_map/ppermute | solution.py:161
  78.4 20.3 %collective-permute-start.14 = (bf16[2,384,128]{2,1,0:T(8,128)(2,1)S(1)}, bf16[2,384,128]{2,1,0:T(8,128)(2,1)S(1)}, u32[]{:S(2)}, u32[]{:S(2)}) collective-permute-start(bf16[2,384,128]{2,1,0:T(8,128)(2,1)S(1)} %gradients.3.refs_10_.refs_6_), channel_id=1, source_target_pairs={{0,16},{2,18},{4,20},{6,22},{8,24},{10,26},{12,28},{14,30},{16,0},... | collective-permute-start | bytes 589832 | tf_op jit(solution)/shard_map/ppermute | solution.py:161
  86.5 13.2 %collective-permute-start.17 = (bf16[3,256,128]{2,1,0:T(8,128)(2,1)S(1)}, bf16[3,256,128]{2,1,0:T(8,128)(2,1)S(1)}, u32[]{:S(2)}, u32[]{:S(2)}) collective-permute-start(bf16[3,256,128]{2,1,0:T(8,128)(2,1)S(1)} %get-tuple-element.68), channel_id=1, source_target_pairs={{0,4},{2,6},{4,0},{6,2},{8,12},{10,14},{12,8},{14,10},{16,20},{18,... | collective-permute-start | bytes 589832 | tf_op jit(solution)/shard_map/ppermute | solution.py:161
  90.2 9.5 %collective-permute-start.18 = (bf16[3,256,128]{2,1,0:T(8,128)(2,1)S(1)}, bf16[3,256,128]{2,1,0:T(8,128)(2,1)S(1)}, u32[]{:S(2)}, u32[]{:S(2)}) collective-permute-start(bf16[3,256,128]{2,1,0:T(8,128)(2,1)S(1)} %get-tuple-element.69), channel_id=1, source_target_pairs={{0,8},{2,10},{4,12},{6,14},{8,0},{10,2},{12,4},{14,6},{16,24},{18,... | collective-permute-start | bytes 589832 | tf_op jit(solution)/shard_map/ppermute | solution.py:161
  90.2 13.8 %collective-permute-start.19 = (bf16[3,256,128]{2,1,0:T(8,128)(2,1)S(1)}, bf16[3,256,128]{2,1,0:T(8,128)(2,1)S(1)}, u32[]{:S(2)}, u32[]{:S(2)}) collective-permute-start(bf16[3,256,128]{2,1,0:T(8,128)(2,1)S(1)} %get-tuple-element.70), channel_id=1, source_target_pairs={{0,12},{2,14},{4,8},{6,10},{8,4},{10,6},{12,0},{14,2},{16,28},{18,... | collective-permute-start | bytes 589832 | tf_op jit(solution)/shard_map/ppermute | solution.py:161
  98.8 5.2 %collective-permute-start.15 = (bf16[2,384,128]{2,1,0:T(8,128)(2,1)S(1)}, bf16[2,384,128]{2,1,0:T(8,128)(2,1)S(1)}, u32[]{:S(2)}, u32[]{:S(2)}) collective-permute-start(bf16[2,384,128]{2,1,0:T(8,128)(2,1)S(1)} %add_convert_fusion.1.refs_3_), channel_id=1, source_target_pairs={{0,2},{2,0},{4,6},{6,4},{8,10},{10,8},{12,14},{14,12},{16,18},{18,... | collective-permute-start | bytes 589832 | tf_op jit(solution)/shard_map/ppermute | solution.py:161
  99.0 0.7 collective-permute-start.16
  106.8 5.6 %collective-permute-start.20 = (bf16[2,256,128]{2,1,0:T(8,128)(2,1)S(1)}, bf16[2,256,128]{2,1,0:T(8,128)(2,1)S(1)}, u32[]{:S(2)}, u32[]{:S(2)}) collective-permute-start(bf16[2,256,128]{2,1,0:T(8,128)(2,1)S(1)} %get-tuple-element.72), channel_id=1, source_target_pairs={{0,4},{2,6},{4,0},{6,2},{8,12},{10,14},{12,8},{14,10},{16,20},{18,... | collective-permute-start | bytes 393224 | tf_op jit(solution)/shard_map/ppermute | solution.py:161
  106.9 6.4 %collective-permute-start.21 = (bf16[2,256,128]{2,1,0:T(8,128)(2,1)S(1)}, bf16[2,256,128]{2,1,0:T(8,128)(2,1)S(1)}, u32[]{:S(2)}, u32[]{:S(2)}) collective-permute-start(bf16[2,256,128]{2,1,0:T(8,128)(2,1)S(1)} %get-tuple-element.73), channel_id=1, source_target_pairs={{0,8},{2,10},{4,12},{6,14},{8,0},{10,2},{12,4},{14,6},{16,24},{18,... | collective-permute-start | bytes 393224 | tf_op jit(solution)/shard_map/ppermute | solution.py:161
  107.0 9.3 %collective-permute-start.22 = (bf16[2,256,128]{2,1,0:T(8,128)(2,1)S(1)}, bf16[2,256,128]{2,1,0:T(8,128)(2,1)S(1)}, u32[]{:S(2)}, u32[]{:S(2)}) collective-permute-start(bf16[2,256,128]{2,1,0:T(8,128)(2,1)S(1)} %get-tuple-element.74), channel_id=1, source_target_pairs={{0,12},{2,14},{4,8},{6,10},{8,4},{10,6},{12,0},{14,2},{16,28},{18,... | collective-permute-start | bytes 393224 | tf_op jit(solution)/shard_map/ppermute | solution.py:161

commit v2 on v0

--- a/solution.py
+++ b/solution.py
@@ -185,6 +185,10 @@
     )(*scalars, *arrays, *after)
 
 
+def head_at(place_ref, share, chip, i):
+    return place_ref[3 + chip * share + i]
+
+
 def pack_kernel(peers, first, count, width_all, fold, with_lone, place_ref, *refs):
     squares_ref, more_ref, q_gain_ref, k_gain_ref, rate_in_ref, rate_out_ref = refs[:6]
     q_ref, k_ref, v_ref = refs[6:9]
@@ -197,26 +201,26 @@
     k_scale_ref[...] = jnp.transpose(jnp.broadcast_to(scales[1:2], (dim, rows)))
     aux_ref[...] = jnp.zeros_like(aux_ref)
 
-    def normed(ref, c, scale_ref, gain_ref, head, some):
-        gain = gain_ref[pl.ds(c * share + head, 1), :]
-        scaled = ref[c, head, 0:some].astype(jnp.float32) * scale_ref[0:some] * gain
+    def normed(ref, scale_ref, gain_ref, head, some):
+        gain = gain_ref[pl.ds(head, 1), :]
+        scaled = ref[head, 0:some].astype(jnp.float32) * scale_ref[0:some] * gain
         return scaled.astype(jnp.bfloat16)
 
     def one_head(step, carry):
         for p in range(peers):
             c = place_ref[0] ^ p
-            head = first + step
-            outs[p][step, 0:rows, :] = normed(q_ref, c, q_scale_ref, q_gain_ref, head, rows)
+            head = head_at(place_ref, share, c, first + step)
+            outs[p][step, 0:rows, :] = normed(q_ref, q_scale_ref, q_gain_ref, head, rows)
             outs[p][step, rows : 2 * rows, :] = normed(
-                k_ref, c, k_scale_ref, k_gain_ref, head, rows
+                k_ref, k_scale_ref, k_gain_ref, head, rows
             )
             for i in range(0, rows, 128):
                 outs[p][step, 2 * rows + i : 2 * rows + i + 128, :] = jnp.transpose(
-                    v_ref[c, head, i : i + 128, :]
+                    v_ref[head, i : i + 128, :]
                 )
             at = 0
             for rate_ref in (rate_in_ref, rate_out_ref):
-                rate = rate_ref[pl.ds(c * share + head, 1), :]
+                rate = rate_ref[pl.ds(head, 1), :]
                 high = rate.astype(jnp.bfloat16).astype(jnp.float32)
                 for part in (high, rate - high):
                     for i in range(0, rows, 128):
@@ -224,10 +228,10 @@
                         at += 1
             if with_lone:
                 for i in range(-(-share // count)):
-                    head = jnp.minimum(step + i * count, share - 1)
-                    q0 = normed(q_ref, c, q_scale_ref, q_gain_ref, head, 16)
-                    k0 = normed(k_ref, c, k_scale_ref, k_gain_ref, head, 16)
-                    for at, array in enumerate((q0, k0, v_ref[c, head, 0:16])):
+                    head = head_at(place_ref, share, c, jnp.minimum(step + i * count, share - 1))
+                    q0 = normed(q_ref, q_scale_ref, q_gain_ref, head, 16)
+                    k0 = normed(k_ref, k_scale_ref, k_gain_ref, head, 16)
+                    for at, array in enumerate((q0, k0, v_ref[head, 0:16])):
                         at += aux_ref.shape[0] // 2 + 3 * i
                         aux_ref[at : at + 1, :] = array.astype(jnp.float32)[0:1]
             some = outs[p].shape[1] - 3 * rows
@@ -240,7 +244,6 @@
 def pack(place, sums, q, k, v, gains, rates, peers, aux_rows, first, count, width_all, fold):
     heads, rows, dim = q.shape
     out_shape = (count, 3 * rows + aux_rows // (2 if first else 1), dim)
-    q, k, v = [x.reshape(peers, heads // peers, rows, dim) for x in (q, k, v)]
     return in_vmem(
         functools.partial(pack_kernel, peers, first, count, width_all, fold, not first),
         "pack",
@@ -308,7 +311,7 @@
     own = pl.multiple_of(place_ref[1] * part, part)
 
     def one_head(step, carry):
-        head = place_ref[0] * share + first + step
+        head = head_at(place_ref, share, place_ref[0], first + step)
         in_half = jnp.concatenate(
             [
                 jnp.transpose(in_ref[head, :, pl.ds(at, part)].astype(jnp.float32))
@@ -378,7 +381,7 @@
     vt_scr[dim:, :] = jnp.ones((vt_scr.shape[0] - dim, vt_scr.shape[1]), vt_scr.dtype)
 
     def one_head(step, carry):
-        window = window_ref[chip * share + first + step]
+        window = window_ref[head_at(place_ref, share, chip, first + step)]
         for p, own, keys, values in key_value_blocks(peers, rows, step, refs):
             at = pl.multiple_of(((chip ^ p) * 2 + (core if own else 1 - core)) * rows, rows)
             k_scr[pl.ds(at, rows), :] = keys[...]
@@ -517,7 +520,7 @@
     part = hid // 2
 
     def one_head(step, carry):
-        head = chip * share + first + step
+        head = head_at(place_ref, share, chip, first + step)
         for summed, lane in ((own_ref, core), (other_ref, 1 - core)):
             at = pl.multiple_of(lane * part, part)
             grad_in_scr[pl.ds(at, part), :] = summed[step, 0:part, :].astype(jnp.float32)
@@ -569,13 +572,15 @@
 def place_kernel(peers, chunks, share, place_ref, *refs):
     pieces, out_ref, sems = refs[:-2], refs[-2], refs[-1]
     copies = []
-    for first, heads in chunks:
+    for n, (first, heads) in enumerate(chunks):
         for p in range(peers):
-            at = (place_ref[0] ^ p) * share + first
-            i = len(copies)
-            copies.append(
-                pltpu.make_async_copy(pieces[i], out_ref.at[pl.ds(at, heads)], sems.at[i])
-            )
+            for i in range(heads):
+                head = head_at(place_ref, share, place_ref[0] ^ p, first + i)
+                copies.append(
+                    pltpu.make_async_copy(
+                        pieces[n * peers + p].at[i], out_ref.at[head], sems.at[len(copies)]
+                    )
+                )
     for copy in copies:
         copy.start()
     for copy in copies:
@@ -590,7 +595,7 @@
         in_specs=[pl.BlockSpec(memory_space=pltpu.SMEM)]
         + [pl.BlockSpec(memory_space=pltpu.VMEM)] * len(pieces),
         out_specs=pl.BlockSpec(memory_space=pl.ANY),
-        scratch_shapes=[pltpu.SemaphoreType.DMA((len(pieces),))],
+        scratch_shapes=[pltpu.SemaphoreType.DMA((peers * share,))],
         compiler_params=pltpu.CompilerParams(vmem_limit_bytes=VMEM_BYTES),
         name="put_in_place",
     )(place, *pieces)
@@ -630,7 +635,14 @@
     half = own_index // half_peers
     chip = own_index % half_peers // 2
     core = own_index % 2
-    place = jnp.stack([chip, core, half]).astype(jnp.int32)
+    number = jnp.arange(heads, dtype=jnp.int32)
+    order = half_window * heads + number
+    rank = jnp.sum((order[None, :] > order[:, None]).astype(jnp.int32), axis=1)
+    turn, seat = rank // peers, rank % peers
+    taker = jnp.where(turn % 2 == 0, seat, peers - 1 - seat)
+    slot = taker * share + jnp.where(turn % 2 == 0, 0, chunks[0][1]) + turn // 2
+    table = jnp.sum(jnp.where(slot[:, None] == number[None, :], number[:, None], 0), axis=0)
+    place = jnp.concatenate([jnp.stack([chip, core, half]).astype(jnp.int32), table])
 
     def dealt(sent):
         pairs = [

time: 116 us -> 115 us (level)
  Pallas kernels: 46.8 us -> 42.1 us
  waiting for transfers between devices: 37.7 us -> 40 us
    pallas_call x11, Pallas kernels: 45.2 us -> 40.3 us  [in_vmem(): pl.pallas_call(kernel, out_shape=out_shape, in_specs=specs, out_specs=jax...]
    ppermute x21, waiting for transfers between devices: 36.2 us -> 38.8 us  [exchanged(): return lax.ppermute(x, 'tok', pairs)]
  transfers between devices with their start and end apart: 22 -> 22, of which waited for: 11 -> 11; matrix products, arithmetic and copies ran while one was open for 0% -> 0% of each run, Pallas kernels for 35% -> 31%
where the time goes in v2:
time: 115 us; the launch traced here: 114 us
  Pallas kernels  42.1 us (37%)
  waiting for transfers between devices  40 us (35%)
  starting transfers between devices  27 us (23%)
  other arithmetic  2.67 us (2%)
  local copies, waits for them, and re-layouts  1.35 us (1%)
    pallas_call x11, Pallas kernels, in_vmem(): pl.pallas_call(kernel, out_shape=out_shape, in_specs=specs, out_specs=jax...  40.3 us
    ppermute x21, waiting for transfers between devices, exchanged(): return lax.ppermute(x, 'tok', pairs)  38.8 us
    ppermute x21, starting transfers between devices, exchanged(): return lax.ppermute(x, 'tok', pairs)  24 us
    ppermute x1, starting transfers between devices, regrouped_body(): sums = (squares, lax.ppermute(squares, 'head', [(0, 1), (1, 0)]))  3.02 us
  transfers between devices with their start and end apart: 22, of which 11 were waited for; matrix products, arithmetic and copies ran while one was open for 0% of the time, Pallas kernels for 31%

profile of v2, /device:TPU:0, one launch (start us, length us, event | category | flops | bytes accessed | tf_op | source)
XLA Modules:
  0.0 113.5 jit_solution(10141487771736711464)
XLA Ops:
  0.0 1.8 %multiply_reduce_fusion.1 = f32[256]{0:T(256)S(1)} fusion(bf16[256,20,128]{2,0,1:T(8,128)(2,1)} %param.11), kind=kLoop, calls=%fused_computation.1 | loop fusion | flops 1965824 | bytes 1311744 | tf_op jit(solution)/shard_map/reduce_sum | solution.py:665
  1.8 0.3 multiply_reduce_fusion
  2.2 3.0 %collective-permute-start = (f32[2,256]{1,0:T(2,128)S(1)}, f32[2,256]{1,0:T(2,128)S(1)}, u32[]{:S(2)}, u32[]{:S(2)}) collective-permute-start(f32[2,256]{1,0:T(2,128)S(1)} %pad_maximum_fusion.refs_0_), channel_id=1, source_target_pairs={{0,1},{1,0},{2,3},{3,2},{4,5},{5,4},{6,7},{7,6},{8,9},{9,8},{10,11... | collective-permute-start | bytes 6152 | tf_op jit(solution)/shard_map/ppermute | solution.py:668
  5.2 0.2 convert_reduce_fusion
  5.4 0.1 select_reduce_fusion
  5.5 0.1 pad_add_fusion.place_ref
  5.6 1.2 %collective-permute-done.refs_1_ = f32[2,256]{1,0:T(2,128)S(1)} collective-permute-done((f32[2,256]{1,0:T(2,128)S(1)}, f32[2,256]{1,0:T(2,128)S(1)}, u32[]{:S(2)}, u32[]{:S(2)}) %collective-permute-start) | collective-permute-done | bytes 2080 | tf_op jit(solution)/shard_map/ppermute | solution.py:668
  6.8 1.3 %copy-done.3 = bf16[256,20,128]{2,0,1:T(8,128)(2,1)S(1)} copy-done((bf16[256,20,128]{2,0,1:T(8,128)(2,1)S(1)}, bf16[256,20,128]{2,0,1:T(8,128)(2,1)}, u32[]{:S(2)}) %copy-start.3) | copy-done | bytes 1310744
  8.1 1.3 %pack.2 = (bf16[3,800,128]{2,1,0:T(8,128)(2,1)S(1)}, bf16[3,800,128]{2,1,0:T(8,128)(2,1)S(1)}, bf16[3,800,128]{2,1,0:T(8,128)(2,1)S(1)}, bf16[3,800,128]{2,1,0:T(8,128)(2,1)S(1)}) custom-call(s32[23]{0:T(128)S(1)} %pad_add_fusion.place_ref, f32[2,256]{1,0:T(2,128)S(1)} %pad_maximum_fusion.refs_0_, f32[2,256]{1,0:T(2,128)S(1)} %collective-permute-done.refs_1_, ...), custom_call_target="tpu_custom_call" | custom-call | tf_op jit(solution)/shard_map/pack/pallas_call | solution.py:176
  9.5 2.1 %collective-permute-start.1 = (bf16[3,800,128]{2,1,0:T(8,128)(2,1)S(1)}, bf16[3,800,128]{2,1,0:T(8,128)(2,1)S(1)}, u32[]{:S(2)}, u32[]{:S(2)}) collective-permute-start(bf16[3,800,128]{2,1,0:T(8,128)(2,1)S(1)} %get-tuple-element.40), channel_id=1, source_target_pairs={{0,4},{2,6},{4,0},{6,2},{8,12},{10,14},{12,8},{14,10},{16,20},{18,... | collective-permute-start | bytes 1843208 | tf_op jit(solution)/shard_map/ppermute | solution.py:161
  11.6 1.6 %collective-permute-start.2 = (bf16[3,800,128]{2,1,0:T(8,128)(2,1)S(1)}, bf16[3,800,128]{2,1,0:T(8,128)(2,1)S(1)}, u32[]{:S(2)}, u32[]{:S(2)}) collective-permute-start(bf16[3,800,128]{2,1,0:T(8,128)(2,1)S(1)} %get-tuple-element.41), channel_id=1, source_target_pairs={{0,8},{2,10},{4,12},{6,14},{8,0},{10,2},{12,4},{14,6},{16,24},{18,... | collective-permute-start | bytes 1843208 | tf_op jit(solution)/shard_map/ppermute | solution.py:161
  13.2 1.1 pack.3
  14.2 11.1 %collective-permute-done.1.refs_1_.refs_7_ = bf16[3,800,128]{2,1,0:T(8,128)(2,1)S(1)} collective-permute-done((bf16[3,800,128]{2,1,0:T(8,128)(2,1)S(1)}, bf16[3,800,128]{2,1,0:T(8,128)(2,1)S(1)}, u32[]{:S(2)}, u32[]{:S(2)}) %collective-permute-start.1) | collective-permute-done | bytes 614432 | tf_op jit(solution)/shard_map/ppermute | solution.py:161
  25.4 3.0 %collective-permute-done.2.refs_2_.refs_8_ = bf16[3,800,128]{2,1,0:T(8,128)(2,1)S(1)} collective-permute-done((bf16[3,800,128]{2,1,0:T(8,128)(2,1)S(1)}, bf16[3,800,128]{2,1,0:T(8,128)(2,1)S(1)}, u32[]{:S(2)}, u32[]{:S(2)}) %collective-permute-start.2) | collective-permute-done | bytes 614432 | tf_op jit(solution)/shard_map/ppermute | solution.py:161
  28.4 10.3 %collective-permute-done.3.refs_3_.refs_9_ = bf16[3,800,128]{2,1,0:T(8,128)(2,1)S(1)} collective-permute-done((bf16[3,800,128]{2,1,0:T(8,128)(2,1)S(1)}, bf16[3,800,128]{2,1,0:T(8,128)(2,1)S(1)}, u32[]{:S(2)}, u32[]{:S(2)}) %collective-permute-start.3) | collective-permute-done | bytes 614432 | tf_op jit(solution)/shard_map/ppermute | solution.py:161
  38.7 0.1 stack.26.own_ref
  38.9 3.5 %collective-permute-done.4.other_ref.refs_4_ = bf16[4,3,544,128]{3,2,1,0:T(8,128)(2,1)S(1)} collective-permute-done((bf16[4,3,544,128]{3,2,1,0:T(8,128)(2,1)S(1)}, bf16[4,3,544,128]{3,2,1,0:T(8,128)(2,1)S(1)}, u32[]{:S(2)}, u32[]{:S(2)}) %collective-permute-start.4) | collective-permute-done | bytes 1671200 | tf_op jit(solution)/shard_map/ppermute | solution.py:161
  42.5 0.6 lone_rows.1
  43.0 1.3 %collective-permute-start.5 = (bf16[3,16,128]{2,1,0:T(8,128)(2,1)S(1)}, bf16[3,16,128]{2,1,0:T(8,128)(2,1)S(1)}, u32[]{:S(2)}, u32[]{:S(2)}) collective-permute-start(bf16[3,16,128]{2,1,0:T(8,128)(2,1)S(1)} %lone_rows.1), channel_id=1, source_target_pairs={{16,0},{18,2},{20,4},{22,6},{24,8},{26,10},{28,12},{30,14},{17,1},... | collective-permute-start | bytes 36872 | tf_op jit(solution)/shard_map/ppermute | solution.py:161
  44.3 1.8 %collective-permute-start.10 = (bf16[2,784,128]{2,1,0:T(8,128)(2,1)S(1)}, bf16[2,784,128]{2,1,0:T(8,128)(2,1)S(1)}, u32[]{:S(2)}, u32[]{:S(2)}) collective-permute-start(bf16[2,784,128]{2,1,0:T(8,128)(2,1)S(1)} %get-tuple-element.56), channel_id=1, source_target_pairs={{0,8},{2,10},{4,12},{6,14},{8,0},{10,2},{12,4},{14,6},{16,24},{18,... | collective-permute-start | bytes 1204232 | tf_op jit(solution)/shard_map/ppermute | solution.py:161
  46.1 1.4 %collective-permute-start.11 = (bf16[2,784,128]{2,1,0:T(8,128)(2,1)S(1)}, bf16[2,784,128]{2,1,0:T(8,128)(2,1)S(1)}, u32[]{:S(2)}, u32[]{:S(2)}) collective-permute-start(bf16[2,784,128]{2,1,0:T(8,128)(2,1)S(1)} %get-tuple-element.57), channel_id=1, source_target_pairs={{0,12},{2,14},{4,8},{6,10},{8,4},{10,6},{12,0},{14,2},{16,28},{18,... | collective-permute-start | bytes 1204232 | tf_op jit(solution)/shard_map/ppermute | solution.py:161
  47.5 0.4 collective-permute-start.9
  47.9 6.1 %gradients.2.refs_6_ = bf16[3,384,128]{2,1,0:T(8,128)(2,1)S(1)} custom-call(s32[23]{0:T(128)S(1)} %pad_add_fusion.place_ref, bf16[20,128,512]{2,1,0:T(8,128)(2,1)S(1)} %copy-done.2, bf16[20,256,128]{2,1,0:T(8,128)(2,1)S(1)} %copy-done.4, bf16[3,800,128]{2,1,0:T(8,128)(2,1)S(1)} %get-tuple-element.47.refs_0_.refs_6_, ...), custom_call_target="tpu_custom_call" | custom-call | tf_op jit(solution)/shard_map/gradients/pallas_call | solution.py:176
  54.0 3.6 %collective-permute-start.6 = (bf16[3,384,128]{2,1,0:T(8,128)(2,1)S(1)}, bf16[3,384,128]{2,1,0:T(8,128)(2,1)S(1)}, u32[]{:S(2)}, u32[]{:S(2)}) collective-permute-start(bf16[3,384,128]{2,1,0:T(8,128)(2,1)S(1)} %gradients.2.refs_6_), channel_id=1, source_target_pairs={{0,16},{2,18},{4,20},{6,22},{8,24},{10,26},{12,28},{14,30},{16,0},... | collective-permute-start | bytes 884744 | tf_op jit(solution)/shard_map/ppermute | solution.py:161
  57.6 12.7 %attend.2 = (f32[4,3,256,128]{3,2,1,0:T(8,128)S(1)}, f32[3,16,128]{2,1,0:T(8,128)S(1)}) custom-call(s32[23]{0:T(128)S(1)} %pad_add_fusion.place_ref, s32[20]{0:T(128)S(1)} %copy-done.9, s32[3]{0:T(128)S(1)} %copy-done.10, bf16[3,800,128]{2,1,0:T(8,128)(2,1)S(1)} %get-tuple-element.47.refs_0_.refs_6_, ...), custom_call_target="tpu_custom_call" | custom-call | flops 51539607552 | tf_op jit(solution)/shard_map/attend/pallas_call | solution.py:176
  70.3 0.1 add_convert_fusion.refs_3_
  70.4 1.6 %collective-permute-done.11.refs_3_.refs_9_ = bf16[2,784,128]{2,1,0:T(8,128)(2,1)S(1)} collective-permute-done((bf16[2,784,128]{2,1,0:T(8,128)(2,1)S(1)}, bf16[2,784,128]{2,1,0:T(8,128)(2,1)S(1)}, u32[]{:S(2)}, u32[]{:S(2)}) %collective-permute-start.11) | collective-permute-done | bytes 401440 | tf_op jit(solution)/shard_map/ppermute | solution.py:161
  72.2 0.5 collective-permute-start.7
  72.7 0.7 collective-permute-start.8
  73.3 1.5 %collective-permute-done.12.refs_4_ = bf16[4,2,528,128]{3,2,1,0:T(8,128)(2,1)S(1)} collective-permute-done((bf16[4,2,528,128]{3,2,1,0:T(8,128)(2,1)S(1)}, bf16[4,2,528,128]{3,2,1,0:T(8,128)(2,1)S(1)}, u32[]{:S(2)}, u32[]{:S(2)}) %collective-permute-start.12) | collective-permute-done | bytes 1081376 | tf_op jit(solution)/shard_map/ppermute | solution.py:161
  74.9 4.2 %gradients.3.refs_10_.refs_6_ = bf16[2,384,128]{2,1,0:T(8,128)(2,1)S(1)} custom-call(s32[23]{0:T(128)S(1)} %pad_add_fusion.place_ref, bf16[20,128,512]{2,1,0:T(8,128)(2,1)S(1)} %copy-done.2, bf16[20,256,128]{2,1,0:T(8,128)(2,1)S(1)} %copy-done.4, bf16[2,784,128]{2,1,0:T(8,128)(2,1)S(1)} %get-tuple-element.58.refs_0_.refs_6_, ...), custom_call_target="tpu_custom_call" | custom-call | tf_op jit(solution)/shard_map/gradients/pallas_call | solution.py:176
  79.1 1.5 %collective-permute-start.16 = (bf16[2,384,128]{2,1,0:T(8,128)(2,1)S(1)}, bf16[2,384,128]{2,1,0:T(8,128)(2,1)S(1)}, u32[]{:S(2)}, u32[]{:S(2)}) collective-permute-start(bf16[2,384,128]{2,1,0:T(8,128)(2,1)S(1)} %gradients.3.refs_10_.refs_6_), channel_id=1, source_target_pairs={{0,16},{2,18},{4,20},{6,22},{8,24},{10,26},{12,28},{14,30},{16,0},... | collective-permute-start | bytes 589832 | tf_op jit(solution)/shard_map/ppermute | solution.py:161
  80.6 4.0 %finish.2 = (bf16[3,256,128]{2,1,0:T(8,128)(2,1)S(1)}, bf16[3,256,128]{2,1,0:T(8,128)(2,1)S(1)}, bf16[3,256,128]{2,1,0:T(8,128)(2,1)S(1)}, bf16[3,256,128]{2,1,0:T(8,128)(2,1)S(1)}) custom-call(s32[23]{0:T(128)S(1)} %pad_add_fusion.place_ref, f32[4,3,256,128]{3,2,1,0:T(8,128)S(1)} %get-tuple-element.51.refs_5_.refs_0_, bf16[20,128,512]{2,1,0:T(8,128)(2,1)S(1)} %copy-done.2, ...), custom_call_target="tpu_custom_call" | custom-call | flops 19327352832 | tf_op jit(solution)/shard_map/finish/pallas_call | solution.py:176
  84.6 1.6 %collective-permute-start.13 = (bf16[3,256,128]{2,1,0:T(8,128)(2,1)S(1)}, bf16[3,256,128]{2,1,0:T(8,128)(2,1)S(1)}, u32[]{:S(2)}, u32[]{:S(2)}) collective-permute-start(bf16[3,256,128]{2,1,0:T(8,128)(2,1)S(1)} %get-tuple-element.63), channel_id=1, source_target_pairs={{0,4},{2,6},{4,0},{6,2},{8,12},{10,14},{12,8},{14,10},{16,20},{18,... | collective-permute-start | bytes 589832 | tf_op jit(solution)/shard_map/ppermute | solution.py:161
  86.2 2.1 %collective-permute-start.14 = (bf16[3,256,128]{2,1,0:T(8,128)(2,1)S(1)}, bf16[3,256,128]{2,1,0:T(8,128)(2,1)S(1)}, u32[]{:S(2)}, u32[]{:S(2)}) collective-permute-start(bf16[3,256,128]{2,1,0:T(8,128)(2,1)S(1)} %get-tuple-element.64), channel_id=1, source_target_pairs={{0,8},{2,10},{4,12},{6,14},{8,0},{10,2},{12,4},{14,6},{16,24},{18,... | collective-permute-start | bytes 589832 | tf_op jit(solution)/shard_map/ppermute | solution.py:161
  88.3 1.0 collective-permute-start.15
  89.3 7.4 %attend.3 = (f32[4,2,256,128]{3,2,1,0:T(8,128)S(1)}, f32[2,16,128]{2,1,0:T(8,128)S(1)}) custom-call(s32[23]{0:T(128)S(1)} %pad_add_fusion.place_ref, s32[20]{0:T(128)S(1)} %copy-done.9, s32[3]{0:T(128)S(1)} %copy-done.10, bf16[2,784,128]{2,1,0:T(8,128)(2,1)S(1)} %get-tuple-element.58.refs_0_.refs_6_, ...), custom_call_target="tpu_custom_call" | custom-call | flops 34359738368 | tf_op jit(solution)/shard_map/attend/pallas_call | solution.py:176
  96.7 0.2 collective-permute-start.17
  96.9 0.7 collective-permute-start.18
  97.6 1.8 %collective-permute-done.15.refs_13_.refs_3_ = bf16[3,256,128]{2,1,0:T(8,128)(2,1)S(1)} collective-permute-done((bf16[3,256,128]{2,1,0:T(8,128)(2,1)S(1)}, bf16[3,256,128]{2,1,0:T(8,128)(2,1)S(1)}, u32[]{:S(2)}, u32[]{:S(2)}) %collective-permute-start.15) | collective-permute-done | bytes 196640 | tf_op jit(solution)/shard_map/ppermute | solution.py:161
  99.3 2.8 %finish.3 = (bf16[2,256,128]{2,1,0:T(8,128)(2,1)S(1)}, bf16[2,256,128]{2,1,0:T(8,128)(2,1)S(1)}, bf16[2,256,128]{2,1,0:T(8,128)(2,1)S(1)}, bf16[2,256,128]{2,1,0:T(8,128)(2,1)S(1)}) custom-call(s32[23]{0:T(128)S(1)} %pad_add_fusion.place_ref, f32[4,2,256,128]{3,2,1,0:T(8,128)S(1)} %get-tuple-element.66.refs_0_, bf16[20,128,512]{2,1,0:T(8,128)(2,1)S(1)} %copy-done.2, ...), custom_call_target="tpu_custom_call" | custom-call | flops 12884901888 | tf_op jit(solution)/shard_map/finish/pallas_call | solution.py:176
  102.2 1.9 %collective-permute-start.19 = (bf16[2,256,128]{2,1,0:T(8,128)(2,1)S(1)}, bf16[2,256,128]{2,1,0:T(8,128)(2,1)S(1)}, u32[]{:S(2)}, u32[]{:S(2)}) collective-permute-start(bf16[2,256,128]{2,1,0:T(8,128)(2,1)S(1)} %get-tuple-element.70), channel_id=1, source_target_pairs={{0,4},{2,6},{4,0},{6,2},{8,12},{10,14},{12,8},{14,10},{16,20},{18,... | collective-permute-start | bytes 393224 | tf_op jit(solution)/shard_map/ppermute | solution.py:161
  104.0 0.3 collective-permute-start.20
  104.3 1.4 %collective-permute-start.21 = (bf16[2,256,128]{2,1,0:T(8,128)(2,1)S(1)}, bf16[2,256,128]{2,1,0:T(8,128)(2,1)S(1)}, u32[]{:S(2)}, u32[]{:S(2)}) collective-permute-start(bf16[2,256,128]{2,1,0:T(8,128)(2,1)S(1)} %get-tuple-element.72), channel_id=1, source_target_pairs={{0,12},{2,14},{4,8},{6,10},{8,4},{10,6},{12,0},{14,2},{16,28},{18,... | collective-permute-start | bytes 393224 | tf_op jit(solution)/shard_map/ppermute | solution.py:161
  105.7 2.2 %collective-permute-done.19.refs_5_ = bf16[2,256,128]{2,1,0:T(8,128)(2,1)S(1)} collective-permute-done((bf16[2,256,128]{2,1,0:T(8,128)(2,1)S(1)}, bf16[2,256,128]{2,1,0:T(8,128)(2,1)S(1)}, u32[]{:S(2)}, u32[]{:S(2)}) %collective-permute-start.19) | collective-permute-done | bytes 131104 | tf_op jit(solution)/shard_map/ppermute | solution.py:161
  107.9 2.4 %collective-permute-done.20.refs_6_ = bf16[2,256,128]{2,1,0:T(8,128)(2,1)S(1)} collective-permute-done((bf16[2,256,128]{2,1,0:T(8,128)(2,1)S(1)}, bf16[2,256,128]{2,1,0:T(8,128)(2,1)S(1)}, u32[]{:S(2)}, u32[]{:S(2)}) %collective-permute-start.20) | collective-permute-done | bytes 131104 | tf_op jit(solution)/shard_map/ppermute | solution.py:161
  110.3 1.3 %collective-permute-done.21.refs_7_ = bf16[2,256,128]{2,1,0:T(8,128)(2,1)S(1)} collective-permute-done((bf16[2,256,128]{2,1,0:T(8,128)(2,1)S(1)}, bf16[2,256,128]{2,1,0:T(8,128)(2,1)S(1)}, u32[]{:S(2)}, u32[]{:S(2)}) %collective-permute-start.21) | collective-permute-done | bytes 131104 | tf_op jit(solution)/shard_map/ppermute | solution.py:161
  111.6 1.8 %put_in_place.1 = bf16[20,256,128]{2,1,0:T(8,128)(2,1)} custom-call(s32[23]{0:T(128)S(1)} %pad_add_fusion.place_ref, bf16[3,256,128]{2,1,0:T(8,128)(2,1)S(1)} %get-tuple-element.62.refs_7_.refs_10_.refs_0_, bf16[3,256,128]{2,1,0:T(8,128)(2,1)S(1)} %collective-permute-done.13.refs_11_.refs_1_, ...), custom_call_target="tpu_custom_call" | custom-call | tf_op jit(solution)/shard_map/put_in_place/pallas_call | solution.py:592
  (40 shorter events, 0.4 us)
Async XLA Ops:
  0.0 1.8 %copy-start = (bf16[256,20,128]{2,0,1:T(8,128)(2,1)S(1)}, bf16[256,20,128]{2,0,1:T(8,128)(2,1)}, u32[]{:S(2)}) copy-start(bf16[256,20,128]{2,0,1:T(8,128)(2,1)} %param.12) | copy-start | bytes 3932164
  0.0 6.8 %copy-start.1 = (bf16[256,20,128]{2,0,1:T(8,128)(2,1)S(1)}, bf16[256,20,128]{2,0,1:T(8,128)(2,1)}, u32[]{:S(2)}) copy-start(bf16[256,20,128]{2,0,1:T(8,128)(2,1)} %param.11) | copy-start | bytes 3932164
  0.0 5.2 %copy-start.9 = (s32[20]{0:T(128)S(1)}, s32[20]{0:T(128)}, u32[]{:S(2)}) copy-start(s32[20]{0:T(128)} %window_ref.3) | copy-start | bytes 244
  0.0 6.8 %copy-start.7 = (f32[20,128]{1,0:T(8,128)S(1)}, f32[20,128]{1,0:T(8,128)}, u32[]{:S(2)}) copy-start(f32[20,128]{1,0:T(8,128)} %refs_2_.5) | copy-start | bytes 30724
  0.0 6.8 %copy-start.8 = (f32[20,128]{1,0:T(8,128)S(1)}, f32[20,128]{1,0:T(8,128)}, u32[]{:S(2)}) copy-start(f32[20,128]{1,0:T(8,128)} %refs_3_.3) | copy-start | bytes 30724
  0.0 6.8 %copy-start.5 = (f32[20,256]{1,0:T(8,128)S(1)}, f32[20,256]{1,0:T(8,128)}, u32[]{:S(2)}) copy-start(f32[20,256]{1,0:T(8,128)} %refs_4_.3) | copy-start | bytes 61444
  0.0 6.8 %copy-start.6 = (f32[20,256]{1,0:T(8,128)S(1)}, f32[20,256]{1,0:T(8,128)}, u32[]{:S(2)}) copy-start(f32[20,256]{1,0:T(8,128)} %refs_5_.3) | copy-start | bytes 61444
  2.2 4.6 %collective-permute-start = (f32[2,256]{1,0:T(2,128)S(1)}, f32[2,256]{1,0:T(2,128)S(1)}, u32[]{:S(2)}, u32[]{:S(2)}) collective-permute-start(f32[2,256]{1,0:T(2,128)S(1)} %pad_maximum_fusion.refs_0_), channel_id=1, source_target_pairs={{0,1},{1,0},{2,3},{3,2},{4,5},{5,4},{6,7},{7,6},{8,9},{9,8},{10,11... | collective-permute-start | bytes 6152 | tf_op jit(solution)/shard_map/ppermute | solution.py:668
  6.8 1.3 %copy-start.3 = (bf16[256,20,128]{2,0,1:T(8,128)(2,1)S(1)}, bf16[256,20,128]{2,0,1:T(8,128)(2,1)}, u32[]{:S(2)}) copy-start(bf16[256,20,128]{2,0,1:T(8,128)(2,1)} %param.13) | copy-start | bytes 3932164
  9.5 15.9 %collective-permute-start.1 = (bf16[3,800,128]{2,1,0:T(8,128)(2,1)S(1)}, bf16[3,800,128]{2,1,0:T(8,128)(2,1)S(1)}, u32[]{:S(2)}, u32[]{:S(2)}) collective-permute-start(bf16[3,800,128]{2,1,0:T(8,128)(2,1)S(1)} %get-tuple-element.40), channel_id=1, source_target_pairs={{0,4},{2,6},{4,0},{6,2},{8,12},{10,14},{12,8},{14,10},{16,20},{18,... | collective-permute-start | bytes 1843208 | tf_op jit(solution)/shard_map/ppermute | solution.py:161
  11.6 16.8 %collective-permute-start.2 = (bf16[3,800,128]{2,1,0:T(8,128)(2,1)S(1)}, bf16[3,800,128]{2,1,0:T(8,128)(2,1)S(1)}, u32[]{:S(2)}, u32[]{:S(2)}) collective-permute-start(bf16[3,800,128]{2,1,0:T(8,128)(2,1)S(1)} %get-tuple-element.41), channel_id=1, source_target_pairs={{0,8},{2,10},{4,12},{6,14},{8,0},{10,2},{12,4},{14,6},{16,24},{18,... | collective-permute-start | bytes 1843208 | tf_op jit(solution)/shard_map/ppermute | solution.py:161
  13.2 25.5 %collective-permute-start.3 = (bf16[3,800,128]{2,1,0:T(8,128)(2,1)S(1)}, bf16[3,800,128]{2,1,0:T(8,128)(2,1)S(1)}, u32[]{:S(2)}, u32[]{:S(2)}) collective-permute-start(bf16[3,800,128]{2,1,0:T(8,128)(2,1)S(1)} %get-tuple-element.42), channel_id=1, source_target_pairs={{0,12},{2,14},{4,8},{6,10},{8,4},{10,6},{12,0},{14,2},{16,28},{18,... | collective-permute-start | bytes 1843208 | tf_op jit(solution)/shard_map/ppermute | solution.py:161
  38.7 9.2 %copy-start.4 = (bf16[20,256,128]{2,1,0:T(8,128)(2,1)S(1)}, bf16[20,256,128]{2,1,0:T(8,128)(2,1)}, u32[]{:S(2)}) copy-start(bf16[20,256,128]{2,1,0:T(8,128)(2,1)} %refs_2_.7) | copy-start | bytes 3932164
  38.8 9.1 %copy-start.2 = (bf16[20,128,512]{2,1,0:T(8,128)(2,1)S(1)}, bf16[20,128,512]{2,1,0:T(8,128)(2,1)}, u32[]{:S(2)}) copy-start(bf16[20,128,512]{2,1,0:T(8,128)(2,1)} %refs_1_.3) | copy-start | bytes 7864324
  38.8 3.6 %collective-permute-start.4 = (bf16[4,3,544,128]{3,2,1,0:T(8,128)(2,1)S(1)}, bf16[4,3,544,128]{3,2,1,0:T(8,128)(2,1)S(1)}, u32[]{:S(2)}, u32[]{:S(2)}) collective-permute-start(bf16[4,3,544,128]{3,2,1,0:T(8,128)(2,1)S(1)} %stack.26.own_ref), channel_id=1, source_target_pairs={{0,2},{2,0},{4,6},{6,4},{8,10},{10,8},{12,14},{14,12},{16,18},{18,... | collective-permute-start | bytes 5013512 | tf_op jit(solution)/shard_map/ppermute | solution.py:161
  43.0 14.6 %copy-start.10 = (s32[3]{0:T(128)S(1)}, s32[3]{0:T(128)}, u32[]{:S(2)}) copy-start(s32[3]{0:T(128)} %edge_ref.3) | copy-start | bytes 40
  43.0 14.6 %collective-permute-start.5 = (bf16[3,16,128]{2,1,0:T(8,128)(2,1)S(1)}, bf16[3,16,128]{2,1,0:T(8,128)(2,1)S(1)}, u32[]{:S(2)}, u32[]{:S(2)}) collective-permute-start(bf16[3,16,128]{2,1,0:T(8,128)(2,1)S(1)} %lone_rows.1), channel_id=1, source_target_pairs={{16,0},{18,2},{20,4},{22,6},{24,8},{26,10},{28,12},{30,14},{17,1},... | collective-permute-start | bytes 36872 | tf_op jit(solution)/shard_map/ppermute | solution.py:161
  44.3 26.1 %collective-permute-start.10 = (bf16[2,784,128]{2,1,0:T(8,128)(2,1)S(1)}, bf16[2,784,128]{2,1,0:T(8,128)(2,1)S(1)}, u32[]{:S(2)}, u32[]{:S(2)}) collective-permute-start(bf16[2,784,128]{2,1,0:T(8,128)(2,1)S(1)} %get-tuple-element.56), channel_id=1, source_target_pairs={{0,8},{2,10},{4,12},{6,14},{8,0},{10,2},{12,4},{14,6},{16,24},{18,... | collective-permute-start | bytes 1204232 | tf_op jit(solution)/shard_map/ppermute | solution.py:161
  46.1 25.9 %collective-permute-start.11 = (bf16[2,784,128]{2,1,0:T(8,128)(2,1)S(1)}, bf16[2,784,128]{2,1,0:T(8,128)(2,1)S(1)}, u32[]{:S(2)}, u32[]{:S(2)}) collective-permute-start(bf16[2,784,128]{2,1,0:T(8,128)(2,1)S(1)} %get-tuple-element.57), channel_id=1, source_target_pairs={{0,12},{2,14},{4,8},{6,10},{8,4},{10,6},{12,0},{14,2},{16,28},{18,... | collective-permute-start | bytes 1204232 | tf_op jit(solution)/shard_map/ppermute | solution.py:161
  47.5 24.5 %collective-permute-start.9 = (bf16[2,784,128]{2,1,0:T(8,128)(2,1)S(1)}, bf16[2,784,128]{2,1,0:T(8,128)(2,1)S(1)}, u32[]{:S(2)}, u32[]{:S(2)}) collective-permute-start(bf16[2,784,128]{2,1,0:T(8,128)(2,1)S(1)} %get-tuple-element.55), channel_id=1, source_target_pairs={{0,4},{2,6},{4,0},{6,2},{8,12},{10,14},{12,8},{14,10},{16,20},{18,... | collective-permute-start | bytes 1204232 | tf_op jit(solution)/shard_map/ppermute | solution.py:161
  54.0 16.3 %collective-permute-start.6 = (bf16[3,384,128]{2,1,0:T(8,128)(2,1)S(1)}, bf16[3,384,128]{2,1,0:T(8,128)(2,1)S(1)}, u32[]{:S(2)}, u32[]{:S(2)}) collective-permute-start(bf16[3,384,128]{2,1,0:T(8,128)(2,1)S(1)} %gradients.2.refs_6_), channel_id=1, source_target_pairs={{0,16},{2,18},{4,20},{6,22},{8,24},{10,26},{12,28},{14,30},{16,0},... | collective-permute-start | bytes 884744 | tf_op jit(solution)/shard_map/ppermute | solution.py:161
  72.1 2.8 %collective-permute-start.12 = (bf16[4,2,528,128]{3,2,1,0:T(8,128)(2,1)S(1)}, bf16[4,2,528,128]{3,2,1,0:T(8,128)(2,1)S(1)}, u32[]{:S(2)}, u32[]{:S(2)}) collective-permute-start(bf16[4,2,528,128]{3,2,1,0:T(8,128)(2,1)S(1)} %stack.27), channel_id=1, source_target_pairs={{0,2},{2,0},{4,6},{6,4},{8,10},{10,8},{12,14},{14,12},{16,18},{18,... | collective-permute-start | bytes 3244040 | tf_op jit(solution)/shard_map/ppermute | solution.py:161
  72.2 8.4 %collective-permute-start.7 = (bf16[3,384,128]{2,1,0:T(8,128)(2,1)S(1)}, bf16[3,384,128]{2,1,0:T(8,128)(2,1)S(1)}, u32[]{:S(2)}, u32[]{:S(2)}) collective-permute-start(bf16[3,384,128]{2,1,0:T(8,128)(2,1)S(1)} %add_convert_fusion.refs_3_), channel_id=1, source_target_pairs={{0,2},{2,0},{4,6},{6,4},{8,10},{10,8},{12,14},{14,12},{16,18},{18,... | collective-permute-start | bytes 884744 | tf_op jit(solution)/shard_map/ppermute | solution.py:161
  72.7 7.9 %collective-permute-start.8 = (f32[3,16,128]{2,1,0:T(8,128)S(1)}, f32[3,16,128]{2,1,0:T(8,128)S(1)}, u32[]{:S(2)}, u32[]{:S(2)}) collective-permute-start(f32[3,16,128]{2,1,0:T(8,128)S(1)} %get-tuple-element.53), channel_id=1, source_target_pairs={{2,16},{6,20},{10,24},{14,28},{3,17},{7,21},{11,25},{15,29}} | collective-permute-start | bytes 73736 | tf_op jit(solution)/shard_map/ppermute | solution.py:161
  79.1 17.5 %collective-permute-start.16 = (bf16[2,384,128]{2,1,0:T(8,128)(2,1)S(1)}, bf16[2,384,128]{2,1,0:T(8,128)(2,1)S(1)}, u32[]{:S(2)}, u32[]{:S(2)}) collective-permute-start(bf16[2,384,128]{2,1,0:T(8,128)(2,1)S(1)} %gradients.3.refs_10_.refs_6_), channel_id=1, source_target_pairs={{0,16},{2,18},{4,20},{6,22},{8,24},{10,26},{12,28},{14,30},{16,0},... | collective-permute-start | bytes 589832 | tf_op jit(solution)/shard_map/ppermute | solution.py:161
  84.6 13.0 %collective-permute-start.13 = (bf16[3,256,128]{2,1,0:T(8,128)(2,1)S(1)}, bf16[3,256,128]{2,1,0:T(8,128)(2,1)S(1)}, u32[]{:S(2)}, u32[]{:S(2)}) collective-permute-start(bf16[3,256,128]{2,1,0:T(8,128)(2,1)S(1)} %get-tuple-element.63), channel_id=1, source_target_pairs={{0,4},{2,6},{4,0},{6,2},{8,12},{10,14},{12,8},{14,10},{16,20},{18,... | collective-permute-start | bytes 589832 | tf_op jit(solution)/shard_map/ppermute | solution.py:161
  86.2 11.4 %collective-permute-start.14 = (bf16[3,256,128]{2,1,0:T(8,128)(2,1)S(1)}, bf16[3,256,128]{2,1,0:T(8,128)(2,1)S(1)}, u32[]{:S(2)}, u32[]{:S(2)}) collective-permute-start(bf16[3,256,128]{2,1,0:T(8,128)(2,1)S(1)} %get-tuple-element.64), channel_id=1, source_target_pairs={{0,8},{2,10},{4,12},{6,14},{8,0},{10,2},{12,4},{14,6},{16,24},{18,... | collective-permute-start | bytes 589832 | tf_op jit(solution)/shard_map/ppermute | solution.py:161
  88.3 11.0 %collective-permute-start.15 = (bf16[3,256,128]{2,1,0:T(8,128)(2,1)S(1)}, bf16[3,256,128]{2,1,0:T(8,128)(2,1)S(1)}, u32[]{:S(2)}, u32[]{:S(2)}) collective-permute-start(bf16[3,256,128]{2,1,0:T(8,128)(2,1)S(1)} %get-tuple-element.65), channel_id=1, source_target_pairs={{0,12},{2,14},{4,8},{6,10},{8,4},{10,6},{12,0},{14,2},{16,28},{18,... | collective-permute-start | bytes 589832 | tf_op jit(solution)/shard_map/ppermute | solution.py:161
  96.7 2.6 %collective-permute-start.17 = (bf16[2,384,128]{2,1,0:T(8,128)(2,1)S(1)}, bf16[2,384,128]{2,1,0:T(8,128)(2,1)S(1)}, u32[]{:S(2)}, u32[]{:S(2)}) collective-permute-start(bf16[2,384,128]{2,1,0:T(8,128)(2,1)S(1)} %add_convert_fusion.1.refs_3_), channel_id=1, source_target_pairs={{0,2},{2,0},{4,6},{6,4},{8,10},{10,8},{12,14},{14,12},{16,18},{18,... | collective-permute-start | bytes 589832 | tf_op jit(solution)/shard_map/ppermute | solution.py:161
  96.9 0.7 collective-permute-start.18
  102.2 5.7 %collective-permute-start.19 = (bf16[2,256,128]{2,1,0:T(8,128)(2,1)S(1)}, bf16[2,256,128]{2,1,0:T(8,128)(2,1)S(1)}, u32[]{:S(2)}, u32[]{:S(2)}) collective-permute-start(bf16[2,256,128]{2,1,0:T(8,128)(2,1)S(1)} %get-tuple-element.70), channel_id=1, source_target_pairs={{0,4},{2,6},{4,0},{6,2},{8,12},{10,14},{12,8},{14,10},{16,20},{18,... | collective-permute-start | bytes 393224 | tf_op jit(solution)/shard_map/ppermute | solution.py:161
  104.0 6.2 %collective-permute-start.20 = (bf16[2,256,128]{2,1,0:T(8,128)(2,1)S(1)}, bf16[2,256,128]{2,1,0:T(8,128)(2,1)S(1)}, u32[]{:S(2)}, u32[]{:S(2)}) collective-permute-start(bf16[2,256,128]{2,1,0:T(8,128)(2,1)S(1)} %get-tuple-element.71), channel_id=1, source_target_pairs={{0,8},{2,10},{4,12},{6,14},{8,0},{10,2},{12,4},{14,6},{16,24},{18,... | collective-permute-start | bytes 393224 | tf_op jit(solution)/shard_map/ppermute | solution.py:161
  104.3 7.3 %collective-permute-start.21 = (bf16[2,256,128]{2,1,0:T(8,128)(2,1)S(1)}, bf16[2,256,128]{2,1,0:T(8,128)(2,1)S(1)}, u32[]{:S(2)}, u32[]{:S(2)}) collective-permute-start(bf16[2,256,128]{2,1,0:T(8,128)(2,1)S(1)} %get-tuple-element.72), channel_id=1, source_target_pairs={{0,12},{2,14},{4,8},{6,10},{8,4},{10,6},{12,0},{14,2},{16,28},{18,... | collective-permute-start | bytes 393224 | tf_op jit(solution)/shard_map/ppermute | solution.py:161

commit v3 on v2

--- a/solution.py
+++ b/solution.py
@@ -723,6 +723,8 @@
         grad = gradients(place, fast_in, fast_out, packets, share, rows, first, before)
         from_half = exchanged(grad, half_pairs)
         before = [grad]
+        if not ready and len(received) > 1:
+            before += received[1][1:2]
         if ready:
             outs = finished(ready, [grad])
             before.append(outs[0])

time: 115 us -> 115 us (level)
  waiting for transfers between devices: 40 us -> 37.8 us
  Pallas kernels: 42.1 us -> 43.5 us
  starting transfers between devices: 27 us -> 28.3 us
    ppermute x21, waiting for transfers between devices: 38.8 us -> 36.7 us  [exchanged(): return lax.ppermute(x, 'tok', pairs)]
    pallas_call x11, Pallas kernels: 40.3 us -> 41.7 us  [in_vmem(): pl.pallas_call(kernel, out_shape=out_shape, in_specs=specs, out_specs=jax...]
    ppermute x21, starting transfers between devices: 24 us -> 25.3 us  [exchanged(): return lax.ppermute(x, 'tok', pairs)]
  transfers between devices with their start and end apart: 22 -> 22, of which waited for: 11 -> 11; matrix products, arithmetic and copies ran while one was open for 0% -> 0% of each run, Pallas kernels for 31% -> 33%
where the time goes in v3:
time: 115 us; the launch traced here: 114 us
  Pallas kernels  43.5 us (38%)
  waiting for transfers between devices  37.8 us (33%)
  starting transfers between devices  28.3 us (25%)
  other arithmetic  2.67 us (2%)
  local copies, waits for them, and re-layouts  1.35 us (1%)
    pallas_call x11, Pallas kernels, in_vmem(): pl.pallas_call(kernel, out_shape=out_shape, in_specs=specs, out_specs=jax...  41.7 us
    ppermute x21, waiting for transfers between devices, exchanged(): return lax.ppermute(x, 'tok', pairs)  36.7 us
    ppermute x21, starting transfers between devices, exchanged(): return lax.ppermute(x, 'tok', pairs)  25.3 us
    ppermute x1, starting transfers between devices, regrouped_body(): sums = (squares, lax.ppermute(squares, 'head', [(0, 1), (1, 0)]))  3.02 us
  transfers between devices with their start and end apart: 22, of which 11 were waited for; matrix products, arithmetic and copies ran while one was open for 0% of the time, Pallas kernels for 33%

profile of v3, /device:TPU:0, one launch (start us, length us, event | category | flops | bytes accessed | tf_op | source)
XLA Modules:
  0.0 114.1 jit_solution(10544090007984910040)
XLA Ops:
  0.0 1.8 %multiply_reduce_fusion.1 = f32[256]{0:T(256)S(1)} fusion(bf16[256,20,128]{2,0,1:T(8,128)(2,1)} %param.11), kind=kLoop, calls=%fused_computation.1 | loop fusion | flops 1965824 | bytes 1311744 | tf_op jit(solution)/shard_map/reduce_sum | solution.py:665
  1.8 0.3 multiply_reduce_fusion
  2.2 3.0 %collective-permute-start = (f32[2,256]{1,0:T(2,128)S(1)}, f32[2,256]{1,0:T(2,128)S(1)}, u32[]{:S(2)}, u32[]{:S(2)}) collective-permute-start(f32[2,256]{1,0:T(2,128)S(1)} %pad_maximum_fusion.refs_0_), channel_id=1, source_target_pairs={{0,1},{1,0},{2,3},{3,2},{4,5},{5,4},{6,7},{7,6},{8,9},{9,8},{10,11... | collective-permute-start | bytes 6152 | tf_op jit(solution)/shard_map/ppermute | solution.py:668
  5.2 0.2 convert_reduce_fusion
  5.4 0.1 select_reduce_fusion
  5.5 0.1 pad_add_fusion.place_ref
  5.6 1.2 %collective-permute-done.refs_1_ = f32[2,256]{1,0:T(2,128)S(1)} collective-permute-done((f32[2,256]{1,0:T(2,128)S(1)}, f32[2,256]{1,0:T(2,128)S(1)}, u32[]{:S(2)}, u32[]{:S(2)}) %collective-permute-start) | collective-permute-done | bytes 2080 | tf_op jit(solution)/shard_map/ppermute | solution.py:668
  6.8 1.3 %copy-done.3 = bf16[256,20,128]{2,0,1:T(8,128)(2,1)S(1)} copy-done((bf16[256,20,128]{2,0,1:T(8,128)(2,1)S(1)}, bf16[256,20,128]{2,0,1:T(8,128)(2,1)}, u32[]{:S(2)}) %copy-start.3) | copy-done | bytes 1310744
  8.1 1.3 %pack.2 = (bf16[3,800,128]{2,1,0:T(8,128)(2,1)S(1)}, bf16[3,800,128]{2,1,0:T(8,128)(2,1)S(1)}, bf16[3,800,128]{2,1,0:T(8,128)(2,1)S(1)}, bf16[3,800,128]{2,1,0:T(8,128)(2,1)S(1)}) custom-call(s32[23]{0:T(128)S(1)} %pad_add_fusion.place_ref, f32[2,256]{1,0:T(2,128)S(1)} %pad_maximum_fusion.refs_0_, f32[2,256]{1,0:T(2,128)S(1)} %collective-permute-done.refs_1_, ...), custom_call_target="tpu_custom_call" | custom-call | tf_op jit(solution)/shard_map/pack/pallas_call | solution.py:176
  9.5 2.1 %collective-permute-start.1 = (bf16[3,800,128]{2,1,0:T(8,128)(2,1)S(1)}, bf16[3,800,128]{2,1,0:T(8,128)(2,1)S(1)}, u32[]{:S(2)}, u32[]{:S(2)}) collective-permute-start(bf16[3,800,128]{2,1,0:T(8,128)(2,1)S(1)} %get-tuple-element.40), channel_id=1, source_target_pairs={{0,4},{2,6},{4,0},{6,2},{8,12},{10,14},{12,8},{14,10},{16,20},{18,... | collective-permute-start | bytes 1843208 | tf_op jit(solution)/shard_map/ppermute | solution.py:161
  11.6 1.6 %collective-permute-start.2 = (bf16[3,800,128]{2,1,0:T(8,128)(2,1)S(1)}, bf16[3,800,128]{2,1,0:T(8,128)(2,1)S(1)}, u32[]{:S(2)}, u32[]{:S(2)}) collective-permute-start(bf16[3,800,128]{2,1,0:T(8,128)(2,1)S(1)} %get-tuple-element.41), channel_id=1, source_target_pairs={{0,8},{2,10},{4,12},{6,14},{8,0},{10,2},{12,4},{14,6},{16,24},{18,... | collective-permute-start | bytes 1843208 | tf_op jit(solution)/shard_map/ppermute | solution.py:161
  13.2 1.1 pack.3
  14.2 11.1 %collective-permute-done.1.refs_1_.refs_7_ = bf16[3,800,128]{2,1,0:T(8,128)(2,1)S(1)} collective-permute-done((bf16[3,800,128]{2,1,0:T(8,128)(2,1)S(1)}, bf16[3,800,128]{2,1,0:T(8,128)(2,1)S(1)}, u32[]{:S(2)}, u32[]{:S(2)}) %collective-permute-start.1) | collective-permute-done | bytes 614432 | tf_op jit(solution)/shard_map/ppermute | solution.py:161
  25.4 3.0 %collective-permute-done.2.refs_2_.refs_8_ = bf16[3,800,128]{2,1,0:T(8,128)(2,1)S(1)} collective-permute-done((bf16[3,800,128]{2,1,0:T(8,128)(2,1)S(1)}, bf16[3,800,128]{2,1,0:T(8,128)(2,1)S(1)}, u32[]{:S(2)}, u32[]{:S(2)}) %collective-permute-start.2) | collective-permute-done | bytes 614432 | tf_op jit(solution)/shard_map/ppermute | solution.py:161
  28.4 10.3 %collective-permute-done.3.refs_3_.refs_9_ = bf16[3,800,128]{2,1,0:T(8,128)(2,1)S(1)} collective-permute-done((bf16[3,800,128]{2,1,0:T(8,128)(2,1)S(1)}, bf16[3,800,128]{2,1,0:T(8,128)(2,1)S(1)}, u32[]{:S(2)}, u32[]{:S(2)}) %collective-permute-start.3) | collective-permute-done | bytes 614432 | tf_op jit(solution)/shard_map/ppermute | solution.py:161
  38.7 0.1 stack.26.own_ref
  38.8 0.1 collective-permute-start.4
  38.9 1.7 %collective-permute-start.6 = (bf16[2,784,128]{2,1,0:T(8,128)(2,1)S(1)}, bf16[2,784,128]{2,1,0:T(8,128)(2,1)S(1)}, u32[]{:S(2)}, u32[]{:S(2)}) collective-permute-start(bf16[2,784,128]{2,1,0:T(8,128)(2,1)S(1)} %get-tuple-element.51), channel_id=1, source_target_pairs={{0,4},{2,6},{4,0},{6,2},{8,12},{10,14},{12,8},{14,10},{16,20},{18,... | collective-permute-start | bytes 1204232 | tf_op jit(solution)/shard_map/ppermute | solution.py:161
  40.7 1.8 %collective-permute-done.4.other_ref.refs_4_ = bf16[4,3,544,128]{3,2,1,0:T(8,128)(2,1)S(1)} collective-permute-done((bf16[4,3,544,128]{3,2,1,0:T(8,128)(2,1)S(1)}, bf16[4,3,544,128]{3,2,1,0:T(8,128)(2,1)S(1)}, u32[]{:S(2)}, u32[]{:S(2)}) %collective-permute-start.4) | collective-permute-done | bytes 1671200 | tf_op jit(solution)/shard_map/ppermute | solution.py:161
  42.5 0.6 lone_rows.1
  43.0 1.3 %collective-permute-start.5 = (bf16[3,16,128]{2,1,0:T(8,128)(2,1)S(1)}, bf16[3,16,128]{2,1,0:T(8,128)(2,1)S(1)}, u32[]{:S(2)}, u32[]{:S(2)}) collective-permute-start(bf16[3,16,128]{2,1,0:T(8,128)(2,1)S(1)} %lone_rows.1), channel_id=1, source_target_pairs={{16,0},{18,2},{20,4},{22,6},{24,8},{26,10},{28,12},{30,14},{17,1},... | collective-permute-start | bytes 36872 | tf_op jit(solution)/shard_map/ppermute | solution.py:161
  44.3 1.8 %collective-permute-start.10 = (bf16[2,784,128]{2,1,0:T(8,128)(2,1)S(1)}, bf16[2,784,128]{2,1,0:T(8,128)(2,1)S(1)}, u32[]{:S(2)}, u32[]{:S(2)}) collective-permute-start(bf16[2,784,128]{2,1,0:T(8,128)(2,1)S(1)} %get-tuple-element.56), channel_id=1, source_target_pairs={{0,8},{2,10},{4,12},{6,14},{8,0},{10,2},{12,4},{14,6},{16,24},{18,... | collective-permute-start | bytes 1204232 | tf_op jit(solution)/shard_map/ppermute | solution.py:161
  46.1 1.4 %collective-permute-start.11 = (bf16[2,784,128]{2,1,0:T(8,128)(2,1)S(1)}, bf16[2,784,128]{2,1,0:T(8,128)(2,1)S(1)}, u32[]{:S(2)}, u32[]{:S(2)}) collective-permute-start(bf16[2,784,128]{2,1,0:T(8,128)(2,1)S(1)} %get-tuple-element.57), channel_id=1, source_target_pairs={{0,12},{2,14},{4,8},{6,10},{8,4},{10,6},{12,0},{14,2},{16,28},{18,... | collective-permute-start | bytes 1204232 | tf_op jit(solution)/shard_map/ppermute | solution.py:161
  47.5 6.1 %gradients.2.refs_6_ = bf16[3,384,128]{2,1,0:T(8,128)(2,1)S(1)} custom-call(s32[23]{0:T(128)S(1)} %pad_add_fusion.place_ref, bf16[20,128,512]{2,1,0:T(8,128)(2,1)S(1)} %copy-done.2, bf16[20,256,128]{2,1,0:T(8,128)(2,1)S(1)} %copy-done.4, bf16[3,800,128]{2,1,0:T(8,128)(2,1)S(1)} %get-tuple-element.47.refs_0_.refs_6_, ...), custom_call_target="tpu_custom_call" | custom-call | tf_op jit(solution)/shard_map/gradients/pallas_call | solution.py:176
  53.6 3.6 %collective-permute-start.7 = (bf16[3,384,128]{2,1,0:T(8,128)(2,1)S(1)}, bf16[3,384,128]{2,1,0:T(8,128)(2,1)S(1)}, u32[]{:S(2)}, u32[]{:S(2)}) collective-permute-start(bf16[3,384,128]{2,1,0:T(8,128)(2,1)S(1)} %gradients.2.refs_6_), channel_id=1, source_target_pairs={{0,16},{2,18},{4,20},{6,22},{8,24},{10,26},{12,28},{14,30},{16,0},... | collective-permute-start | bytes 884744 | tf_op jit(solution)/shard_map/ppermute | solution.py:161
  57.3 13.1 %attend.2 = (f32[4,3,256,128]{3,2,1,0:T(8,128)S(1)}, f32[3,16,128]{2,1,0:T(8,128)S(1)}) custom-call(s32[23]{0:T(128)S(1)} %pad_add_fusion.place_ref, s32[20]{0:T(128)S(1)} %copy-done.9, s32[3]{0:T(128)S(1)} %copy-done.10, bf16[3,800,128]{2,1,0:T(8,128)(2,1)S(1)} %get-tuple-element.47.refs_0_.refs_6_, ...), custom_call_target="tpu_custom_call" | custom-call | flops 51539607552 | tf_op jit(solution)/shard_map/attend/pallas_call | solution.py:176
  70.4 0.1 add_convert_fusion.refs_3_
  70.5 1.5 %collective-permute-done.11.refs_3_.refs_9_ = bf16[2,784,128]{2,1,0:T(8,128)(2,1)S(1)} collective-permute-done((bf16[2,784,128]{2,1,0:T(8,128)(2,1)S(1)}, bf16[2,784,128]{2,1,0:T(8,128)(2,1)S(1)}, u32[]{:S(2)}, u32[]{:S(2)}) %collective-permute-start.11) | collective-permute-done | bytes 401440 | tf_op jit(solution)/shard_map/ppermute | solution.py:161
  72.2 0.5 collective-permute-start.8
  72.7 0.7 collective-permute-start.9
  73.3 1.5 %collective-permute-done.12.refs_4_ = bf16[4,2,528,128]{3,2,1,0:T(8,128)(2,1)S(1)} collective-permute-done((bf16[4,2,528,128]{3,2,1,0:T(8,128)(2,1)S(1)}, bf16[4,2,528,128]{3,2,1,0:T(8,128)(2,1)S(1)}, u32[]{:S(2)}, u32[]{:S(2)}) %collective-permute-start.12) | collective-permute-done | bytes 1081376 | tf_op jit(solution)/shard_map/ppermute | solution.py:161
  74.9 4.3 %gradients.3.refs_10_.refs_6_ = bf16[2,384,128]{2,1,0:T(8,128)(2,1)S(1)} custom-call(s32[23]{0:T(128)S(1)} %pad_add_fusion.place_ref, bf16[20,128,512]{2,1,0:T(8,128)(2,1)S(1)} %copy-done.2, bf16[20,256,128]{2,1,0:T(8,128)(2,1)S(1)} %copy-done.4, bf16[2,784,128]{2,1,0:T(8,128)(2,1)S(1)} %get-tuple-element.58.refs_0_.refs_6_, ...), custom_call_target="tpu_custom_call" | custom-call | tf_op jit(solution)/shard_map/gradients/pallas_call | solution.py:176
  79.1 1.4 %collective-permute-start.16 = (bf16[2,384,128]{2,1,0:T(8,128)(2,1)S(1)}, bf16[2,384,128]{2,1,0:T(8,128)(2,1)S(1)}, u32[]{:S(2)}, u32[]{:S(2)}) collective-permute-start(bf16[2,384,128]{2,1,0:T(8,128)(2,1)S(1)} %gradients.3.refs_10_.refs_6_), channel_id=1, source_target_pairs={{0,16},{2,18},{4,20},{6,22},{8,24},{10,26},{12,28},{14,30},{16,0},... | collective-permute-start | bytes 589832 | tf_op jit(solution)/shard_map/ppermute | solution.py:161
  80.6 4.0 %finish.2 = (bf16[3,256,128]{2,1,0:T(8,128)(2,1)S(1)}, bf16[3,256,128]{2,1,0:T(8,128)(2,1)S(1)}, bf16[3,256,128]{2,1,0:T(8,128)(2,1)S(1)}, bf16[3,256,128]{2,1,0:T(8,128)(2,1)S(1)}) custom-call(s32[23]{0:T(128)S(1)} %pad_add_fusion.place_ref, f32[4,3,256,128]{3,2,1,0:T(8,128)S(1)} %get-tuple-element.52.refs_5_.refs_0_, bf16[20,128,512]{2,1,0:T(8,128)(2,1)S(1)} %copy-done.2, ...), custom_call_target="tpu_custom_call" | custom-call | flops 19327352832 | tf_op jit(solution)/shard_map/finish/pallas_call | solution.py:176
  84.6 1.6 %collective-permute-start.13 = (bf16[3,256,128]{2,1,0:T(8,128)(2,1)S(1)}, bf16[3,256,128]{2,1,0:T(8,128)(2,1)S(1)}, u32[]{:S(2)}, u32[]{:S(2)}) collective-permute-start(bf16[3,256,128]{2,1,0:T(8,128)(2,1)S(1)} %get-tuple-element.63), channel_id=1, source_target_pairs={{0,4},{2,6},{4,0},{6,2},{8,12},{10,14},{12,8},{14,10},{16,20},{18,... | collective-permute-start | bytes 589832 | tf_op jit(solution)/shard_map/ppermute | solution.py:161
  86.2 2.2 %collective-permute-start.14 = (bf16[3,256,128]{2,1,0:T(8,128)(2,1)S(1)}, bf16[3,256,128]{2,1,0:T(8,128)(2,1)S(1)}, u32[]{:S(2)}, u32[]{:S(2)}) collective-permute-start(bf16[3,256,128]{2,1,0:T(8,128)(2,1)S(1)} %get-tuple-element.64), channel_id=1, source_target_pairs={{0,8},{2,10},{4,12},{6,14},{8,0},{10,2},{12,4},{14,6},{16,24},{18,... | collective-permute-start | bytes 589832 | tf_op jit(solution)/shard_map/ppermute | solution.py:161
  88.3 1.0 collective-permute-start.15
  89.3 8.3 %attend.3 = (f32[4,2,256,128]{3,2,1,0:T(8,128)S(1)}, f32[2,16,128]{2,1,0:T(8,128)S(1)}) custom-call(s32[23]{0:T(128)S(1)} %pad_add_fusion.place_ref, s32[20]{0:T(128)S(1)} %copy-done.9, s32[3]{0:T(128)S(1)} %copy-done.10, bf16[2,784,128]{2,1,0:T(8,128)(2,1)S(1)} %get-tuple-element.58.refs_0_.refs_6_, ...), custom_call_target="tpu_custom_call" | custom-call | flops 34359738368 | tf_op jit(solution)/shard_map/attend/pallas_call | solution.py:176
  97.7 0.7 collective-permute-start.18
  98.4 1.0 collective-permute-done.15.refs_13_.refs_3_
  99.4 2.8 %finish.3 = (bf16[2,256,128]{2,1,0:T(8,128)(2,1)S(1)}, bf16[2,256,128]{2,1,0:T(8,128)(2,1)S(1)}, bf16[2,256,128]{2,1,0:T(8,128)(2,1)S(1)}, bf16[2,256,128]{2,1,0:T(8,128)(2,1)S(1)}) custom-call(s32[23]{0:T(128)S(1)} %pad_add_fusion.place_ref, f32[4,2,256,128]{3,2,1,0:T(8,128)S(1)} %get-tuple-element.66.refs_0_, bf16[20,128,512]{2,1,0:T(8,128)(2,1)S(1)} %copy-done.2, ...), custom_call_target="tpu_custom_call" | custom-call | flops 12884901888 | tf_op jit(solution)/shard_map/finish/pallas_call | solution.py:176
  102.2 1.9 %collective-permute-start.19 = (bf16[2,256,128]{2,1,0:T(8,128)(2,1)S(1)}, bf16[2,256,128]{2,1,0:T(8,128)(2,1)S(1)}, u32[]{:S(2)}, u32[]{:S(2)}) collective-permute-start(bf16[2,256,128]{2,1,0:T(8,128)(2,1)S(1)} %get-tuple-element.70), channel_id=1, source_target_pairs={{0,4},{2,6},{4,0},{6,2},{8,12},{10,14},{12,8},{14,10},{16,20},{18,... | collective-permute-start | bytes 393224 | tf_op jit(solution)/shard_map/ppermute | solution.py:161
  104.1 0.8 collective-permute-start.20
  104.9 0.9 collective-permute-start.21
  105.8 2.1 %collective-permute-done.19.refs_5_ = bf16[2,256,128]{2,1,0:T(8,128)(2,1)S(1)} collective-permute-done((bf16[2,256,128]{2,1,0:T(8,128)(2,1)S(1)}, bf16[2,256,128]{2,1,0:T(8,128)(2,1)S(1)}, u32[]{:S(2)}, u32[]{:S(2)}) %collective-permute-start.19) | collective-permute-done | bytes 131104 | tf_op jit(solution)/shard_map/ppermute | solution.py:161
  107.8 2.1 %collective-permute-done.20.refs_6_ = bf16[2,256,128]{2,1,0:T(8,128)(2,1)S(1)} collective-permute-done((bf16[2,256,128]{2,1,0:T(8,128)(2,1)S(1)}, bf16[2,256,128]{2,1,0:T(8,128)(2,1)S(1)}, u32[]{:S(2)}, u32[]{:S(2)}) %collective-permute-start.20) | collective-permute-done | bytes 131104 | tf_op jit(solution)/shard_map/ppermute | solution.py:161
  109.9 2.2 %collective-permute-done.21.refs_7_ = bf16[2,256,128]{2,1,0:T(8,128)(2,1)S(1)} collective-permute-done((bf16[2,256,128]{2,1,0:T(8,128)(2,1)S(1)}, bf16[2,256,128]{2,1,0:T(8,128)(2,1)S(1)}, u32[]{:S(2)}, u32[]{:S(2)}) %collective-permute-start.21) | collective-permute-done | bytes 131104 | tf_op jit(solution)/shard_map/ppermute | solution.py:161
  112.1 1.8 %put_in_place.1 = bf16[20,256,128]{2,1,0:T(8,128)(2,1)} custom-call(s32[23]{0:T(128)S(1)} %pad_add_fusion.place_ref, bf16[3,256,128]{2,1,0:T(8,128)(2,1)S(1)} %get-tuple-element.62.refs_7_.refs_10_.refs_0_, bf16[3,256,128]{2,1,0:T(8,128)(2,1)S(1)} %collective-permute-done.13.refs_11_.refs_1_, ...), custom_call_target="tpu_custom_call" | custom-call | tf_op jit(solution)/shard_map/put_in_place/pallas_call | solution.py:592
  (40 shorter events, 0.4 us)
Async XLA Ops:
  0.0 1.8 %copy-start = (bf16[256,20,128]{2,0,1:T(8,128)(2,1)S(1)}, bf16[256,20,128]{2,0,1:T(8,128)(2,1)}, u32[]{:S(2)}) copy-start(bf16[256,20,128]{2,0,1:T(8,128)(2,1)} %param.12) | copy-start | bytes 3932164
  0.0 6.8 %copy-start.1 = (bf16[256,20,128]{2,0,1:T(8,128)(2,1)S(1)}, bf16[256,20,128]{2,0,1:T(8,128)(2,1)}, u32[]{:S(2)}) copy-start(bf16[256,20,128]{2,0,1:T(8,128)(2,1)} %param.11) | copy-start | bytes 3932164
  0.0 5.2 %copy-start.9 = (s32[20]{0:T(128)S(1)}, s32[20]{0:T(128)}, u32[]{:S(2)}) copy-start(s32[20]{0:T(128)} %window_ref.3) | copy-start | bytes 244
  0.0 6.8 %copy-start.7 = (f32[20,128]{1,0:T(8,128)S(1)}, f32[20,128]{1,0:T(8,128)}, u32[]{:S(2)}) copy-start(f32[20,128]{1,0:T(8,128)} %refs_2_.5) | copy-start | bytes 30724
  0.0 6.8 %copy-start.8 = (f32[20,128]{1,0:T(8,128)S(1)}, f32[20,128]{1,0:T(8,128)}, u32[]{:S(2)}) copy-start(f32[20,128]{1,0:T(8,128)} %refs_3_.3) | copy-start | bytes 30724
  0.0 6.8 %copy-start.5 = (f32[20,256]{1,0:T(8,128)S(1)}, f32[20,256]{1,0:T(8,128)}, u32[]{:S(2)}) copy-start(f32[20,256]{1,0:T(8,128)} %refs_4_.3) | copy-start | bytes 61444
  0.0 6.8 %copy-start.6 = (f32[20,256]{1,0:T(8,128)S(1)}, f32[20,256]{1,0:T(8,128)}, u32[]{:S(2)}) copy-start(f32[20,256]{1,0:T(8,128)} %refs_5_.3) | copy-start | bytes 61444
  2.2 4.6 %collective-permute-start = (f32[2,256]{1,0:T(2,128)S(1)}, f32[2,256]{1,0:T(2,128)S(1)}, u32[]{:S(2)}, u32[]{:S(2)}) collective-permute-start(f32[2,256]{1,0:T(2,128)S(1)} %pad_maximum_fusion.refs_0_), channel_id=1, source_target_pairs={{0,1},{1,0},{2,3},{3,2},{4,5},{5,4},{6,7},{7,6},{8,9},{9,8},{10,11... | collective-permute-start | bytes 6152 | tf_op jit(solution)/shard_map/ppermute | solution.py:668
  6.8 1.3 %copy-start.3 = (bf16[256,20,128]{2,0,1:T(8,128)(2,1)S(1)}, bf16[256,20,128]{2,0,1:T(8,128)(2,1)}, u32[]{:S(2)}) copy-start(bf16[256,20,128]{2,0,1:T(8,128)(2,1)} %param.13) | copy-start | bytes 3932164
  9.5 15.9 %collective-permute-start.1 = (bf16[3,800,128]{2,1,0:T(8,128)(2,1)S(1)}, bf16[3,800,128]{2,1,0:T(8,128)(2,1)S(1)}, u32[]{:S(2)}, u32[]{:S(2)}) collective-permute-start(bf16[3,800,128]{2,1,0:T(8,128)(2,1)S(1)} %get-tuple-element.40), channel_id=1, source_target_pairs={{0,4},{2,6},{4,0},{6,2},{8,12},{10,14},{12,8},{14,10},{16,20},{18,... | collective-permute-start | bytes 1843208 | tf_op jit(solution)/shard_map/ppermute | solution.py:161
  11.6 16.8 %collective-permute-start.2 = (bf16[3,800,128]{2,1,0:T(8,128)(2,1)S(1)}, bf16[3,800,128]{2,1,0:T(8,128)(2,1)S(1)}, u32[]{:S(2)}, u32[]{:S(2)}) collective-permute-start(bf16[3,800,128]{2,1,0:T(8,128)(2,1)S(1)} %get-tuple-element.41), channel_id=1, source_target_pairs={{0,8},{2,10},{4,12},{6,14},{8,0},{10,2},{12,4},{14,6},{16,24},{18,... | collective-permute-start | bytes 1843208 | tf_op jit(solution)/shard_map/ppermute | solution.py:161
  13.2 25.6 %collective-permute-start.3 = (bf16[3,800,128]{2,1,0:T(8,128)(2,1)S(1)}, bf16[3,800,128]{2,1,0:T(8,128)(2,1)S(1)}, u32[]{:S(2)}, u32[]{:S(2)}) collective-permute-start(bf16[3,800,128]{2,1,0:T(8,128)(2,1)S(1)} %get-tuple-element.42), channel_id=1, source_target_pairs={{0,12},{2,14},{4,8},{6,10},{8,4},{10,6},{12,0},{14,2},{16,28},{18,... | collective-permute-start | bytes 1843208 | tf_op jit(solution)/shard_map/ppermute | solution.py:161
  38.7 8.8 %copy-start.4 = (bf16[20,256,128]{2,1,0:T(8,128)(2,1)S(1)}, bf16[20,256,128]{2,1,0:T(8,128)(2,1)}, u32[]{:S(2)}) copy-start(bf16[20,256,128]{2,1,0:T(8,128)(2,1)} %refs_2_.7) | copy-start | bytes 3932164
  38.8 8.7 %copy-start.2 = (bf16[20,128,512]{2,1,0:T(8,128)(2,1)S(1)}, bf16[20,128,512]{2,1,0:T(8,128)(2,1)}, u32[]{:S(2)}) copy-start(bf16[20,128,512]{2,1,0:T(8,128)(2,1)} %refs_1_.3) | copy-start | bytes 7864324
  38.8 3.6 %collective-permute-start.4 = (bf16[4,3,544,128]{3,2,1,0:T(8,128)(2,1)S(1)}, bf16[4,3,544,128]{3,2,1,0:T(8,128)(2,1)S(1)}, u32[]{:S(2)}, u32[]{:S(2)}) collective-permute-start(bf16[4,3,544,128]{3,2,1,0:T(8,128)(2,1)S(1)} %stack.26.own_ref), channel_id=1, source_target_pairs={{0,2},{2,0},{4,6},{6,4},{8,10},{10,8},{12,14},{14,12},{16,18},{18,... | collective-permute-start | bytes 5013512 | tf_op jit(solution)/shard_map/ppermute | solution.py:161
  38.9 18.3 %collective-permute-start.6 = (bf16[2,784,128]{2,1,0:T(8,128)(2,1)S(1)}, bf16[2,784,128]{2,1,0:T(8,128)(2,1)S(1)}, u32[]{:S(2)}, u32[]{:S(2)}) collective-permute-start(bf16[2,784,128]{2,1,0:T(8,128)(2,1)S(1)} %get-tuple-element.51), channel_id=1, source_target_pairs={{0,4},{2,6},{4,0},{6,2},{8,12},{10,14},{12,8},{14,10},{16,20},{18,... | collective-permute-start | bytes 1204232 | tf_op jit(solution)/shard_map/ppermute | solution.py:161
  43.0 14.2 %copy-start.10 = (s32[3]{0:T(128)S(1)}, s32[3]{0:T(128)}, u32[]{:S(2)}) copy-start(s32[3]{0:T(128)} %edge_ref.3) | copy-start | bytes 40
  43.0 14.2 %collective-permute-start.5 = (bf16[3,16,128]{2,1,0:T(8,128)(2,1)S(1)}, bf16[3,16,128]{2,1,0:T(8,128)(2,1)S(1)}, u32[]{:S(2)}, u32[]{:S(2)}) collective-permute-start(bf16[3,16,128]{2,1,0:T(8,128)(2,1)S(1)} %lone_rows.1), channel_id=1, source_target_pairs={{16,0},{18,2},{20,4},{22,6},{24,8},{26,10},{28,12},{30,14},{17,1},... | collective-permute-start | bytes 36872 | tf_op jit(solution)/shard_map/ppermute | solution.py:161
  44.3 26.2 %collective-permute-start.10 = (bf16[2,784,128]{2,1,0:T(8,128)(2,1)S(1)}, bf16[2,784,128]{2,1,0:T(8,128)(2,1)S(1)}, u32[]{:S(2)}, u32[]{:S(2)}) collective-permute-start(bf16[2,784,128]{2,1,0:T(8,128)(2,1)S(1)} %get-tuple-element.56), channel_id=1, source_target_pairs={{0,8},{2,10},{4,12},{6,14},{8,0},{10,2},{12,4},{14,6},{16,24},{18,... | collective-permute-start | bytes 1204232 | tf_op jit(solution)/shard_map/ppermute | solution.py:161
  46.1 25.9 %collective-permute-start.11 = (bf16[2,784,128]{2,1,0:T(8,128)(2,1)S(1)}, bf16[2,784,128]{2,1,0:T(8,128)(2,1)S(1)}, u32[]{:S(2)}, u32[]{:S(2)}) collective-permute-start(bf16[2,784,128]{2,1,0:T(8,128)(2,1)S(1)} %get-tuple-element.57), channel_id=1, source_target_pairs={{0,12},{2,14},{4,8},{6,10},{8,4},{10,6},{12,0},{14,2},{16,28},{18,... | collective-permute-start | bytes 1204232 | tf_op jit(solution)/shard_map/ppermute | solution.py:161
  53.6 16.8 %collective-permute-start.7 = (bf16[3,384,128]{2,1,0:T(8,128)(2,1)S(1)}, bf16[3,384,128]{2,1,0:T(8,128)(2,1)S(1)}, u32[]{:S(2)}, u32[]{:S(2)}) collective-permute-start(bf16[3,384,128]{2,1,0:T(8,128)(2,1)S(1)} %gradients.2.refs_6_), channel_id=1, source_target_pairs={{0,16},{2,18},{4,20},{6,22},{8,24},{10,26},{12,28},{14,30},{16,0},... | collective-permute-start | bytes 884744 | tf_op jit(solution)/shard_map/ppermute | solution.py:161
  72.1 2.8 %collective-permute-start.12 = (bf16[4,2,528,128]{3,2,1,0:T(8,128)(2,1)S(1)}, bf16[4,2,528,128]{3,2,1,0:T(8,128)(2,1)S(1)}, u32[]{:S(2)}, u32[]{:S(2)}) collective-permute-start(bf16[4,2,528,128]{3,2,1,0:T(8,128)(2,1)S(1)} %stack.27), channel_id=1, source_target_pairs={{0,2},{2,0},{4,6},{6,4},{8,10},{10,8},{12,14},{14,12},{16,18},{18,... | collective-permute-start | bytes 3244040 | tf_op jit(solution)/shard_map/ppermute | solution.py:161
  72.2 8.4 %collective-permute-start.8 = (bf16[3,384,128]{2,1,0:T(8,128)(2,1)S(1)}, bf16[3,384,128]{2,1,0:T(8,128)(2,1)S(1)}, u32[]{:S(2)}, u32[]{:S(2)}) collective-permute-start(bf16[3,384,128]{2,1,0:T(8,128)(2,1)S(1)} %add_convert_fusion.refs_3_), channel_id=1, source_target_pairs={{0,2},{2,0},{4,6},{6,4},{8,10},{10,8},{12,14},{14,12},{16,18},{18,... | collective-permute-start | bytes 884744 | tf_op jit(solution)/shard_map/ppermute | solution.py:161
  72.7 7.9 %collective-permute-start.9 = (f32[3,16,128]{2,1,0:T(8,128)S(1)}, f32[3,16,128]{2,1,0:T(8,128)S(1)}, u32[]{:S(2)}, u32[]{:S(2)}) collective-permute-start(f32[3,16,128]{2,1,0:T(8,128)S(1)} %get-tuple-element.54), channel_id=1, source_target_pairs={{2,16},{6,20},{10,24},{14,28},{3,17},{7,21},{11,25},{15,29}} | collective-permute-start | bytes 73736 | tf_op jit(solution)/shard_map/ppermute | solution.py:161
  79.1 18.4 %collective-permute-start.16 = (bf16[2,384,128]{2,1,0:T(8,128)(2,1)S(1)}, bf16[2,384,128]{2,1,0:T(8,128)(2,1)S(1)}, u32[]{:S(2)}, u32[]{:S(2)}) collective-permute-start(bf16[2,384,128]{2,1,0:T(8,128)(2,1)S(1)} %gradients.3.refs_10_.refs_6_), channel_id=1, source_target_pairs={{0,16},{2,18},{4,20},{6,22},{8,24},{10,26},{12,28},{14,30},{16,0},... | collective-permute-start | bytes 589832 | tf_op jit(solution)/shard_map/ppermute | solution.py:161
  84.6 13.8 %collective-permute-start.13 = (bf16[3,256,128]{2,1,0:T(8,128)(2,1)S(1)}, bf16[3,256,128]{2,1,0:T(8,128)(2,1)S(1)}, u32[]{:S(2)}, u32[]{:S(2)}) collective-permute-start(bf16[3,256,128]{2,1,0:T(8,128)(2,1)S(1)} %get-tuple-element.63), channel_id=1, source_target_pairs={{0,4},{2,6},{4,0},{6,2},{8,12},{10,14},{12,8},{14,10},{16,20},{18,... | collective-permute-start | bytes 589832 | tf_op jit(solution)/shard_map/ppermute | solution.py:161
  86.2 12.3 %collective-permute-start.14 = (bf16[3,256,128]{2,1,0:T(8,128)(2,1)S(1)}, bf16[3,256,128]{2,1,0:T(8,128)(2,1)S(1)}, u32[]{:S(2)}, u32[]{:S(2)}) collective-permute-start(bf16[3,256,128]{2,1,0:T(8,128)(2,1)S(1)} %get-tuple-element.64), channel_id=1, source_target_pairs={{0,8},{2,10},{4,12},{6,14},{8,0},{10,2},{12,4},{14,6},{16,24},{18,... | collective-permute-start | bytes 589832 | tf_op jit(solution)/shard_map/ppermute | solution.py:161
  88.3 11.1 %collective-permute-start.15 = (bf16[3,256,128]{2,1,0:T(8,128)(2,1)S(1)}, bf16[3,256,128]{2,1,0:T(8,128)(2,1)S(1)}, u32[]{:S(2)}, u32[]{:S(2)}) collective-permute-start(bf16[3,256,128]{2,1,0:T(8,128)(2,1)S(1)} %get-tuple-element.65), channel_id=1, source_target_pairs={{0,12},{2,14},{4,8},{6,10},{8,4},{10,6},{12,0},{14,2},{16,28},{18,... | collective-permute-start | bytes 589832 | tf_op jit(solution)/shard_map/ppermute | solution.py:161
  97.6 1.8 %collective-permute-start.17 = (bf16[2,384,128]{2,1,0:T(8,128)(2,1)S(1)}, bf16[2,384,128]{2,1,0:T(8,128)(2,1)S(1)}, u32[]{:S(2)}, u32[]{:S(2)}) collective-permute-start(bf16[2,384,128]{2,1,0:T(8,128)(2,1)S(1)} %add_convert_fusion.1.refs_3_), channel_id=1, source_target_pairs={{0,2},{2,0},{4,6},{6,4},{8,10},{10,8},{12,14},{14,12},{16,18},{18,... | collective-permute-start | bytes 589832 | tf_op jit(solution)/shard_map/ppermute | solution.py:161
  97.7 0.7 collective-permute-start.18
  102.2 5.6 %collective-permute-start.19 = (bf16[2,256,128]{2,1,0:T(8,128)(2,1)S(1)}, bf16[2,256,128]{2,1,0:T(8,128)(2,1)S(1)}, u32[]{:S(2)}, u32[]{:S(2)}) collective-permute-start(bf16[2,256,128]{2,1,0:T(8,128)(2,1)S(1)} %get-tuple-element.70), channel_id=1, source_target_pairs={{0,4},{2,6},{4,0},{6,2},{8,12},{10,14},{12,8},{14,10},{16,20},{18,... | collective-permute-start | bytes 393224 | tf_op jit(solution)/shard_map/ppermute | solution.py:161
  104.1 5.8 %collective-permute-start.20 = (bf16[2,256,128]{2,1,0:T(8,128)(2,1)S(1)}, bf16[2,256,128]{2,1,0:T(8,128)(2,1)S(1)}, u32[]{:S(2)}, u32[]{:S(2)}) collective-permute-start(bf16[2,256,128]{2,1,0:T(8,128)(2,1)S(1)} %get-tuple-element.71), channel_id=1, source_target_pairs={{0,8},{2,10},{4,12},{6,14},{8,0},{10,2},{12,4},{14,6},{16,24},{18,... | collective-permute-start | bytes 393224 | tf_op jit(solution)/shard_map/ppermute | solution.py:161
  104.9 7.3 %collective-permute-start.21 = (bf16[2,256,128]{2,1,0:T(8,128)(2,1)S(1)}, bf16[2,256,128]{2,1,0:T(8,128)(2,1)S(1)}, u32[]{:S(2)}, u32[]{:S(2)}) collective-permute-start(bf16[2,256,128]{2,1,0:T(8,128)(2,1)S(1)} %get-tuple-element.72), channel_id=1, source_target_pairs={{0,12},{2,14},{4,8},{6,10},{8,4},{10,6},{12,0},{14,2},{16,28},{18,... | collective-permute-start | bytes 393224 | tf_op jit(solution)/shard_map/ppermute | solution.py:161

commit v4 on v3

--- a/solution.py
+++ b/solution.py
@@ -640,7 +640,7 @@
     rank = jnp.sum((order[None, :] > order[:, None]).astype(jnp.int32), axis=1)
     turn, seat = rank // peers, rank % peers
     taker = jnp.where(turn % 2 == 0, seat, peers - 1 - seat)
-    slot = taker * share + jnp.where(turn % 2 == 0, 0, chunks[0][1]) + turn // 2
+    slot = taker * share + turn
     table = jnp.sum(jnp.where(slot[:, None] == number[None, :], number[:, None], 0), axis=0)
     place = jnp.concatenate([jnp.stack([chip, core, half]).astype(jnp.int32), table])
 

time: 115 us -> 115 us (level)
  waiting for transfers between devices: 37.8 us -> 39.2 us
    ppermute x21, waiting for transfers between devices: 36.7 us -> 38.1 us  [exchanged(): return lax.ppermute(x, 'tok', pairs)]
  transfers between devices with their start and end apart: 22 -> 22, of which waited for: 11 -> 11; matrix products, arithmetic and copies ran while one was open for 0% -> 0% of each run, Pallas kernels for 33% -> 32%
where the time goes in v4:
time: 115 us
  Pallas kernels  42.4 us (37%)
  waiting for transfers between devices  39.2 us (34%)
  starting transfers between devices  28.7 us (25%)
  other arithmetic  2.67 us (2%)
  local copies, waits for them, and re-layouts  1.35 us (1%)
    pallas_call x11, Pallas kernels, in_vmem(): pl.pallas_call(kernel, out_shape=out_shape, in_specs=specs, out_specs=jax...  40.7 us
    ppermute x21, waiting for transfers between devices, exchanged(): return lax.ppermute(x, 'tok', pairs)  38.1 us
    ppermute x21, starting transfers between devices, exchanged(): return lax.ppermute(x, 'tok', pairs)  25.7 us
    ppermute x1, starting transfers between devices, regrouped_body(): sums = (squares, lax.ppermute(squares, 'head', [(0, 1), (1, 0)]))  3.02 us
  transfers between devices with their start and end apart: 22, of which 11 were waited for; matrix products, arithmetic and copies ran while one was open for 0% of the time, Pallas kernels for 32%

profile of v4, /device:TPU:0, one launch (start us, length us, event | category | flops | bytes accessed | tf_op | source)
XLA Modules:
  0.0 114.8 jit_solution(2675041768904367559)
XLA Ops:
  0.0 1.8 %multiply_reduce_fusion.1 = f32[256]{0:T(256)S(1)} fusion(bf16[256,20,128]{2,0,1:T(8,128)(2,1)} %param.11), kind=kLoop, calls=%fused_computation.1 | loop fusion | flops 1965824 | bytes 1311744 | tf_op jit(solution)/shard_map/reduce_sum | solution.py:665
  1.8 0.3 multiply_reduce_fusion
  2.2 3.0 %collective-permute-start = (f32[2,256]{1,0:T(2,128)S(1)}, f32[2,256]{1,0:T(2,128)S(1)}, u32[]{:S(2)}, u32[]{:S(2)}) collective-permute-start(f32[2,256]{1,0:T(2,128)S(1)} %pad_maximum_fusion.refs_0_), channel_id=1, source_target_pairs={{0,1},{1,0},{2,3},{3,2},{4,5},{5,4},{6,7},{7,6},{8,9},{9,8},{10,11... | collective-permute-start | bytes 6152 | tf_op jit(solution)/shard_map/ppermute | solution.py:668
  5.2 0.2 convert_reduce_fusion
  5.4 0.1 select_reduce_fusion
  5.5 0.1 pad_add_fusion.place_ref
  5.6 1.2 %collective-permute-done.refs_1_ = f32[2,256]{1,0:T(2,128)S(1)} collective-permute-done((f32[2,256]{1,0:T(2,128)S(1)}, f32[2,256]{1,0:T(2,128)S(1)}, u32[]{:S(2)}, u32[]{:S(2)}) %collective-permute-start) | collective-permute-done | bytes 2080 | tf_op jit(solution)/shard_map/ppermute | solution.py:668
  6.8 1.3 %copy-done.3 = bf16[256,20,128]{2,0,1:T(8,128)(2,1)S(1)} copy-done((bf16[256,20,128]{2,0,1:T(8,128)(2,1)S(1)}, bf16[256,20,128]{2,0,1:T(8,128)(2,1)}, u32[]{:S(2)}) %copy-start.3) | copy-done | bytes 1310744
  8.1 1.3 %pack.2 = (bf16[3,800,128]{2,1,0:T(8,128)(2,1)S(1)}, bf16[3,800,128]{2,1,0:T(8,128)(2,1)S(1)}, bf16[3,800,128]{2,1,0:T(8,128)(2,1)S(1)}, bf16[3,800,128]{2,1,0:T(8,128)(2,1)S(1)}) custom-call(s32[23]{0:T(128)S(1)} %pad_add_fusion.place_ref, f32[2,256]{1,0:T(2,128)S(1)} %pad_maximum_fusion.refs_0_, f32[2,256]{1,0:T(2,128)S(1)} %collective-permute-done.refs_1_, ...), custom_call_target="tpu_custom_call" | custom-call | tf_op jit(solution)/shard_map/pack/pallas_call | solution.py:176
  9.5 2.1 %collective-permute-start.1 = (bf16[3,800,128]{2,1,0:T(8,128)(2,1)S(1)}, bf16[3,800,128]{2,1,0:T(8,128)(2,1)S(1)}, u32[]{:S(2)}, u32[]{:S(2)}) collective-permute-start(bf16[3,800,128]{2,1,0:T(8,128)(2,1)S(1)} %get-tuple-element.40), channel_id=1, source_target_pairs={{0,4},{2,6},{4,0},{6,2},{8,12},{10,14},{12,8},{14,10},{16,20},{18,... | collective-permute-start | bytes 1843208 | tf_op jit(solution)/shard_map/ppermute | solution.py:161
  11.6 1.6 %collective-permute-start.2 = (bf16[3,800,128]{2,1,0:T(8,128)(2,1)S(1)}, bf16[3,800,128]{2,1,0:T(8,128)(2,1)S(1)}, u32[]{:S(2)}, u32[]{:S(2)}) collective-permute-start(bf16[3,800,128]{2,1,0:T(8,128)(2,1)S(1)} %get-tuple-element.41), channel_id=1, source_target_pairs={{0,8},{2,10},{4,12},{6,14},{8,0},{10,2},{12,4},{14,6},{16,24},{18,... | collective-permute-start | bytes 1843208 | tf_op jit(solution)/shard_map/ppermute | solution.py:161
  13.2 1.1 pack.3
  14.2 11.1 %collective-permute-done.1.refs_1_.refs_7_ = bf16[3,800,128]{2,1,0:T(8,128)(2,1)S(1)} collective-permute-done((bf16[3,800,128]{2,1,0:T(8,128)(2,1)S(1)}, bf16[3,800,128]{2,1,0:T(8,128)(2,1)S(1)}, u32[]{:S(2)}, u32[]{:S(2)}) %collective-permute-start.1) | collective-permute-done | bytes 614432 | tf_op jit(solution)/shard_map/ppermute | solution.py:161
  25.4 3.0 %collective-permute-done.2.refs_2_.refs_8_ = bf16[3,800,128]{2,1,0:T(8,128)(2,1)S(1)} collective-permute-done((bf16[3,800,128]{2,1,0:T(8,128)(2,1)S(1)}, bf16[3,800,128]{2,1,0:T(8,128)(2,1)S(1)}, u32[]{:S(2)}, u32[]{:S(2)}) %collective-permute-start.2) | collective-permute-done | bytes 614432 | tf_op jit(solution)/shard_map/ppermute | solution.py:161
  28.4 10.3 %collective-permute-done.3.refs_3_.refs_9_ = bf16[3,800,128]{2,1,0:T(8,128)(2,1)S(1)} collective-permute-done((bf16[3,800,128]{2,1,0:T(8,128)(2,1)S(1)}, bf16[3,800,128]{2,1,0:T(8,128)(2,1)S(1)}, u32[]{:S(2)}, u32[]{:S(2)}) %collective-permute-start.3) | collective-permute-done | bytes 614432 | tf_op jit(solution)/shard_map/ppermute | solution.py:161
  38.7 0.1 stack.26.own_ref
  38.9 1.7 %collective-permute-start.6 = (bf16[2,784,128]{2,1,0:T(8,128)(2,1)S(1)}, bf16[2,784,128]{2,1,0:T(8,128)(2,1)S(1)}, u32[]{:S(2)}, u32[]{:S(2)}) collective-permute-start(bf16[2,784,128]{2,1,0:T(8,128)(2,1)S(1)} %get-tuple-element.51), channel_id=1, source_target_pairs={{0,4},{2,6},{4,0},{6,2},{8,12},{10,14},{12,8},{14,10},{16,20},{18,... | collective-permute-start | bytes 1204232 | tf_op jit(solution)/shard_map/ppermute | solution.py:161
  40.7 1.8 %collective-permute-done.4.other_ref.refs_4_ = bf16[4,3,544,128]{3,2,1,0:T(8,128)(2,1)S(1)} collective-permute-done((bf16[4,3,544,128]{3,2,1,0:T(8,128)(2,1)S(1)}, bf16[4,3,544,128]{3,2,1,0:T(8,128)(2,1)S(1)}, u32[]{:S(2)}, u32[]{:S(2)}) %collective-permute-start.4) | collective-permute-done | bytes 1671200 | tf_op jit(solution)/shard_map/ppermute | solution.py:161
  42.5 0.6 lone_rows.1
  43.0 1.3 %collective-permute-start.5 = (bf16[3,16,128]{2,1,0:T(8,128)(2,1)S(1)}, bf16[3,16,128]{2,1,0:T(8,128)(2,1)S(1)}, u32[]{:S(2)}, u32[]{:S(2)}) collective-permute-start(bf16[3,16,128]{2,1,0:T(8,128)(2,1)S(1)} %lone_rows.1), channel_id=1, source_target_pairs={{16,0},{18,2},{20,4},{22,6},{24,8},{26,10},{28,12},{30,14},{17,1},... | collective-permute-start | bytes 36872 | tf_op jit(solution)/shard_map/ppermute | solution.py:161
  44.3 1.8 %collective-permute-start.10 = (bf16[2,784,128]{2,1,0:T(8,128)(2,1)S(1)}, bf16[2,784,128]{2,1,0:T(8,128)(2,1)S(1)}, u32[]{:S(2)}, u32[]{:S(2)}) collective-permute-start(bf16[2,784,128]{2,1,0:T(8,128)(2,1)S(1)} %get-tuple-element.56), channel_id=1, source_target_pairs={{0,8},{2,10},{4,12},{6,14},{8,0},{10,2},{12,4},{14,6},{16,24},{18,... | collective-permute-start | bytes 1204232 | tf_op jit(solution)/shard_map/ppermute | solution.py:161
  46.1 1.4 %collective-permute-start.11 = (bf16[2,784,128]{2,1,0:T(8,128)(2,1)S(1)}, bf16[2,784,128]{2,1,0:T(8,128)(2,1)S(1)}, u32[]{:S(2)}, u32[]{:S(2)}) collective-permute-start(bf16[2,784,128]{2,1,0:T(8,128)(2,1)S(1)} %get-tuple-element.57), channel_id=1, source_target_pairs={{0,12},{2,14},{4,8},{6,10},{8,4},{10,6},{12,0},{14,2},{16,28},{18,... | collective-permute-start | bytes 1204232 | tf_op jit(solution)/shard_map/ppermute | solution.py:161
  47.5 6.1 %gradients.2.refs_6_ = bf16[3,384,128]{2,1,0:T(8,128)(2,1)S(1)} custom-call(s32[23]{0:T(128)S(1)} %pad_add_fusion.place_ref, bf16[20,128,512]{2,1,0:T(8,128)(2,1)S(1)} %copy-done.2, bf16[20,256,128]{2,1,0:T(8,128)(2,1)S(1)} %copy-done.4, bf16[3,800,128]{2,1,0:T(8,128)(2,1)S(1)} %get-tuple-element.47.refs_0_.refs_6_, ...), custom_call_target="tpu_custom_call" | custom-call | tf_op jit(solution)/shard_map/gradients/pallas_call | solution.py:176
  53.6 3.6 %collective-permute-start.7 = (bf16[3,384,128]{2,1,0:T(8,128)(2,1)S(1)}, bf16[3,384,128]{2,1,0:T(8,128)(2,1)S(1)}, u32[]{:S(2)}, u32[]{:S(2)}) collective-permute-start(bf16[3,384,128]{2,1,0:T(8,128)(2,1)S(1)} %gradients.2.refs_6_), channel_id=1, source_target_pairs={{0,16},{2,18},{4,20},{6,22},{8,24},{10,26},{12,28},{14,30},{16,0},... | collective-permute-start | bytes 884744 | tf_op jit(solution)/shard_map/ppermute | solution.py:161
  57.3 13.9 %attend.2 = (f32[4,3,256,128]{3,2,1,0:T(8,128)S(1)}, f32[3,16,128]{2,1,0:T(8,128)S(1)}) custom-call(s32[23]{0:T(128)S(1)} %pad_add_fusion.place_ref, s32[20]{0:T(128)S(1)} %copy-done.9, s32[3]{0:T(128)S(1)} %copy-done.10, bf16[3,800,128]{2,1,0:T(8,128)(2,1)S(1)} %get-tuple-element.47.refs_0_.refs_6_, ...), custom_call_target="tpu_custom_call" | custom-call | flops 51539607552 | tf_op jit(solution)/shard_map/attend/pallas_call | solution.py:176
  71.2 0.1 add_convert_fusion.refs_3_
  71.3 0.7 collective-permute-done.11.refs_3_.refs_9_
  72.1 0.1 collective-permute-start.12
  72.2 0.5 collective-permute-start.8
  72.7 0.7 collective-permute-start.9
  73.3 1.5 %collective-permute-done.12.refs_4_ = bf16[4,2,528,128]{3,2,1,0:T(8,128)(2,1)S(1)} collective-permute-done((bf16[4,2,528,128]{3,2,1,0:T(8,128)(2,1)S(1)}, bf16[4,2,528,128]{3,2,1,0:T(8,128)(2,1)S(1)}, u32[]{:S(2)}, u32[]{:S(2)}) %collective-permute-start.12) | collective-permute-done | bytes 1081376 | tf_op jit(solution)/shard_map/ppermute | solution.py:161
  74.9 4.2 %gradients.3.refs_10_.refs_6_ = bf16[2,384,128]{2,1,0:T(8,128)(2,1)S(1)} custom-call(s32[23]{0:T(128)S(1)} %pad_add_fusion.place_ref, bf16[20,128,512]{2,1,0:T(8,128)(2,1)S(1)} %copy-done.2, bf16[20,256,128]{2,1,0:T(8,128)(2,1)S(1)} %copy-done.4, bf16[2,784,128]{2,1,0:T(8,128)(2,1)S(1)} %get-tuple-element.58.refs_0_.refs_6_, ...), custom_call_target="tpu_custom_call" | custom-call | tf_op jit(solution)/shard_map/gradients/pallas_call | solution.py:176
  79.1 1.4 %collective-permute-start.16 = (bf16[2,384,128]{2,1,0:T(8,128)(2,1)S(1)}, bf16[2,384,128]{2,1,0:T(8,128)(2,1)S(1)}, u32[]{:S(2)}, u32[]{:S(2)}) collective-permute-start(bf16[2,384,128]{2,1,0:T(8,128)(2,1)S(1)} %gradients.3.refs_10_.refs_6_), channel_id=1, source_target_pairs={{0,16},{2,18},{4,20},{6,22},{8,24},{10,26},{12,28},{14,30},{16,0},... | collective-permute-start | bytes 589832 | tf_op jit(solution)/shard_map/ppermute | solution.py:161
  80.6 4.0 %finish.2 = (bf16[3,256,128]{2,1,0:T(8,128)(2,1)S(1)}, bf16[3,256,128]{2,1,0:T(8,128)(2,1)S(1)}, bf16[3,256,128]{2,1,0:T(8,128)(2,1)S(1)}, bf16[3,256,128]{2,1,0:T(8,128)(2,1)S(1)}) custom-call(s32[23]{0:T(128)S(1)} %pad_add_fusion.place_ref, f32[4,3,256,128]{3,2,1,0:T(8,128)S(1)} %get-tuple-element.52.refs_5_.refs_0_, bf16[20,128,512]{2,1,0:T(8,128)(2,1)S(1)} %copy-done.2, ...), custom_call_target="tpu_custom_call" | custom-call | flops 19327352832 | tf_op jit(solution)/shard_map/finish/pallas_call | solution.py:176
  84.6 1.6 %collective-permute-start.13 = (bf16[3,256,128]{2,1,0:T(8,128)(2,1)S(1)}, bf16[3,256,128]{2,1,0:T(8,128)(2,1)S(1)}, u32[]{:S(2)}, u32[]{:S(2)}) collective-permute-start(bf16[3,256,128]{2,1,0:T(8,128)(2,1)S(1)} %get-tuple-element.63), channel_id=1, source_target_pairs={{0,4},{2,6},{4,0},{6,2},{8,12},{10,14},{12,8},{14,10},{16,20},{18,... | collective-permute-start | bytes 589832 | tf_op jit(solution)/shard_map/ppermute | solution.py:161
  86.2 2.2 %collective-permute-start.14 = (bf16[3,256,128]{2,1,0:T(8,128)(2,1)S(1)}, bf16[3,256,128]{2,1,0:T(8,128)(2,1)S(1)}, u32[]{:S(2)}, u32[]{:S(2)}) collective-permute-start(bf16[3,256,128]{2,1,0:T(8,128)(2,1)S(1)} %get-tuple-element.64), channel_id=1, source_target_pairs={{0,8},{2,10},{4,12},{6,14},{8,0},{10,2},{12,4},{14,6},{16,24},{18,... | collective-permute-start | bytes 589832 | tf_op jit(solution)/shard_map/ppermute | solution.py:161
  88.3 1.0 collective-permute-start.15
  89.3 6.5 %attend.3 = (f32[4,2,256,128]{3,2,1,0:T(8,128)S(1)}, f32[2,16,128]{2,1,0:T(8,128)S(1)}) custom-call(s32[23]{0:T(128)S(1)} %pad_add_fusion.place_ref, s32[20]{0:T(128)S(1)} %copy-done.9, s32[3]{0:T(128)S(1)} %copy-done.10, bf16[2,784,128]{2,1,0:T(8,128)(2,1)S(1)} %get-tuple-element.58.refs_0_.refs_6_, ...), custom_call_target="tpu_custom_call" | custom-call | flops 34359738368 | tf_op jit(solution)/shard_map/attend/pallas_call | solution.py:176
  95.8 0.5 collective-permute-start.17
  96.3 0.7 collective-permute-start.18
  97.0 2.4 %collective-permute-done.15.refs_13_.refs_3_ = bf16[3,256,128]{2,1,0:T(8,128)(2,1)S(1)} collective-permute-done((bf16[3,256,128]{2,1,0:T(8,128)(2,1)S(1)}, bf16[3,256,128]{2,1,0:T(8,128)(2,1)S(1)}, u32[]{:S(2)}, u32[]{:S(2)}) %collective-permute-start.15) | collective-permute-done | bytes 196640 | tf_op jit(solution)/shard_map/ppermute | solution.py:161
  99.4 2.8 %finish.3 = (bf16[2,256,128]{2,1,0:T(8,128)(2,1)S(1)}, bf16[2,256,128]{2,1,0:T(8,128)(2,1)S(1)}, bf16[2,256,128]{2,1,0:T(8,128)(2,1)S(1)}, bf16[2,256,128]{2,1,0:T(8,128)(2,1)S(1)}) custom-call(s32[23]{0:T(128)S(1)} %pad_add_fusion.place_ref, f32[4,2,256,128]{3,2,1,0:T(8,128)S(1)} %get-tuple-element.66.refs_0_, bf16[20,128,512]{2,1,0:T(8,128)(2,1)S(1)} %copy-done.2, ...), custom_call_target="tpu_custom_call" | custom-call | flops 12884901888 | tf_op jit(solution)/shard_map/finish/pallas_call | solution.py:176
  102.2 1.8 %collective-permute-start.19 = (bf16[2,256,128]{2,1,0:T(8,128)(2,1)S(1)}, bf16[2,256,128]{2,1,0:T(8,128)(2,1)S(1)}, u32[]{:S(2)}, u32[]{:S(2)}) collective-permute-start(bf16[2,256,128]{2,1,0:T(8,128)(2,1)S(1)} %get-tuple-element.70), channel_id=1, source_target_pairs={{0,4},{2,6},{4,0},{6,2},{8,12},{10,14},{12,8},{14,10},{16,20},{18,... | collective-permute-start | bytes 393224 | tf_op jit(solution)/shard_map/ppermute | solution.py:161
  104.1 1.7 %collective-permute-start.21 = (bf16[2,256,128]{2,1,0:T(8,128)(2,1)S(1)}, bf16[2,256,128]{2,1,0:T(8,128)(2,1)S(1)}, u32[]{:S(2)}, u32[]{:S(2)}) collective-permute-start(bf16[2,256,128]{2,1,0:T(8,128)(2,1)S(1)} %get-tuple-element.72), channel_id=1, source_target_pairs={{0,12},{2,14},{4,8},{6,10},{8,4},{10,6},{12,0},{14,2},{16,28},{18,... | collective-permute-start | bytes 393224 | tf_op jit(solution)/shard_map/ppermute | solution.py:161
  105.8 2.6 %collective-permute-done.19.refs_5_ = bf16[2,256,128]{2,1,0:T(8,128)(2,1)S(1)} collective-permute-done((bf16[2,256,128]{2,1,0:T(8,128)(2,1)S(1)}, bf16[2,256,128]{2,1,0:T(8,128)(2,1)S(1)}, u32[]{:S(2)}, u32[]{:S(2)}) %collective-permute-start.19) | collective-permute-done | bytes 131104 | tf_op jit(solution)/shard_map/ppermute | solution.py:161
  108.4 1.6 %collective-permute-done.20.refs_6_ = bf16[2,256,128]{2,1,0:T(8,128)(2,1)S(1)} collective-permute-done((bf16[2,256,128]{2,1,0:T(8,128)(2,1)S(1)}, bf16[2,256,128]{2,1,0:T(8,128)(2,1)S(1)}, u32[]{:S(2)}, u32[]{:S(2)}) %collective-permute-start.20) | collective-permute-done | bytes 131104 | tf_op jit(solution)/shard_map/ppermute | solution.py:161
  110.1 2.8 %collective-permute-done.21.refs_7_ = bf16[2,256,128]{2,1,0:T(8,128)(2,1)S(1)} collective-permute-done((bf16[2,256,128]{2,1,0:T(8,128)(2,1)S(1)}, bf16[2,256,128]{2,1,0:T(8,128)(2,1)S(1)}, u32[]{:S(2)}, u32[]{:S(2)}) %collective-permute-start.21) | collective-permute-done | bytes 131104 | tf_op jit(solution)/shard_map/ppermute | solution.py:161
  112.9 1.8 %put_in_place.1 = bf16[20,256,128]{2,1,0:T(8,128)(2,1)} custom-call(s32[23]{0:T(128)S(1)} %pad_add_fusion.place_ref, bf16[3,256,128]{2,1,0:T(8,128)(2,1)S(1)} %get-tuple-element.62.refs_7_.refs_10_.refs_0_, bf16[3,256,128]{2,1,0:T(8,128)(2,1)S(1)} %collective-permute-done.13.refs_11_.refs_1_, ...), custom_call_target="tpu_custom_call" | custom-call | tf_op jit(solution)/shard_map/put_in_place/pallas_call | solution.py:592
  (40 shorter events, 0.3 us)
Async XLA Ops:
  0.0 1.8 %copy-start = (bf16[256,20,128]{2,0,1:T(8,128)(2,1)S(1)}, bf16[256,20,128]{2,0,1:T(8,128)(2,1)}, u32[]{:S(2)}) copy-start(bf16[256,20,128]{2,0,1:T(8,128)(2,1)} %param.12) | copy-start | bytes 3932164
  0.0 6.8 %copy-start.1 = (bf16[256,20,128]{2,0,1:T(8,128)(2,1)S(1)}, bf16[256,20,128]{2,0,1:T(8,128)(2,1)}, u32[]{:S(2)}) copy-start(bf16[256,20,128]{2,0,1:T(8,128)(2,1)} %param.11) | copy-start | bytes 3932164
  0.0 5.2 %copy-start.9 = (s32[20]{0:T(128)S(1)}, s32[20]{0:T(128)}, u32[]{:S(2)}) copy-start(s32[20]{0:T(128)} %window_ref.3) | copy-start | bytes 244
  0.0 6.8 %copy-start.7 = (f32[20,128]{1,0:T(8,128)S(1)}, f32[20,128]{1,0:T(8,128)}, u32[]{:S(2)}) copy-start(f32[20,128]{1,0:T(8,128)} %refs_2_.5) | copy-start | bytes 30724
  0.0 6.8 %copy-start.8 = (f32[20,128]{1,0:T(8,128)S(1)}, f32[20,128]{1,0:T(8,128)}, u32[]{:S(2)}) copy-start(f32[20,128]{1,0:T(8,128)} %refs_3_.3) | copy-start | bytes 30724
  0.0 6.8 %copy-start.5 = (f32[20,256]{1,0:T(8,128)S(1)}, f32[20,256]{1,0:T(8,128)}, u32[]{:S(2)}) copy-start(f32[20,256]{1,0:T(8,128)} %refs_4_.3) | copy-start | bytes 61444
  0.0 6.8 %copy-start.6 = (f32[20,256]{1,0:T(8,128)S(1)}, f32[20,256]{1,0:T(8,128)}, u32[]{:S(2)}) copy-start(f32[20,256]{1,0:T(8,128)} %refs_5_.3) | copy-start | bytes 61444
  2.2 4.6 %collective-permute-start = (f32[2,256]{1,0:T(2,128)S(1)}, f32[2,256]{1,0:T(2,128)S(1)}, u32[]{:S(2)}, u32[]{:S(2)}) collective-permute-start(f32[2,256]{1,0:T(2,128)S(1)} %pad_maximum_fusion.refs_0_), channel_id=1, source_target_pairs={{0,1},{1,0},{2,3},{3,2},{4,5},{5,4},{6,7},{7,6},{8,9},{9,8},{10,11... | collective-permute-start | bytes 6152 | tf_op jit(solution)/shard_map/ppermute | solution.py:668
  6.8 1.3 %copy-start.3 = (bf16[256,20,128]{2,0,1:T(8,128)(2,1)S(1)}, bf16[256,20,128]{2,0,1:T(8,128)(2,1)}, u32[]{:S(2)}) copy-start(bf16[256,20,128]{2,0,1:T(8,128)(2,1)} %param.13) | copy-start | bytes 3932164
  9.5 15.9 %collective-permute-start.1 = (bf16[3,800,128]{2,1,0:T(8,128)(2,1)S(1)}, bf16[3,800,128]{2,1,0:T(8,128)(2,1)S(1)}, u32[]{:S(2)}, u32[]{:S(2)}) collective-permute-start(bf16[3,800,128]{2,1,0:T(8,128)(2,1)S(1)} %get-tuple-element.40), channel_id=1, source_target_pairs={{0,4},{2,6},{4,0},{6,2},{8,12},{10,14},{12,8},{14,10},{16,20},{18,... | collective-permute-start | bytes 1843208 | tf_op jit(solution)/shard_map/ppermute | solution.py:161
  11.6 16.8 %collective-permute-start.2 = (bf16[3,800,128]{2,1,0:T(8,128)(2,1)S(1)}, bf16[3,800,128]{2,1,0:T(8,128)(2,1)S(1)}, u32[]{:S(2)}, u32[]{:S(2)}) collective-permute-start(bf16[3,800,128]{2,1,0:T(8,128)(2,1)S(1)} %get-tuple-element.41), channel_id=1, source_target_pairs={{0,8},{2,10},{4,12},{6,14},{8,0},{10,2},{12,4},{14,6},{16,24},{18,... | collective-permute-start | bytes 1843208 | tf_op jit(solution)/shard_map/ppermute | solution.py:161
  13.2 25.5 %collective-permute-start.3 = (bf16[3,800,128]{2,1,0:T(8,128)(2,1)S(1)}, bf16[3,800,128]{2,1,0:T(8,128)(2,1)S(1)}, u32[]{:S(2)}, u32[]{:S(2)}) collective-permute-start(bf16[3,800,128]{2,1,0:T(8,128)(2,1)S(1)} %get-tuple-element.42), channel_id=1, source_target_pairs={{0,12},{2,14},{4,8},{6,10},{8,4},{10,6},{12,0},{14,2},{16,28},{18,... | collective-permute-start | bytes 1843208 | tf_op jit(solution)/shard_map/ppermute | solution.py:161
  38.7 8.8 %copy-start.4 = (bf16[20,256,128]{2,1,0:T(8,128)(2,1)S(1)}, bf16[20,256,128]{2,1,0:T(8,128)(2,1)}, u32[]{:S(2)}) copy-start(bf16[20,256,128]{2,1,0:T(8,128)(2,1)} %refs_2_.7) | copy-start | bytes 3932164
  38.8 8.7 %copy-start.2 = (bf16[20,128,512]{2,1,0:T(8,128)(2,1)S(1)}, bf16[20,128,512]{2,1,0:T(8,128)(2,1)}, u32[]{:S(2)}) copy-start(bf16[20,128,512]{2,1,0:T(8,128)(2,1)} %refs_1_.3) | copy-start | bytes 7864324
  38.8 3.6 %collective-permute-start.4 = (bf16[4,3,544,128]{3,2,1,0:T(8,128)(2,1)S(1)}, bf16[4,3,544,128]{3,2,1,0:T(8,128)(2,1)S(1)}, u32[]{:S(2)}, u32[]{:S(2)}) collective-permute-start(bf16[4,3,544,128]{3,2,1,0:T(8,128)(2,1)S(1)} %stack.26.own_ref), channel_id=1, source_target_pairs={{0,2},{2,0},{4,6},{6,4},{8,10},{10,8},{12,14},{14,12},{16,18},{18,... | collective-permute-start | bytes 5013512 | tf_op jit(solution)/shard_map/ppermute | solution.py:161
  38.9 18.3 %collective-permute-start.6 = (bf16[2,784,128]{2,1,0:T(8,128)(2,1)S(1)}, bf16[2,784,128]{2,1,0:T(8,128)(2,1)S(1)}, u32[]{:S(2)}, u32[]{:S(2)}) collective-permute-start(bf16[2,784,128]{2,1,0:T(8,128)(2,1)S(1)} %get-tuple-element.51), channel_id=1, source_target_pairs={{0,4},{2,6},{4,0},{6,2},{8,12},{10,14},{12,8},{14,10},{16,20},{18,... | collective-permute-start | bytes 1204232 | tf_op jit(solution)/shard_map/ppermute | solution.py:161
  43.0 14.2 %copy-start.10 = (s32[3]{0:T(128)S(1)}, s32[3]{0:T(128)}, u32[]{:S(2)}) copy-start(s32[3]{0:T(128)} %edge_ref.3) | copy-start | bytes 40
  43.0 14.2 %collective-permute-start.5 = (bf16[3,16,128]{2,1,0:T(8,128)(2,1)S(1)}, bf16[3,16,128]{2,1,0:T(8,128)(2,1)S(1)}, u32[]{:S(2)}, u32[]{:S(2)}) collective-permute-start(bf16[3,16,128]{2,1,0:T(8,128)(2,1)S(1)} %lone_rows.1), channel_id=1, source_target_pairs={{16,0},{18,2},{20,4},{22,6},{24,8},{26,10},{28,12},{30,14},{17,1},... | collective-permute-start | bytes 36872 | tf_op jit(solution)/shard_map/ppermute | solution.py:161
  44.3 26.9 %collective-permute-start.10 = (bf16[2,784,128]{2,1,0:T(8,128)(2,1)S(1)}, bf16[2,784,128]{2,1,0:T(8,128)(2,1)S(1)}, u32[]{:S(2)}, u32[]{:S(2)}) collective-permute-start(bf16[2,784,128]{2,1,0:T(8,128)(2,1)S(1)} %get-tuple-element.56), channel_id=1, source_target_pairs={{0,8},{2,10},{4,12},{6,14},{8,0},{10,2},{12,4},{14,6},{16,24},{18,... | collective-permute-start | bytes 1204232 | tf_op jit(solution)/shard_map/ppermute | solution.py:161
  46.1 25.9 %collective-permute-start.11 = (bf16[2,784,128]{2,1,0:T(8,128)(2,1)S(1)}, bf16[2,784,128]{2,1,0:T(8,128)(2,1)S(1)}, u32[]{:S(2)}, u32[]{:S(2)}) collective-permute-start(bf16[2,784,128]{2,1,0:T(8,128)(2,1)S(1)} %get-tuple-element.57), channel_id=1, source_target_pairs={{0,12},{2,14},{4,8},{6,10},{8,4},{10,6},{12,0},{14,2},{16,28},{18,... | collective-permute-start | bytes 1204232 | tf_op jit(solution)/shard_map/ppermute | solution.py:161
  53.6 17.5 %collective-permute-start.7 = (bf16[3,384,128]{2,1,0:T(8,128)(2,1)S(1)}, bf16[3,384,128]{2,1,0:T(8,128)(2,1)S(1)}, u32[]{:S(2)}, u32[]{:S(2)}) collective-permute-start(bf16[3,384,128]{2,1,0:T(8,128)(2,1)S(1)} %gradients.2.refs_6_), channel_id=1, source_target_pairs={{0,16},{2,18},{4,20},{6,22},{8,24},{10,26},{12,28},{14,30},{16,0},... | collective-permute-start | bytes 884744 | tf_op jit(solution)/shard_map/ppermute | solution.py:161
  72.1 2.8 %collective-permute-start.12 = (bf16[4,2,528,128]{3,2,1,0:T(8,128)(2,1)S(1)}, bf16[4,2,528,128]{3,2,1,0:T(8,128)(2,1)S(1)}, u32[]{:S(2)}, u32[]{:S(2)}) collective-permute-start(bf16[4,2,528,128]{3,2,1,0:T(8,128)(2,1)S(1)} %stack.27), channel_id=1, source_target_pairs={{0,2},{2,0},{4,6},{6,4},{8,10},{10,8},{12,14},{14,12},{16,18},{18,... | collective-permute-start | bytes 3244040 | tf_op jit(solution)/shard_map/ppermute | solution.py:161
  72.2 8.4 %collective-permute-start.8 = (bf16[3,384,128]{2,1,0:T(8,128)(2,1)S(1)}, bf16[3,384,128]{2,1,0:T(8,128)(2,1)S(1)}, u32[]{:S(2)}, u32[]{:S(2)}) collective-permute-start(bf16[3,384,128]{2,1,0:T(8,128)(2,1)S(1)} %add_convert_fusion.refs_3_), channel_id=1, source_target_pairs={{0,2},{2,0},{4,6},{6,4},{8,10},{10,8},{12,14},{14,12},{16,18},{18,... | collective-permute-start | bytes 884744 | tf_op jit(solution)/shard_map/ppermute | solution.py:161
  72.7 7.9 %collective-permute-start.9 = (f32[3,16,128]{2,1,0:T(8,128)S(1)}, f32[3,16,128]{2,1,0:T(8,128)S(1)}, u32[]{:S(2)}, u32[]{:S(2)}) collective-permute-start(f32[3,16,128]{2,1,0:T(8,128)S(1)} %get-tuple-element.54), channel_id=1, source_target_pairs={{2,16},{6,20},{10,24},{14,28},{3,17},{7,21},{11,25},{15,29}} | collective-permute-start | bytes 73736 | tf_op jit(solution)/shard_map/ppermute | solution.py:161
  79.1 16.7 %collective-permute-start.16 = (bf16[2,384,128]{2,1,0:T(8,128)(2,1)S(1)}, bf16[2,384,128]{2,1,0:T(8,128)(2,1)S(1)}, u32[]{:S(2)}, u32[]{:S(2)}) collective-permute-start(bf16[2,384,128]{2,1,0:T(8,128)(2,1)S(1)} %gradients.3.refs_10_.refs_6_), channel_id=1, source_target_pairs={{0,16},{2,18},{4,20},{6,22},{8,24},{10,26},{12,28},{14,30},{16,0},... | collective-permute-start | bytes 589832 | tf_op jit(solution)/shard_map/ppermute | solution.py:161
  84.6 12.4 %collective-permute-start.13 = (bf16[3,256,128]{2,1,0:T(8,128)(2,1)S(1)}, bf16[3,256,128]{2,1,0:T(8,128)(2,1)S(1)}, u32[]{:S(2)}, u32[]{:S(2)}) collective-permute-start(bf16[3,256,128]{2,1,0:T(8,128)(2,1)S(1)} %get-tuple-element.63), channel_id=1, source_target_pairs={{0,4},{2,6},{4,0},{6,2},{8,12},{10,14},{12,8},{14,10},{16,20},{18,... | collective-permute-start | bytes 589832 | tf_op jit(solution)/shard_map/ppermute | solution.py:161
  86.2 10.8 %collective-permute-start.14 = (bf16[3,256,128]{2,1,0:T(8,128)(2,1)S(1)}, bf16[3,256,128]{2,1,0:T(8,128)(2,1)S(1)}, u32[]{:S(2)}, u32[]{:S(2)}) collective-permute-start(bf16[3,256,128]{2,1,0:T(8,128)(2,1)S(1)} %get-tuple-element.64), channel_id=1, source_target_pairs={{0,8},{2,10},{4,12},{6,14},{8,0},{10,2},{12,4},{14,6},{16,24},{18,... | collective-permute-start | bytes 589832 | tf_op jit(solution)/shard_map/ppermute | solution.py:161
  88.3 11.1 %collective-permute-start.15 = (bf16[3,256,128]{2,1,0:T(8,128)(2,1)S(1)}, bf16[3,256,128]{2,1,0:T(8,128)(2,1)S(1)}, u32[]{:S(2)}, u32[]{:S(2)}) collective-permute-start(bf16[3,256,128]{2,1,0:T(8,128)(2,1)S(1)} %get-tuple-element.65), channel_id=1, source_target_pairs={{0,12},{2,14},{4,8},{6,10},{8,4},{10,6},{12,0},{14,2},{16,28},{18,... | collective-permute-start | bytes 589832 | tf_op jit(solution)/shard_map/ppermute | solution.py:161
  95.8 3.6 %collective-permute-start.17 = (bf16[2,384,128]{2,1,0:T(8,128)(2,1)S(1)}, bf16[2,384,128]{2,1,0:T(8,128)(2,1)S(1)}, u32[]{:S(2)}, u32[]{:S(2)}) collective-permute-start(bf16[2,384,128]{2,1,0:T(8,128)(2,1)S(1)} %add_convert_fusion.1.refs_3_), channel_id=1, source_target_pairs={{0,2},{2,0},{4,6},{6,4},{8,10},{10,8},{12,14},{14,12},{16,18},{18,... | collective-permute-start | bytes 589832 | tf_op jit(solution)/shard_map/ppermute | solution.py:161
  96.3 0.7 collective-permute-start.18
  102.2 6.2 %collective-permute-start.19 = (bf16[2,256,128]{2,1,0:T(8,128)(2,1)S(1)}, bf16[2,256,128]{2,1,0:T(8,128)(2,1)S(1)}, u32[]{:S(2)}, u32[]{:S(2)}) collective-permute-start(bf16[2,256,128]{2,1,0:T(8,128)(2,1)S(1)} %get-tuple-element.70), channel_id=1, source_target_pairs={{0,4},{2,6},{4,0},{6,2},{8,12},{10,14},{12,8},{14,10},{16,20},{18,... | collective-permute-start | bytes 393224 | tf_op jit(solution)/shard_map/ppermute | solution.py:161
  104.1 6.0 %collective-permute-start.20 = (bf16[2,256,128]{2,1,0:T(8,128)(2,1)S(1)}, bf16[2,256,128]{2,1,0:T(8,128)(2,1)S(1)}, u32[]{:S(2)}, u32[]{:S(2)}) collective-permute-start(bf16[2,256,128]{2,1,0:T(8,128)(2,1)S(1)} %get-tuple-element.71), channel_id=1, source_target_pairs={{0,8},{2,10},{4,12},{6,14},{8,0},{10,2},{12,4},{14,6},{16,24},{18,... | collective-permute-start | bytes 393224 | tf_op jit(solution)/shard_map/ppermute | solution.py:161
  104.1 8.8 %collective-permute-start.21 = (bf16[2,256,128]{2,1,0:T(8,128)(2,1)S(1)}, bf16[2,256,128]{2,1,0:T(8,128)(2,1)S(1)}, u32[]{:S(2)}, u32[]{:S(2)}) collective-permute-start(bf16[2,256,128]{2,1,0:T(8,128)(2,1)S(1)} %get-tuple-element.72), channel_id=1, source_target_pairs={{0,12},{2,14},{4,8},{6,10},{8,4},{10,6},{12,0},{14,2},{16,28},{18,... | collective-permute-start | bytes 393224 | tf_op jit(solution)/shard_map/ppermute | solution.py:161

commit v5 on v4

--- a/solution.py
+++ b/solution.py
@@ -744,7 +744,7 @@
         from_half, _ = lax.optimization_barrier((from_half, attended))
         own_sum = (grad.astype(jnp.float32) + from_half.astype(jnp.float32)).astype(jnp.bfloat16)
         ready = (attended, (own_sum, exchanged(own_sum, core_pairs)), patch, own, first)
-    pieces = pieces + dealt(finished(ready, pieces))
+    pieces = pieces + dealt(finished(ready, pieces[:-1]))
     whole = put_in_place(place, pieces, peers, chunks, share)
     return jnp.transpose(whole, (1, 0, 2))
 

time: 115 us -> 113 us (0.983); the launches traced: 115 us -> 112 us
  waiting for transfers between devices: 39.2 us -> 35.3 us
    ppermute x21, waiting for transfers between devices: 38.1 us -> 34.2 us  [exchanged(): return lax.ppermute(x, 'tok', pairs)]
  transfers between devices with their start and end apart: 22 -> 22, of which waited for: 11 -> 9; matrix products, arithmetic and copies ran while one was open for 0% -> 0% of each run, Pallas kernels for 32% -> 36%
where the time goes in v5:
time: 113 us; the launch traced here: 112 us
  Pallas kernels  43 us (38%)
  waiting for transfers between devices  35.3 us (31%)
  starting transfers between devices  28.8 us (25%)
  other arithmetic  2.67 us (2%)
  local copies, waits for them, and re-layouts  1.35 us (1%)
    pallas_call x11, Pallas kernels, in_vmem(): pl.pallas_call(kernel, out_shape=out_shape, in_specs=specs, out_specs=jax...  41.3 us
    ppermute x21, waiting for transfers between devices, exchanged(): return lax.ppermute(x, 'tok', pairs)  34.2 us
    ppermute x21, starting transfers between devices, exchanged(): return lax.ppermute(x, 'tok', pairs)  25.8 us
    ppermute x1, starting transfers between devices, regrouped_body(): sums = (squares, lax.ppermute(squares, 'head', [(0, 1), (1, 0)]))  3.02 us
  transfers between devices with their start and end apart: 22, of which 9 were waited for; matrix products, arithmetic and copies ran while one was open for 0% of the time, Pallas kernels for 36%

profile of v5, /device:TPU:0, one launch (start us, length us, event | category | flops | bytes accessed | tf_op | source)
XLA Modules:
  0.0 111.7 jit_solution(744571786742326638)
XLA Ops:
  0.0 1.8 %multiply_reduce_fusion.1 = f32[256]{0:T(256)S(1)} fusion(bf16[256,20,128]{2,0,1:T(8,128)(2,1)} %param.11), kind=kLoop, calls=%fused_computation.1 | loop fusion | flops 1965824 | bytes 1311744 | tf_op jit(solution)/shard_map/reduce_sum | solution.py:665
  1.8 0.3 multiply_reduce_fusion
  2.2 3.0 %collective-permute-start = (f32[2,256]{1,0:T(2,128)S(1)}, f32[2,256]{1,0:T(2,128)S(1)}, u32[]{:S(2)}, u32[]{:S(2)}) collective-permute-start(f32[2,256]{1,0:T(2,128)S(1)} %pad_maximum_fusion.refs_0_), channel_id=1, source_target_pairs={{0,1},{1,0},{2,3},{3,2},{4,5},{5,4},{6,7},{7,6},{8,9},{9,8},{10,11... | collective-permute-start | bytes 6152 | tf_op jit(solution)/shard_map/ppermute | solution.py:668
  5.2 0.2 convert_reduce_fusion
  5.4 0.1 select_reduce_fusion
  5.5 0.1 pad_add_fusion.place_ref
  5.6 1.2 %collective-permute-done.refs_1_ = f32[2,256]{1,0:T(2,128)S(1)} collective-permute-done((f32[2,256]{1,0:T(2,128)S(1)}, f32[2,256]{1,0:T(2,128)S(1)}, u32[]{:S(2)}, u32[]{:S(2)}) %collective-permute-start) | collective-permute-done | bytes 2080 | tf_op jit(solution)/shard_map/ppermute | solution.py:668
  6.8 1.3 %copy-done.3 = bf16[256,20,128]{2,0,1:T(8,128)(2,1)S(1)} copy-done((bf16[256,20,128]{2,0,1:T(8,128)(2,1)S(1)}, bf16[256,20,128]{2,0,1:T(8,128)(2,1)}, u32[]{:S(2)}) %copy-start.3) | copy-done | bytes 1310744
  8.1 1.3 %pack.2 = (bf16[3,800,128]{2,1,0:T(8,128)(2,1)S(1)}, bf16[3,800,128]{2,1,0:T(8,128)(2,1)S(1)}, bf16[3,800,128]{2,1,0:T(8,128)(2,1)S(1)}, bf16[3,800,128]{2,1,0:T(8,128)(2,1)S(1)}) custom-call(s32[23]{0:T(128)S(1)} %pad_add_fusion.place_ref, f32[2,256]{1,0:T(2,128)S(1)} %pad_maximum_fusion.refs_0_, f32[2,256]{1,0:T(2,128)S(1)} %collective-permute-done.refs_1_, ...), custom_call_target="tpu_custom_call" | custom-call | tf_op jit(solution)/shard_map/pack/pallas_call | solution.py:176
  9.5 2.1 %collective-permute-start.1 = (bf16[3,800,128]{2,1,0:T(8,128)(2,1)S(1)}, bf16[3,800,128]{2,1,0:T(8,128)(2,1)S(1)}, u32[]{:S(2)}, u32[]{:S(2)}) collective-permute-start(bf16[3,800,128]{2,1,0:T(8,128)(2,1)S(1)} %get-tuple-element.40), channel_id=1, source_target_pairs={{0,4},{2,6},{4,0},{6,2},{8,12},{10,14},{12,8},{14,10},{16,20},{18,... | collective-permute-start | bytes 1843208 | tf_op jit(solution)/shard_map/ppermute | solution.py:161
  11.6 1.6 %collective-permute-start.2 = (bf16[3,800,128]{2,1,0:T(8,128)(2,1)S(1)}, bf16[3,800,128]{2,1,0:T(8,128)(2,1)S(1)}, u32[]{:S(2)}, u32[]{:S(2)}) collective-permute-start(bf16[3,800,128]{2,1,0:T(8,128)(2,1)S(1)} %get-tuple-element.41), channel_id=1, source_target_pairs={{0,8},{2,10},{4,12},{6,14},{8,0},{10,2},{12,4},{14,6},{16,24},{18,... | collective-permute-start | bytes 1843208 | tf_op jit(solution)/shard_map/ppermute | solution.py:161
  13.2 1.1 pack.3
  14.2 11.1 %collective-permute-done.1.refs_1_.refs_7_ = bf16[3,800,128]{2,1,0:T(8,128)(2,1)S(1)} collective-permute-done((bf16[3,800,128]{2,1,0:T(8,128)(2,1)S(1)}, bf16[3,800,128]{2,1,0:T(8,128)(2,1)S(1)}, u32[]{:S(2)}, u32[]{:S(2)}) %collective-permute-start.1) | collective-permute-done | bytes 614432 | tf_op jit(solution)/shard_map/ppermute | solution.py:161
  25.4 3.0 %collective-permute-done.2.refs_2_.refs_8_ = bf16[3,800,128]{2,1,0:T(8,128)(2,1)S(1)} collective-permute-done((bf16[3,800,128]{2,1,0:T(8,128)(2,1)S(1)}, bf16[3,800,128]{2,1,0:T(8,128)(2,1)S(1)}, u32[]{:S(2)}, u32[]{:S(2)}) %collective-permute-start.2) | collective-permute-done | bytes 614432 | tf_op jit(solution)/shard_map/ppermute | solution.py:161
  28.4 10.3 %collective-permute-done.3.refs_3_.refs_9_ = bf16[3,800,128]{2,1,0:T(8,128)(2,1)S(1)} collective-permute-done((bf16[3,800,128]{2,1,0:T(8,128)(2,1)S(1)}, bf16[3,800,128]{2,1,0:T(8,128)(2,1)S(1)}, u32[]{:S(2)}, u32[]{:S(2)}) %collective-permute-start.3) | collective-permute-done | bytes 614432 | tf_op jit(solution)/shard_map/ppermute | solution.py:161
  38.7 0.1 stack.26.own_ref
  38.8 0.1 collective-permute-start.4
  38.9 1.7 %collective-permute-start.6 = (bf16[2,784,128]{2,1,0:T(8,128)(2,1)S(1)}, bf16[2,784,128]{2,1,0:T(8,128)(2,1)S(1)}, u32[]{:S(2)}, u32[]{:S(2)}) collective-permute-start(bf16[2,784,128]{2,1,0:T(8,128)(2,1)S(1)} %get-tuple-element.51), channel_id=1, source_target_pairs={{0,4},{2,6},{4,0},{6,2},{8,12},{10,14},{12,8},{14,10},{16,20},{18,... | collective-permute-start | bytes 1204232 | tf_op jit(solution)/shard_map/ppermute | solution.py:161
  40.7 1.8 %collective-permute-done.4.other_ref.refs_4_ = bf16[4,3,544,128]{3,2,1,0:T(8,128)(2,1)S(1)} collective-permute-done((bf16[4,3,544,128]{3,2,1,0:T(8,128)(2,1)S(1)}, bf16[4,3,544,128]{3,2,1,0:T(8,128)(2,1)S(1)}, u32[]{:S(2)}, u32[]{:S(2)}) %collective-permute-start.4) | collective-permute-done | bytes 1671200 | tf_op jit(solution)/shard_map/ppermute | solution.py:161
  42.5 0.6 lone_rows.1
  43.0 1.3 %collective-permute-start.5 = (bf16[3,16,128]{2,1,0:T(8,128)(2,1)S(1)}, bf16[3,16,128]{2,1,0:T(8,128)(2,1)S(1)}, u32[]{:S(2)}, u32[]{:S(2)}) collective-permute-start(bf16[3,16,128]{2,1,0:T(8,128)(2,1)S(1)} %lone_rows.1), channel_id=1, source_target_pairs={{16,0},{18,2},{20,4},{22,6},{24,8},{26,10},{28,12},{30,14},{17,1},... | collective-permute-start | bytes 36872 | tf_op jit(solution)/shard_map/ppermute | solution.py:161
  44.3 1.8 %collective-permute-start.10 = (bf16[2,784,128]{2,1,0:T(8,128)(2,1)S(1)}, bf16[2,784,128]{2,1,0:T(8,128)(2,1)S(1)}, u32[]{:S(2)}, u32[]{:S(2)}) collective-permute-start(bf16[2,784,128]{2,1,0:T(8,128)(2,1)S(1)} %get-tuple-element.56), channel_id=1, source_target_pairs={{0,8},{2,10},{4,12},{6,14},{8,0},{10,2},{12,4},{14,6},{16,24},{18,... | collective-permute-start | bytes 1204232 | tf_op jit(solution)/shard_map/ppermute | solution.py:161
  46.1 1.4 %collective-permute-start.11 = (bf16[2,784,128]{2,1,0:T(8,128)(2,1)S(1)}, bf16[2,784,128]{2,1,0:T(8,128)(2,1)S(1)}, u32[]{:S(2)}, u32[]{:S(2)}) collective-permute-start(bf16[2,784,128]{2,1,0:T(8,128)(2,1)S(1)} %get-tuple-element.57), channel_id=1, source_target_pairs={{0,12},{2,14},{4,8},{6,10},{8,4},{10,6},{12,0},{14,2},{16,28},{18,... | collective-permute-start | bytes 1204232 | tf_op jit(solution)/shard_map/ppermute | solution.py:161
  47.5 6.1 %gradients.2.refs_6_ = bf16[3,384,128]{2,1,0:T(8,128)(2,1)S(1)} custom-call(s32[23]{0:T(128)S(1)} %pad_add_fusion.place_ref, bf16[20,128,512]{2,1,0:T(8,128)(2,1)S(1)} %copy-done.2, bf16[20,256,128]{2,1,0:T(8,128)(2,1)S(1)} %copy-done.4, bf16[3,800,128]{2,1,0:T(8,128)(2,1)S(1)} %get-tuple-element.47.refs_0_.refs_6_, ...), custom_call_target="tpu_custom_call" | custom-call | tf_op jit(solution)/shard_map/gradients/pallas_call | solution.py:176
  53.6 3.6 %collective-permute-start.7 = (bf16[3,384,128]{2,1,0:T(8,128)(2,1)S(1)}, bf16[3,384,128]{2,1,0:T(8,128)(2,1)S(1)}, u32[]{:S(2)}, u32[]{:S(2)}) collective-permute-start(bf16[3,384,128]{2,1,0:T(8,128)(2,1)S(1)} %gradients.2.refs_6_), channel_id=1, source_target_pairs={{0,16},{2,18},{4,20},{6,22},{8,24},{10,26},{12,28},{14,30},{16,0},... | collective-permute-start | bytes 884744 | tf_op jit(solution)/shard_map/ppermute | solution.py:161
  57.3 14.5 %attend.2 = (f32[4,3,256,128]{3,2,1,0:T(8,128)S(1)}, f32[3,16,128]{2,1,0:T(8,128)S(1)}) custom-call(s32[23]{0:T(128)S(1)} %pad_add_fusion.place_ref, s32[20]{0:T(128)S(1)} %copy-done.9, s32[3]{0:T(128)S(1)} %copy-done.10, bf16[3,800,128]{2,1,0:T(8,128)(2,1)S(1)} %get-tuple-element.47.refs_0_.refs_6_, ...), custom_call_target="tpu_custom_call" | custom-call | flops 51539607552 | tf_op jit(solution)/shard_map/attend/pallas_call | solution.py:176
  71.7 0.1 add_convert_fusion.refs_3_
  71.8 0.2 collective-permute-done.11.refs_3_.refs_9_
  72.1 0.1 collective-permute-start.12
  72.2 0.5 collective-permute-start.8
  72.7 0.7 collective-permute-start.9
  73.3 1.5 %collective-permute-done.12.refs_4_ = bf16[4,2,528,128]{3,2,1,0:T(8,128)(2,1)S(1)} collective-permute-done((bf16[4,2,528,128]{3,2,1,0:T(8,128)(2,1)S(1)}, bf16[4,2,528,128]{3,2,1,0:T(8,128)(2,1)S(1)}, u32[]{:S(2)}, u32[]{:S(2)}) %collective-permute-start.12) | collective-permute-done | bytes 1081376 | tf_op jit(solution)/shard_map/ppermute | solution.py:161
  74.9 4.3 %gradients.3.refs_10_.refs_6_ = bf16[2,384,128]{2,1,0:T(8,128)(2,1)S(1)} custom-call(s32[23]{0:T(128)S(1)} %pad_add_fusion.place_ref, bf16[20,128,512]{2,1,0:T(8,128)(2,1)S(1)} %copy-done.2, bf16[20,256,128]{2,1,0:T(8,128)(2,1)S(1)} %copy-done.4, bf16[2,784,128]{2,1,0:T(8,128)(2,1)S(1)} %get-tuple-element.58.refs_0_.refs_6_, ...), custom_call_target="tpu_custom_call" | custom-call | tf_op jit(solution)/shard_map/gradients/pallas_call | solution.py:176
  79.1 1.4 %collective-permute-start.16 = (bf16[2,384,128]{2,1,0:T(8,128)(2,1)S(1)}, bf16[2,384,128]{2,1,0:T(8,128)(2,1)S(1)}, u32[]{:S(2)}, u32[]{:S(2)}) collective-permute-start(bf16[2,384,128]{2,1,0:T(8,128)(2,1)S(1)} %gradients.3.refs_10_.refs_6_), channel_id=1, source_target_pairs={{0,16},{2,18},{4,20},{6,22},{8,24},{10,26},{12,28},{14,30},{16,0},... | collective-permute-start | bytes 589832 | tf_op jit(solution)/shard_map/ppermute | solution.py:161
  80.6 4.0 %finish.2 = (bf16[3,256,128]{2,1,0:T(8,128)(2,1)S(1)}, bf16[3,256,128]{2,1,0:T(8,128)(2,1)S(1)}, bf16[3,256,128]{2,1,0:T(8,128)(2,1)S(1)}, bf16[3,256,128]{2,1,0:T(8,128)(2,1)S(1)}) custom-call(s32[23]{0:T(128)S(1)} %pad_add_fusion.place_ref, f32[4,3,256,128]{3,2,1,0:T(8,128)S(1)} %get-tuple-element.52.refs_5_.refs_0_, bf16[20,128,512]{2,1,0:T(8,128)(2,1)S(1)} %copy-done.2, ...), custom_call_target="tpu_custom_call" | custom-call | flops 19327352832 | tf_op jit(solution)/shard_map/finish/pallas_call | solution.py:176
  84.6 1.6 %collective-permute-start.13 = (bf16[3,256,128]{2,1,0:T(8,128)(2,1)S(1)}, bf16[3,256,128]{2,1,0:T(8,128)(2,1)S(1)}, u32[]{:S(2)}, u32[]{:S(2)}) collective-permute-start(bf16[3,256,128]{2,1,0:T(8,128)(2,1)S(1)} %get-tuple-element.63), channel_id=1, source_target_pairs={{0,4},{2,6},{4,0},{6,2},{8,12},{10,14},{12,8},{14,10},{16,20},{18,... | collective-permute-start | bytes 589832 | tf_op jit(solution)/shard_map/ppermute | solution.py:161
  86.2 2.2 %collective-permute-start.14 = (bf16[3,256,128]{2,1,0:T(8,128)(2,1)S(1)}, bf16[3,256,128]{2,1,0:T(8,128)(2,1)S(1)}, u32[]{:S(2)}, u32[]{:S(2)}) collective-permute-start(bf16[3,256,128]{2,1,0:T(8,128)(2,1)S(1)} %get-tuple-element.64), channel_id=1, source_target_pairs={{0,8},{2,10},{4,12},{6,14},{8,0},{10,2},{12,4},{14,6},{16,24},{18,... | collective-permute-start | bytes 589832 | tf_op jit(solution)/shard_map/ppermute | solution.py:161
  88.3 6.5 %attend.3 = (f32[4,2,256,128]{3,2,1,0:T(8,128)S(1)}, f32[2,16,128]{2,1,0:T(8,128)S(1)}) custom-call(s32[23]{0:T(128)S(1)} %pad_add_fusion.place_ref, s32[20]{0:T(128)S(1)} %copy-done.9, s32[3]{0:T(128)S(1)} %copy-done.10, bf16[2,784,128]{2,1,0:T(8,128)(2,1)S(1)} %get-tuple-element.58.refs_0_.refs_6_, ...), custom_call_target="tpu_custom_call" | custom-call | flops 34359738368 | tf_op jit(solution)/shard_map/attend/pallas_call | solution.py:176
  94.9 0.5 collective-permute-start.17
  95.4 0.7 collective-permute-start.18
  96.0 1.1 %collective-permute-start.15 = (bf16[3,256,128]{2,1,0:T(8,128)(2,1)S(1)}, bf16[3,256,128]{2,1,0:T(8,128)(2,1)S(1)}, u32[]{:S(2)}, u32[]{:S(2)}) collective-permute-start(bf16[3,256,128]{2,1,0:T(8,128)(2,1)S(1)} %get-tuple-element.65), channel_id=1, source_target_pairs={{0,12},{2,14},{4,8},{6,10},{8,4},{10,6},{12,0},{14,2},{16,28},{18,... | collective-permute-start | bytes 589832 | tf_op jit(solution)/shard_map/ppermute | solution.py:161
  97.2 2.9 %finish.3 = (bf16[2,256,128]{2,1,0:T(8,128)(2,1)S(1)}, bf16[2,256,128]{2,1,0:T(8,128)(2,1)S(1)}, bf16[2,256,128]{2,1,0:T(8,128)(2,1)S(1)}, bf16[2,256,128]{2,1,0:T(8,128)(2,1)S(1)}) custom-call(s32[23]{0:T(128)S(1)} %pad_add_fusion.place_ref, f32[4,2,256,128]{3,2,1,0:T(8,128)S(1)} %get-tuple-element.66.refs_0_, bf16[20,128,512]{2,1,0:T(8,128)(2,1)S(1)} %copy-done.2, ...), custom_call_target="tpu_custom_call" | custom-call | flops 12884901888 | tf_op jit(solution)/shard_map/finish/pallas_call | solution.py:176
  100.0 0.6 collective-permute-start.19
  100.6 1.9 %collective-permute-start.20 = (bf16[2,256,128]{2,1,0:T(8,128)(2,1)S(1)}, bf16[2,256,128]{2,1,0:T(8,128)(2,1)S(1)}, u32[]{:S(2)}, u32[]{:S(2)}) collective-permute-start(bf16[2,256,128]{2,1,0:T(8,128)(2,1)S(1)} %get-tuple-element.71), channel_id=1, source_target_pairs={{0,8},{2,10},{4,12},{6,14},{8,0},{10,2},{12,4},{14,6},{16,24},{18,... | collective-permute-start | bytes 393224 | tf_op jit(solution)/shard_map/ppermute | solution.py:161
  102.5 1.1 collective-permute-start.21
  103.6 3.4 %collective-permute-done.19.refs_5_ = bf16[2,256,128]{2,1,0:T(8,128)(2,1)S(1)} collective-permute-done((bf16[2,256,128]{2,1,0:T(8,128)(2,1)S(1)}, bf16[2,256,128]{2,1,0:T(8,128)(2,1)S(1)}, u32[]{:S(2)}, u32[]{:S(2)}) %collective-permute-start.19) | collective-permute-done | bytes 131104 | tf_op jit(solution)/shard_map/ppermute | solution.py:161
  107.0 2.7 %collective-permute-done.21.refs_7_ = bf16[2,256,128]{2,1,0:T(8,128)(2,1)S(1)} collective-permute-done((bf16[2,256,128]{2,1,0:T(8,128)(2,1)S(1)}, bf16[2,256,128]{2,1,0:T(8,128)(2,1)S(1)}, u32[]{:S(2)}, u32[]{:S(2)}) %collective-permute-start.21) | collective-permute-done | bytes 131104 | tf_op jit(solution)/shard_map/ppermute | solution.py:161
  109.7 1.8 %put_in_place.1 = bf16[20,256,128]{2,1,0:T(8,128)(2,1)} custom-call(s32[23]{0:T(128)S(1)} %pad_add_fusion.place_ref, bf16[3,256,128]{2,1,0:T(8,128)(2,1)S(1)} %get-tuple-element.62.refs_7_.refs_10_.refs_0_, bf16[3,256,128]{2,1,0:T(8,128)(2,1)S(1)} %collective-permute-done.13.refs_11_.refs_1_, ...), custom_call_target="tpu_custom_call" | custom-call | tf_op jit(solution)/shard_map/put_in_place/pallas_call | solution.py:592
  (40 shorter events, 0.2 us)
Async XLA Ops:
  0.0 1.8 %copy-start = (bf16[256,20,128]{2,0,1:T(8,128)(2,1)S(1)}, bf16[256,20,128]{2,0,1:T(8,128)(2,1)}, u32[]{:S(2)}) copy-start(bf16[256,20,128]{2,0,1:T(8,128)(2,1)} %param.12) | copy-start | bytes 3932164
  0.0 6.8 %copy-start.1 = (bf16[256,20,128]{2,0,1:T(8,128)(2,1)S(1)}, bf16[256,20,128]{2,0,1:T(8,128)(2,1)}, u32[]{:S(2)}) copy-start(bf16[256,20,128]{2,0,1:T(8,128)(2,1)} %param.11) | copy-start | bytes 3932164
  0.0 5.2 %copy-start.9 = (s32[20]{0:T(128)S(1)}, s32[20]{0:T(128)}, u32[]{:S(2)}) copy-start(s32[20]{0:T(128)} %window_ref.3) | copy-start | bytes 244
  0.0 6.8 %copy-start.7 = (f32[20,128]{1,0:T(8,128)S(1)}, f32[20,128]{1,0:T(8,128)}, u32[]{:S(2)}) copy-start(f32[20,128]{1,0:T(8,128)} %refs_2_.5) | copy-start | bytes 30724
  0.0 6.8 %copy-start.8 = (f32[20,128]{1,0:T(8,128)S(1)}, f32[20,128]{1,0:T(8,128)}, u32[]{:S(2)}) copy-start(f32[20,128]{1,0:T(8,128)} %refs_3_.3) | copy-start | bytes 30724
  0.0 6.8 %copy-start.5 = (f32[20,256]{1,0:T(8,128)S(1)}, f32[20,256]{1,0:T(8,128)}, u32[]{:S(2)}) copy-start(f32[20,256]{1,0:T(8,128)} %refs_4_.3) | copy-start | bytes 61444
  0.0 6.8 %copy-start.6 = (f32[20,256]{1,0:T(8,128)S(1)}, f32[20,256]{1,0:T(8,128)}, u32[]{:S(2)}) copy-start(f32[20,256]{1,0:T(8,128)} %refs_5_.3) | copy-start | bytes 61444
  2.2 4.6 %collective-permute-start = (f32[2,256]{1,0:T(2,128)S(1)}, f32[2,256]{1,0:T(2,128)S(1)}, u32[]{:S(2)}, u32[]{:S(2)}) collective-permute-start(f32[2,256]{1,0:T(2,128)S(1)} %pad_maximum_fusion.refs_0_), channel_id=1, source_target_pairs={{0,1},{1,0},{2,3},{3,2},{4,5},{5,4},{6,7},{7,6},{8,9},{9,8},{10,11... | collective-permute-start | bytes 6152 | tf_op jit(solution)/shard_map/ppermute | solution.py:668
  6.8 1.3 %copy-start.3 = (bf16[256,20,128]{2,0,1:T(8,128)(2,1)S(1)}, bf16[256,20,128]{2,0,1:T(8,128)(2,1)}, u32[]{:S(2)}) copy-start(bf16[256,20,128]{2,0,1:T(8,128)(2,1)} %param.13) | copy-start | bytes 3932164
  9.5 15.9 %collective-permute-start.1 = (bf16[3,800,128]{2,1,0:T(8,128)(2,1)S(1)}, bf16[3,800,128]{2,1,0:T(8,128)(2,1)S(1)}, u32[]{:S(2)}, u32[]{:S(2)}) collective-permute-start(bf16[3,800,128]{2,1,0:T(8,128)(2,1)S(1)} %get-tuple-element.40), channel_id=1, source_target_pairs={{0,4},{2,6},{4,0},{6,2},{8,12},{10,14},{12,8},{14,10},{16,20},{18,... | collective-permute-start | bytes 1843208 | tf_op jit(solution)/shard_map/ppermute | solution.py:161
  11.6 16.8 %collective-permute-start.2 = (bf16[3,800,128]{2,1,0:T(8,128)(2,1)S(1)}, bf16[3,800,128]{2,1,0:T(8,128)(2,1)S(1)}, u32[]{:S(2)}, u32[]{:S(2)}) collective-permute-start(bf16[3,800,128]{2,1,0:T(8,128)(2,1)S(1)} %get-tuple-element.41), channel_id=1, source_target_pairs={{0,8},{2,10},{4,12},{6,14},{8,0},{10,2},{12,4},{14,6},{16,24},{18,... | collective-permute-start | bytes 1843208 | tf_op jit(solution)/shard_map/ppermute | solution.py:161
  13.2 25.5 %collective-permute-start.3 = (bf16[3,800,128]{2,1,0:T(8,128)(2,1)S(1)}, bf16[3,800,128]{2,1,0:T(8,128)(2,1)S(1)}, u32[]{:S(2)}, u32[]{:S(2)}) collective-permute-start(bf16[3,800,128]{2,1,0:T(8,128)(2,1)S(1)} %get-tuple-element.42), channel_id=1, source_target_pairs={{0,12},{2,14},{4,8},{6,10},{8,4},{10,6},{12,0},{14,2},{16,28},{18,... | collective-permute-start | bytes 1843208 | tf_op jit(solution)/shard_map/ppermute | solution.py:161
  38.7 8.8 %copy-start.4 = (bf16[20,256,128]{2,1,0:T(8,128)(2,1)S(1)}, bf16[20,256,128]{2,1,0:T(8,128)(2,1)}, u32[]{:S(2)}) copy-start(bf16[20,256,128]{2,1,0:T(8,128)(2,1)} %refs_2_.7) | copy-start | bytes 3932164
  38.8 8.7 %copy-start.2 = (bf16[20,128,512]{2,1,0:T(8,128)(2,1)S(1)}, bf16[20,128,512]{2,1,0:T(8,128)(2,1)}, u32[]{:S(2)}) copy-start(bf16[20,128,512]{2,1,0:T(8,128)(2,1)} %refs_1_.3) | copy-start | bytes 7864324
  38.8 3.6 %collective-permute-start.4 = (bf16[4,3,544,128]{3,2,1,0:T(8,128)(2,1)S(1)}, bf16[4,3,544,128]{3,2,1,0:T(8,128)(2,1)S(1)}, u32[]{:S(2)}, u32[]{:S(2)}) collective-permute-start(bf16[4,3,544,128]{3,2,1,0:T(8,128)(2,1)S(1)} %stack.26.own_ref), channel_id=1, source_target_pairs={{0,2},{2,0},{4,6},{6,4},{8,10},{10,8},{12,14},{14,12},{16,18},{18,... | collective-permute-start | bytes 5013512 | tf_op jit(solution)/shard_map/ppermute | solution.py:161
  38.9 18.3 %collective-permute-start.6 = (bf16[2,784,128]{2,1,0:T(8,128)(2,1)S(1)}, bf16[2,784,128]{2,1,0:T(8,128)(2,1)S(1)}, u32[]{:S(2)}, u32[]{:S(2)}) collective-permute-start(bf16[2,784,128]{2,1,0:T(8,128)(2,1)S(1)} %get-tuple-element.51), channel_id=1, source_target_pairs={{0,4},{2,6},{4,0},{6,2},{8,12},{10,14},{12,8},{14,10},{16,20},{18,... | collective-permute-start | bytes 1204232 | tf_op jit(solution)/shard_map/ppermute | solution.py:161
  43.0 14.2 %copy-start.10 = (s32[3]{0:T(128)S(1)}, s32[3]{0:T(128)}, u32[]{:S(2)}) copy-start(s32[3]{0:T(128)} %edge_ref.3) | copy-start | bytes 40
  43.0 14.2 %collective-permute-start.5 = (bf16[3,16,128]{2,1,0:T(8,128)(2,1)S(1)}, bf16[3,16,128]{2,1,0:T(8,128)(2,1)S(1)}, u32[]{:S(2)}, u32[]{:S(2)}) collective-permute-start(bf16[3,16,128]{2,1,0:T(8,128)(2,1)S(1)} %lone_rows.1), channel_id=1, source_target_pairs={{16,0},{18,2},{20,4},{22,6},{24,8},{26,10},{28,12},{30,14},{17,1},... | collective-permute-start | bytes 36872 | tf_op jit(solution)/shard_map/ppermute | solution.py:161
  44.3 27.5 %collective-permute-start.10 = (bf16[2,784,128]{2,1,0:T(8,128)(2,1)S(1)}, bf16[2,784,128]{2,1,0:T(8,128)(2,1)S(1)}, u32[]{:S(2)}, u32[]{:S(2)}) collective-permute-start(bf16[2,784,128]{2,1,0:T(8,128)(2,1)S(1)} %get-tuple-element.56), channel_id=1, source_target_pairs={{0,8},{2,10},{4,12},{6,14},{8,0},{10,2},{12,4},{14,6},{16,24},{18,... | collective-permute-start | bytes 1204232 | tf_op jit(solution)/shard_map/ppermute | solution.py:161
  46.1 25.9 %collective-permute-start.11 = (bf16[2,784,128]{2,1,0:T(8,128)(2,1)S(1)}, bf16[2,784,128]{2,1,0:T(8,128)(2,1)S(1)}, u32[]{:S(2)}, u32[]{:S(2)}) collective-permute-start(bf16[2,784,128]{2,1,0:T(8,128)(2,1)S(1)} %get-tuple-element.57), channel_id=1, source_target_pairs={{0,12},{2,14},{4,8},{6,10},{8,4},{10,6},{12,0},{14,2},{16,28},{18,... | collective-permute-start | bytes 1204232 | tf_op jit(solution)/shard_map/ppermute | solution.py:161
  53.6 18.1 %collective-permute-start.7 = (bf16[3,384,128]{2,1,0:T(8,128)(2,1)S(1)}, bf16[3,384,128]{2,1,0:T(8,128)(2,1)S(1)}, u32[]{:S(2)}, u32[]{:S(2)}) collective-permute-start(bf16[3,384,128]{2,1,0:T(8,128)(2,1)S(1)} %gradients.2.refs_6_), channel_id=1, source_target_pairs={{0,16},{2,18},{4,20},{6,22},{8,24},{10,26},{12,28},{14,30},{16,0},... | collective-permute-start | bytes 884744 | tf_op jit(solution)/shard_map/ppermute | solution.py:161
  72.1 2.8 %collective-permute-start.12 = (bf16[4,2,528,128]{3,2,1,0:T(8,128)(2,1)S(1)}, bf16[4,2,528,128]{3,2,1,0:T(8,128)(2,1)S(1)}, u32[]{:S(2)}, u32[]{:S(2)}) collective-permute-start(bf16[4,2,528,128]{3,2,1,0:T(8,128)(2,1)S(1)} %stack.27), channel_id=1, source_target_pairs={{0,2},{2,0},{4,6},{6,4},{8,10},{10,8},{12,14},{14,12},{16,18},{18,... | collective-permute-start | bytes 3244040 | tf_op jit(solution)/shard_map/ppermute | solution.py:161
  72.2 8.4 %collective-permute-start.8 = (bf16[3,384,128]{2,1,0:T(8,128)(2,1)S(1)}, bf16[3,384,128]{2,1,0:T(8,128)(2,1)S(1)}, u32[]{:S(2)}, u32[]{:S(2)}) collective-permute-start(bf16[3,384,128]{2,1,0:T(8,128)(2,1)S(1)} %add_convert_fusion.refs_3_), channel_id=1, source_target_pairs={{0,2},{2,0},{4,6},{6,4},{8,10},{10,8},{12,14},{14,12},{16,18},{18,... | collective-permute-start | bytes 884744 | tf_op jit(solution)/shard_map/ppermute | solution.py:161
  72.7 7.9 %collective-permute-start.9 = (f32[3,16,128]{2,1,0:T(8,128)S(1)}, f32[3,16,128]{2,1,0:T(8,128)S(1)}, u32[]{:S(2)}, u32[]{:S(2)}) collective-permute-start(f32[3,16,128]{2,1,0:T(8,128)S(1)} %get-tuple-element.54), channel_id=1, source_target_pairs={{2,16},{6,20},{10,24},{14,28},{3,17},{7,21},{11,25},{15,29}} | collective-permute-start | bytes 73736 | tf_op jit(solution)/shard_map/ppermute | solution.py:161
  79.1 15.7 %collective-permute-start.16 = (bf16[2,384,128]{2,1,0:T(8,128)(2,1)S(1)}, bf16[2,384,128]{2,1,0:T(8,128)(2,1)S(1)}, u32[]{:S(2)}, u32[]{:S(2)}) collective-permute-start(bf16[2,384,128]{2,1,0:T(8,128)(2,1)S(1)} %gradients.3.refs_10_.refs_6_), channel_id=1, source_target_pairs={{0,16},{2,18},{4,20},{6,22},{8,24},{10,26},{12,28},{14,30},{16,0},... | collective-permute-start | bytes 589832 | tf_op jit(solution)/shard_map/ppermute | solution.py:161
  84.6 12.6 %collective-permute-start.13 = (bf16[3,256,128]{2,1,0:T(8,128)(2,1)S(1)}, bf16[3,256,128]{2,1,0:T(8,128)(2,1)S(1)}, u32[]{:S(2)}, u32[]{:S(2)}) collective-permute-start(bf16[3,256,128]{2,1,0:T(8,128)(2,1)S(1)} %get-tuple-element.63), channel_id=1, source_target_pairs={{0,4},{2,6},{4,0},{6,2},{8,12},{10,14},{12,8},{14,10},{16,20},{18,... | collective-permute-start | bytes 589832 | tf_op jit(solution)/shard_map/ppermute | solution.py:161
  86.2 11.0 %collective-permute-start.14 = (bf16[3,256,128]{2,1,0:T(8,128)(2,1)S(1)}, bf16[3,256,128]{2,1,0:T(8,128)(2,1)S(1)}, u32[]{:S(2)}, u32[]{:S(2)}) collective-permute-start(bf16[3,256,128]{2,1,0:T(8,128)(2,1)S(1)} %get-tuple-element.64), channel_id=1, source_target_pairs={{0,8},{2,10},{4,12},{6,14},{8,0},{10,2},{12,4},{14,6},{16,24},{18,... | collective-permute-start | bytes 589832 | tf_op jit(solution)/shard_map/ppermute | solution.py:161
  94.9 2.3 %collective-permute-start.17 = (bf16[2,384,128]{2,1,0:T(8,128)(2,1)S(1)}, bf16[2,384,128]{2,1,0:T(8,128)(2,1)S(1)}, u32[]{:S(2)}, u32[]{:S(2)}) collective-permute-start(bf16[2,384,128]{2,1,0:T(8,128)(2,1)S(1)} %add_convert_fusion.1.refs_3_), channel_id=1, source_target_pairs={{0,2},{2,0},{4,6},{6,4},{8,10},{10,8},{12,14},{14,12},{16,18},{18,... | collective-permute-start | bytes 589832 | tf_op jit(solution)/shard_map/ppermute | solution.py:161
  95.4 1.8 %collective-permute-start.18 = (f32[2,16,128]{2,1,0:T(8,128)S(1)}, f32[2,16,128]{2,1,0:T(8,128)S(1)}, u32[]{:S(2)}, u32[]{:S(2)}) collective-permute-start(f32[2,16,128]{2,1,0:T(8,128)S(1)} %get-tuple-element.68), channel_id=1, source_target_pairs={{2,16},{6,20},{10,24},{14,28},{3,17},{7,21},{11,25},{15,29}} | collective-permute-start | bytes 49160 | tf_op jit(solution)/shard_map/ppermute | solution.py:161
  96.0 7.6 %collective-permute-start.15 = (bf16[3,256,128]{2,1,0:T(8,128)(2,1)S(1)}, bf16[3,256,128]{2,1,0:T(8,128)(2,1)S(1)}, u32[]{:S(2)}, u32[]{:S(2)}) collective-permute-start(bf16[3,256,128]{2,1,0:T(8,128)(2,1)S(1)} %get-tuple-element.65), channel_id=1, source_target_pairs={{0,12},{2,14},{4,8},{6,10},{8,4},{10,6},{12,0},{14,2},{16,28},{18,... | collective-permute-start | bytes 589832 | tf_op jit(solution)/shard_map/ppermute | solution.py:161
  100.0 7.0 %collective-permute-start.19 = (bf16[2,256,128]{2,1,0:T(8,128)(2,1)S(1)}, bf16[2,256,128]{2,1,0:T(8,128)(2,1)S(1)}, u32[]{:S(2)}, u32[]{:S(2)}) collective-permute-start(bf16[2,256,128]{2,1,0:T(8,128)(2,1)S(1)} %get-tuple-element.70), channel_id=1, source_target_pairs={{0,4},{2,6},{4,0},{6,2},{8,12},{10,14},{12,8},{14,10},{16,20},{18,... | collective-permute-start | bytes 393224 | tf_op jit(solution)/shard_map/ppermute | solution.py:161
  100.6 6.4 %collective-permute-start.20 = (bf16[2,256,128]{2,1,0:T(8,128)(2,1)S(1)}, bf16[2,256,128]{2,1,0:T(8,128)(2,1)S(1)}, u32[]{:S(2)}, u32[]{:S(2)}) collective-permute-start(bf16[2,256,128]{2,1,0:T(8,128)(2,1)S(1)} %get-tuple-element.71), channel_id=1, source_target_pairs={{0,8},{2,10},{4,12},{6,14},{8,0},{10,2},{12,4},{14,6},{16,24},{18,... | collective-permute-start | bytes 393224 | tf_op jit(solution)/shard_map/ppermute | solution.py:161
  102.5 7.2 %collective-permute-start.21 = (bf16[2,256,128]{2,1,0:T(8,128)(2,1)S(1)}, bf16[2,256,128]{2,1,0:T(8,128)(2,1)S(1)}, u32[]{:S(2)}, u32[]{:S(2)}) collective-permute-start(bf16[2,256,128]{2,1,0:T(8,128)(2,1)S(1)} %get-tuple-element.72), channel_id=1, source_target_pairs={{0,12},{2,14},{4,8},{6,10},{8,4},{10,6},{12,0},{14,2},{16,28},{18,... | collective-permute-start | bytes 393224 | tf_op jit(solution)/shard_map/ppermute | solution.py:161
